TPU v7x, 32 devices: a whole 2x2x4 slice. The times are simulated.
32 devices in a mesh: dp: 4 (over y, x), seq: 8 (over z, core).
Axes of the slice: x: 2, y: 2, z: 4, core: 2. Of those that a mesh axis runs over, the one named last changes fastest.
Arguments:
- hidden: bfloat16 [4, 1024, 2048], P('dp', 'seq'), may hold values from -6 to 6
- token_document_numbers: int32 [4, 1024], P('dp', 'seq'), may hold values from 0 to 1023, as said below
- sequence_adapter_index: int32 [4], P('dp'), may hold values from 0 to 3, each once
- cotangent: bfloat16 [4, 1024, 2048], P('dp', 'seq'), may hold values from -6 to 6
- attention_norm_gain: float32 [2048], replicated, may hold values from 0.25 to 1.75
- feedforward_norm_gain: float32 [2048], replicated, may hold values from 0.25 to 1.75
- query_weight: bfloat16 [2048, 2048], P(('dp', 'seq')), may hold values from -0.5 to 0.5
- key_weight: bfloat16 [2048, 512], P(('dp', 'seq')), may hold values from -0.5 to 0.5
- value_weight: bfloat16 [2048, 512], P(('dp', 'seq')), may hold values from -0.125 to 0.125
- attention_output_weight: bfloat16 [2048, 2048], P(('dp', 'seq')), may hold values from -1.5 to 1.5
- gate_weight: bfloat16 [2048, 8192], P(('dp', 'seq')), may hold values from -0.125 to 0.125
- up_weight: bfloat16 [2048, 8192], P(('dp', 'seq')), may hold values from -0.125 to 0.125
- down_weight: bfloat16 [8192, 2048], P(('dp', 'seq')), may hold values from -0.5 to 0.5
- adapter_query_key_value_input: bfloat16 [4, 2048, 48], replicated, may hold values from -0.125 to 0.125
- adapter_query_output: bfloat16 [4, 16, 2048], replicated, may hold values from -1.5 to 1.5
- adapter_key_value_output: bfloat16 [4, 16, 1024], replicated, may hold values from -1.5 to 1.5
- adapter_projection_input: bfloat16 [4, 2048, 16], replicated, may hold values from -0.125 to 0.125
- adapter_projection_output: bfloat16 [4, 16, 2048], replicated, may hold values from -1.5 to 1.5
- adapter_gate_up_input: bfloat16 [4, 2048, 32], replicated, may hold values from -0.125 to 0.125
- adapter_gate_up_output: bfloat16 [4, 16, 16384], replicated, may hold values from -1.5 to 1.5
- adapter_down_input: bfloat16 [4, 8192, 16], replicated, may hold values from -0.0625 to 0.0625
- adapter_down_output: bfloat16 [4, 16, 2048], replicated, may hold values from -1.5 to 1.5
Outputs:
- mixed: bfloat16 [4, 1024, 2048], P('dp', 'seq')
- grad_hidden: bfloat16 [4, 1024, 2048], P('dp', 'seq')
- grad_lora_qkv_in: float32 [4, 2048, 48], P(None, ('dp', 'seq'))
- grad_lora_q_out: float32 [4, 16, 2048], P(None, None, ('dp', 'seq'))
- grad_lora_kv_out: float32 [4, 16, 1024], P(None, None, ('dp', 'seq'))
- grad_lora_o_in: float32 [4, 2048, 16], P(None, ('dp', 'seq'))
- grad_lora_o_out: float32 [4, 16, 2048], P(None, None, ('dp', 'seq'))
- grad_lora_gu_in: float32 [4, 2048, 32], P(None, ('dp', 'seq'))
- grad_lora_gu_out: float32 [4, 16, 16384], P(None, None, ('dp', 'seq'))
- grad_lora_down_in: float32 [4, 8192, 16], P(None, ('dp', 'seq'))
- grad_lora_down_out: float32 [4, 16, 2048], P(None, None, ('dp', 'seq'))
Inputs may be any that keep to these rules, and one draw needn't show every extreme that they name: `token_document_numbers`: along each sequence the ids start at 0 and never fall; the last segment of every sequence is padding of 1 to 64 tokens and has the id 1024 - 1. `sequence_adapter_index`: every adapter is used by exactly one sequence.
All inputs are finite; a program needn't handle non-finite values.
Results may differ from a plain program's by a relative error of at most 0.02.
Values may be sent and summed in bfloat16 or wider, within the bound.
A program may use at most 320 MiB of HBM per device.

v0:
```python
import math

import jax
import jax.numpy as jnp
from jax import lax
from jax.sharding import PartitionSpec as P

NH = 32
KVH = 8
HD = 64


EPSILON = 1e-05
RESIDUAL_SCALE = 0.22
SCORE_SCALE = 1.0 / 64.0
ROPE_BASE = 10000000.0


def rms_scale(values, gain):
    mean_square = jnp.mean(values * values, axis=-1, keepdims=True)
    return values * lax.rsqrt(mean_square + EPSILON) * gain


def rotate(values, cos_table, sin_table):
    half_width = values.shape[-1] // 2
    first_half = values[..., :half_width]
    second_half = values[..., half_width:]
    cos_part = cos_table[:, None, :]
    sin_part = sin_table[:, None, :]
    return jnp.concatenate(
        [
            first_half * cos_part - second_half * sin_part,
            second_half * cos_part + first_half * sin_part,
        ],
        axis=-1,
    )


def angle_tables(positions, head_size):
    steps = jnp.arange(head_size // 2).astype(jnp.float32)
    frequency = jnp.exp(steps * (-2.0 * math.log(ROPE_BASE) / head_size))
    angles = positions[:, None] * frequency[None, :]
    return (jnp.cos(angles), jnp.sin(angles))


def project(operand, matrix):
    flat = operand.reshape(-1, operand.shape[-1])
    result = jnp.dot(flat, matrix, preferred_element_type=jnp.float32)
    return result.reshape(operand.shape[:-1] + (matrix.shape[1],))


def project_t(operand, matrix):
    flat = operand.reshape(-1, operand.shape[-1])
    result = lax.dot_general(
        flat, matrix, (((1,), (1,)), ((), ())), preferred_element_type=jnp.float32
    )
    return result.reshape(operand.shape[:-1] + (matrix.shape[0],))


def seq_in(operand, matrix):
    return jnp.einsum("sti,sir->str", operand, matrix, preferred_element_type=jnp.float32)


def seq_out(operand, matrix):
    return jnp.einsum("str,sro->sto", operand, matrix, preferred_element_type=jnp.float32)


def seq_back(operand, matrix):
    return jnp.einsum("sto,sro->str", operand, matrix, preferred_element_type=jnp.float32)


def seq_in_back(operand, matrix):
    return jnp.einsum("str,sir->sti", operand, matrix, preferred_element_type=jnp.float32)


def seq_outer(operand, other):
    return jnp.einsum("sti,sto->sio", operand, other, preferred_element_type=jnp.float32)


def block_scores(query_block, key_heads, seg_block, segments, start_row, block_rows):
    length = key_heads.shape[1]
    key_pos = jnp.arange(length, dtype=jnp.int32)
    query_pos = start_row + jnp.arange(block_rows, dtype=jnp.int32)
    scores = (
        jnp.einsum("sqhd,skhd->shqk", query_block, key_heads, preferred_element_type=jnp.float32)
        * SCORE_SCALE
    )
    allowed = (key_pos[None, None, :] <= query_pos[None, :, None]) & (
        seg_block[:, :, None] == segments[:, None, :]
    )
    return jnp.where(allowed[:, None], scores, -1e30)


def attend_forward(query_heads, key_heads, value_heads, segments):
    seq_count, length, local_heads, head_size = query_heads.shape
    block_rows = min(512, length)

    def one_block(block_index):
        start_row = block_index * block_rows
        query_block = lax.dynamic_slice_in_dim(query_heads, start_row, block_rows, 1)
        seg_block = lax.dynamic_slice_in_dim(segments, start_row, block_rows, 1)
        scores = block_scores(query_block, key_heads, seg_block, segments, start_row, block_rows)
        row_max = jnp.max(scores, axis=-1, keepdims=True)
        weights = jnp.exp(scores - row_max)
        totals = jnp.sum(weights, axis=-1, keepdims=True)
        weights_low = (weights / totals).astype(jnp.bfloat16)
        output = jnp.einsum(
            "shqk,skhd->sqhd", weights_low, value_heads, preferred_element_type=jnp.float32
        )
        return (output.astype(jnp.bfloat16), (row_max + jnp.log(totals))[..., 0])

    outputs, log_totals = lax.map(one_block, jnp.arange(length // block_rows, dtype=jnp.int32))
    outputs = jnp.moveaxis(outputs, 0, 1).reshape(seq_count, length, local_heads, head_size)
    return (outputs, log_totals)


def attend_backward(query_heads, key_heads, value_heads, segments, log_totals, grad_heads):
    seq_count, length, local_heads, head_size = query_heads.shape
    block_rows = min(512, length)

    def one_block(carry, block_index):
        grad_keys, grad_values = carry
        start_row = block_index * block_rows
        query_block = lax.dynamic_slice_in_dim(query_heads, start_row, block_rows, 1)
        seg_block = lax.dynamic_slice_in_dim(segments, start_row, block_rows, 1)
        grad_block = lax.dynamic_slice_in_dim(grad_heads, start_row, block_rows, 1)
        scores = block_scores(query_block, key_heads, seg_block, segments, start_row, block_rows)
        weights = jnp.exp(scores - log_totals[block_index][..., None])
        grad_weights = jnp.einsum(
            "sqhd,skhd->shqk", grad_block, value_heads, preferred_element_type=jnp.float32
        )
        row_dot = jnp.sum(weights * grad_weights, axis=-1, keepdims=True)
        grad_scores = (weights * (grad_weights - row_dot)).astype(jnp.bfloat16)
        grad_query = (
            jnp.einsum(
                "shqk,skhd->sqhd", grad_scores, key_heads, preferred_element_type=jnp.float32
            )
            * SCORE_SCALE
        )
        grad_keys = (
            grad_keys
            + jnp.einsum(
                "shqk,sqhd->skhd", grad_scores, query_block, preferred_element_type=jnp.float32
            )
            * SCORE_SCALE
        )
        grad_values = grad_values + jnp.einsum(
            "shqk,sqhd->skhd",
            weights.astype(jnp.bfloat16),
            grad_block,
            preferred_element_type=jnp.float32,
        )
        return ((grad_keys, grad_values), grad_query.astype(jnp.bfloat16))

    zero_grads = jnp.zeros(key_heads.shape, jnp.float32)
    (grad_keys, grad_values), grad_query = lax.scan(
        one_block, (zero_grads, zero_grads), jnp.arange(length // block_rows, dtype=jnp.int32)
    )
    grad_query = jnp.moveaxis(grad_query, 0, 1).reshape(seq_count, length, local_heads, head_size)
    return (grad_query, grad_keys.astype(jnp.bfloat16), grad_values.astype(jnp.bfloat16))


def local(
    hidden,
    token_document_numbers,
    sequence_adapter_index,
    cotangent,
    attention_norm_gain,
    feedforward_norm_gain,
    query_weight,
    key_weight,
    value_weight,
    attention_output_weight,
    gate_weight,
    up_weight,
    down_weight,
    adapter_query_key_value_input,
    adapter_query_output,
    adapter_key_value_output,
    adapter_projection_input,
    adapter_projection_output,
    adapter_gate_up_input,
    adapter_gate_up_output,
    adapter_down_input,
    adapter_down_output,
):
    seq_count, tok_count, width = hidden.shape
    groups = NH // KVH
    adapter_rank_size = adapter_projection_input.shape[2]
    positions = (lax.axis_index("seq") * tok_count + jnp.arange(tok_count, dtype=jnp.int32)).astype(
        jnp.float32
    )
    cos_table, sin_table = angle_tables(positions, HD)
    hidden_f = hidden.astype(jnp.float32)
    select_query_key_value_input = adapter_query_key_value_input[sequence_adapter_index]
    select_query_output = adapter_query_output[sequence_adapter_index]
    select_key_value_output = adapter_key_value_output[sequence_adapter_index]
    select_projection_input = adapter_projection_input[sequence_adapter_index]
    select_projection_output = adapter_projection_output[sequence_adapter_index]
    select_gate_up_input = adapter_gate_up_input[sequence_adapter_index]
    select_gate_up_output = adapter_gate_up_output[sequence_adapter_index]
    select_down_input = adapter_down_input[sequence_adapter_index]
    select_down_output = adapter_down_output[sequence_adapter_index]
    all_segments = lax.all_gather(token_document_numbers, "seq", axis=1, tiled=True)
    query_full, key_full, value_full, out_full = (
        lax.all_gather(query_weight, ("dp", "seq"), axis=0, tiled=True),
        lax.all_gather(key_weight, ("dp", "seq"), axis=0, tiled=True),
        lax.all_gather(value_weight, ("dp", "seq"), axis=0, tiled=True),
        lax.all_gather(attention_output_weight, ("dp", "seq"), axis=0, tiled=True),
    )
    key_width = key_full.shape[1]
    norm_one = rms_scale(hidden_f, attention_norm_gain).astype(jnp.bfloat16)
    low_qkv = seq_in(norm_one, select_query_key_value_input).astype(jnp.bfloat16)
    query_pre = project(norm_one, query_full) + seq_out(
        low_qkv[..., :adapter_rank_size], select_query_output
    )
    key_pre = project(norm_one, key_full) + seq_out(
        low_qkv[..., adapter_rank_size : 2 * adapter_rank_size],
        select_key_value_output[..., :key_width],
    )
    value_pre = project(norm_one, value_full) + seq_out(
        low_qkv[..., 2 * adapter_rank_size :], select_key_value_output[..., key_width:]
    )
    query_rot = rotate(
        query_pre.reshape(seq_count, tok_count, NH, HD), cos_table, sin_table
    ).astype(jnp.bfloat16)
    key_rot = rotate(key_pre.reshape(seq_count, tok_count, KVH, HD), cos_table, sin_table).astype(
        jnp.bfloat16
    )
    value_low = value_pre.reshape(seq_count, tok_count, KVH, HD).astype(jnp.bfloat16)
    key_rep = jnp.repeat(key_rot, groups, axis=2)
    value_rep = jnp.repeat(value_low, groups, axis=2)
    query_heads, key_heads, value_heads = (
        lax.all_to_all(query_rot, "seq", split_axis=2, concat_axis=1, tiled=True),
        lax.all_to_all(key_rep, "seq", split_axis=2, concat_axis=1, tiled=True),
        lax.all_to_all(value_rep, "seq", split_axis=2, concat_axis=1, tiled=True),
    )
    attn_heads, log_totals = attend_forward(query_heads, key_heads, value_heads, all_segments)
    attn_tokens = lax.all_to_all(
        attn_heads, "seq", split_axis=1, concat_axis=2, tiled=True
    ).reshape(seq_count, tok_count, width)
    low_out = seq_in(attn_tokens, select_projection_input).astype(jnp.bfloat16)
    branch = project(attn_tokens, out_full) + seq_out(low_out, select_projection_output)
    middle = hidden_f + RESIDUAL_SCALE * branch
    gate_full, up_full, down_full = (
        lax.all_gather(gate_weight, ("dp", "seq"), axis=0, tiled=True),
        lax.all_gather(up_weight, ("dp", "seq"), axis=0, tiled=True),
        lax.all_gather(down_weight, ("dp", "seq"), axis=0, tiled=True),
    )
    ff_width = gate_full.shape[1]
    norm_two = rms_scale(middle, feedforward_norm_gain).astype(jnp.bfloat16)
    low_gu = seq_in(norm_two, select_gate_up_input).astype(jnp.bfloat16)
    gate = project(norm_two, gate_full) + seq_out(
        low_gu[..., :adapter_rank_size], select_gate_up_output[..., :ff_width]
    )
    up_proj = project(norm_two, up_full) + seq_out(
        low_gu[..., adapter_rank_size:], select_gate_up_output[..., ff_width:]
    )
    activation = (jax.nn.silu(gate) * up_proj).astype(jnp.bfloat16)
    low_down = seq_in(activation, select_down_input).astype(jnp.bfloat16)
    ffn = project(activation, down_full) + seq_out(low_down, select_down_output)
    mixed = (middle + RESIDUAL_SCALE * ffn).astype(jnp.bfloat16)
    gate_back, up_back, down_back = (
        lax.all_gather(gate_weight, ("dp", "seq"), axis=0, tiled=True),
        lax.all_gather(up_weight, ("dp", "seq"), axis=0, tiled=True),
        lax.all_gather(down_weight, ("dp", "seq"), axis=0, tiled=True),
    )
    grad_out = cotangent.astype(jnp.float32)
    grad_ffn = (RESIDUAL_SCALE * grad_out).astype(jnp.bfloat16)
    grad_low_down = seq_back(grad_ffn, select_down_output).astype(jnp.bfloat16)
    grad_act = project_t(grad_ffn, down_back) + seq_in_back(grad_low_down, select_down_input)
    g_down_out = seq_outer(low_down, grad_ffn)
    g_down_in = seq_outer(activation, grad_low_down)
    _, act_pull = jax.vjp(lambda gate_val, up_val: jax.nn.silu(gate_val) * up_val, gate, up_proj)
    grad_gate, grad_up = act_pull(grad_act)
    grad_gate = grad_gate.astype(jnp.bfloat16)
    grad_up = grad_up.astype(jnp.bfloat16)
    grad_low_gu = jnp.concatenate(
        [
            seq_back(grad_gate, select_gate_up_output[..., :ff_width]),
            seq_back(grad_up, select_gate_up_output[..., ff_width:]),
        ],
        axis=-1,
    ).astype(jnp.bfloat16)
    grad_norm_two = (
        project_t(grad_gate, gate_back)
        + project_t(grad_up, up_back)
        + seq_in_back(grad_low_gu, select_gate_up_input)
    )
    g_gu_out = jnp.concatenate(
        [
            seq_outer(low_gu[..., :adapter_rank_size], grad_gate),
            seq_outer(low_gu[..., adapter_rank_size:], grad_up),
        ],
        axis=-1,
    )
    g_gu_in = seq_outer(norm_two, grad_low_gu)
    _, second_pull = jax.vjp(lambda values: rms_scale(values, feedforward_norm_gain), middle)
    grad_middle = grad_out + second_pull(grad_norm_two)[0]
    query_back, key_back, value_back, out_back = (
        lax.all_gather(query_weight, ("dp", "seq"), axis=0, tiled=True),
        lax.all_gather(key_weight, ("dp", "seq"), axis=0, tiled=True),
        lax.all_gather(value_weight, ("dp", "seq"), axis=0, tiled=True),
        lax.all_gather(attention_output_weight, ("dp", "seq"), axis=0, tiled=True),
    )
    grad_branch = (RESIDUAL_SCALE * grad_middle).astype(jnp.bfloat16)
    grad_low_out = seq_back(grad_branch, select_projection_output).astype(jnp.bfloat16)
    grad_attn = (
        project_t(grad_branch, out_back) + seq_in_back(grad_low_out, select_projection_input)
    ).astype(jnp.bfloat16)
    g_o_out = seq_outer(low_out, grad_branch)
    g_o_in = seq_outer(attn_tokens, grad_low_out)
    grad_heads = lax.all_to_all(
        grad_attn.reshape(seq_count, tok_count, NH, HD),
        "seq",
        split_axis=2,
        concat_axis=1,
        tiled=True,
    )
    grad_q_heads, grad_k_heads, grad_v_heads = attend_backward(
        query_heads, key_heads, value_heads, all_segments, log_totals, grad_heads
    )
    grad_q_tok, grad_k_tok, grad_v_tok = (
        lax.all_to_all(grad_q_heads, "seq", split_axis=1, concat_axis=2, tiled=True),
        lax.all_to_all(grad_k_heads, "seq", split_axis=1, concat_axis=2, tiled=True),
        lax.all_to_all(grad_v_heads, "seq", split_axis=1, concat_axis=2, tiled=True),
    )
    grad_query = (
        rotate(grad_q_tok.astype(jnp.float32), cos_table, -sin_table)
        .reshape(seq_count, tok_count, width)
        .astype(jnp.bfloat16)
    )
    grad_key_sum = jnp.sum(
        grad_k_tok.astype(jnp.float32).reshape(seq_count, tok_count, KVH, groups, HD), axis=3
    )
    grad_key = (
        rotate(grad_key_sum, cos_table, -sin_table)
        .reshape(seq_count, tok_count, key_width)
        .astype(jnp.bfloat16)
    )
    grad_value_sum = jnp.sum(
        grad_v_tok.astype(jnp.float32).reshape(seq_count, tok_count, KVH, groups, HD), axis=3
    )
    grad_value = grad_value_sum.reshape(seq_count, tok_count, key_width).astype(jnp.bfloat16)
    grad_low_qkv = jnp.concatenate(
        [
            seq_back(grad_query, select_query_output),
            seq_back(grad_key, select_key_value_output[..., :key_width]),
            seq_back(grad_value, select_key_value_output[..., key_width:]),
        ],
        axis=-1,
    ).astype(jnp.bfloat16)
    grad_norm_one = (
        project_t(grad_query, query_back)
        + project_t(grad_key, key_back)
        + project_t(grad_value, value_back)
        + seq_in_back(grad_low_qkv, select_query_key_value_input)
    )
    g_q_out = seq_outer(low_qkv[..., :adapter_rank_size], grad_query)
    g_kv_out = jnp.concatenate(
        [
            seq_outer(low_qkv[..., adapter_rank_size : 2 * adapter_rank_size], grad_key),
            seq_outer(low_qkv[..., 2 * adapter_rank_size :], grad_value),
        ],
        axis=-1,
    )
    g_qkv_in = seq_outer(norm_one, grad_low_qkv)
    _, first_pull = jax.vjp(lambda values: rms_scale(values, attention_norm_gain), hidden_f)
    grad_hidden = (grad_middle + first_pull(grad_norm_one)[0]).astype(jnp.bfloat16)
    adapter_numbers = jnp.arange(adapter_query_key_value_input.shape[0], dtype=jnp.int32)
    chooser = (sequence_adapter_index[:, None] == adapter_numbers[None, :]).astype(jnp.float32)

    def spread(per_sequence):
        return jnp.einsum("sa,sij->aij", chooser, per_sequence, precision=lax.Precision.HIGHEST)

    summed = (
        lax.psum_scatter(spread(g_qkv_in), ("dp", "seq"), scatter_dimension=1, tiled=True),
        lax.psum_scatter(spread(g_q_out), ("dp", "seq"), scatter_dimension=2, tiled=True),
        lax.psum_scatter(spread(g_kv_out), ("dp", "seq"), scatter_dimension=2, tiled=True),
        lax.psum_scatter(spread(g_o_in), ("dp", "seq"), scatter_dimension=1, tiled=True),
        lax.psum_scatter(spread(g_o_out), ("dp", "seq"), scatter_dimension=2, tiled=True),
        lax.psum_scatter(spread(g_gu_in), ("dp", "seq"), scatter_dimension=1, tiled=True),
        lax.psum_scatter(spread(g_gu_out), ("dp", "seq"), scatter_dimension=2, tiled=True),
        lax.psum_scatter(spread(g_down_in), ("dp", "seq"), scatter_dimension=1, tiled=True),
        lax.psum_scatter(spread(g_down_out), ("dp", "seq"), scatter_dimension=2, tiled=True),
    )
    return (
        mixed,
        grad_hidden,
        summed[0],
        summed[1],
        summed[2],
        summed[3],
        summed[4],
        summed[5],
        summed[6],
        summed[7],
        summed[8],
    )


def solution(mesh):
    in_specs = (
        P("dp", "seq", None),
        P("dp", "seq"),
        P("dp"),
        P("dp", "seq", None),
        P(),
        P(),
        P(("dp", "seq"), None),
        P(("dp", "seq"), None),
        P(("dp", "seq"), None),
        P(("dp", "seq"), None),
        P(("dp", "seq"), None),
        P(("dp", "seq"), None),
        P(("dp", "seq"), None),
        P(),
        P(),
        P(),
        P(),
        P(),
        P(),
        P(),
        P(),
        P(),
    )
    out_specs = (
        P("dp", "seq", None),
        P("dp", "seq", None),
        P(None, ("dp", "seq"), None),
        P(None, None, ("dp", "seq")),
        P(None, None, ("dp", "seq")),
        P(None, ("dp", "seq"), None),
        P(None, None, ("dp", "seq")),
        P(None, ("dp", "seq"), None),
        P(None, None, ("dp", "seq")),
        P(None, ("dp", "seq"), None),
        P(None, None, ("dp", "seq")),
    )
    return jax.shard_map(local, mesh=mesh, in_specs=in_specs, out_specs=out_specs, check_vma=False)
```

profile of v0, /device:TPU:8, one launch (start us, length us, event | category | flops | bytes accessed | tf_op | source)
XLA Modules:
  0.0 2194.6 jit_solution(7147869503700385107)
XLA Ops:
  17.4 50.4 %all-gather.10.cloned.1.call-done = bf16[2048,512]{1,0:T(8,128)(2,1)} async-done(((bf16[64,512]{1,0:T(8,128)(2,1)}), bf16[2048,512]{1,0:T(8,128)(2,1)}) %all-gather.10.cloned.1.call-update) | async-done | bytes 2097168 | tf_op jit(solution)/shard_map/all_gather | solution.py:207
  71.0 4.9 all-to-all-start.1
  76.8 51.4 %all-gather.12.cloned.1.call-done = bf16[2048,512]{1,0:T(8,128)(2,1)} async-done(((bf16[64,512]{1,0:T(8,128)(2,1)}), bf16[2048,512]{1,0:T(8,128)(2,1)}) %all-gather.12.cloned.1.call-update) | async-done | bytes 2097168 | tf_op jit(solution)/shard_map/all_gather | solution.py:208
  131.5 5.5 all-to-all-start.2
  136.9 76.2 %all-gather.8.cloned.1.call-done = bf16[2048,2048]{1,0:T(8,128)(2,1)} async-done(((bf16[64,2048]{1,0:T(8,128)(2,1)}), bf16[2048,2048]{1,0:T(8,128)(2,1)}) %all-gather.8.cloned.1.call-update) | async-done | bytes 8388624 | tf_op jit(solution)/shard_map/all_gather | solution.py:206
  213.2 4.7 fusion.161
  222.6 3.9 all-to-all-start
  226.5 19.4 all_gather.31
  251.9 18.8 while.36
  257.8 3.6 fusion.242
  267.2 3.6 fusion.242
  273.1 3.3 reshape.1238
  276.4 5.4 all-to-all-start.3
  283.1 18.7 all-to-all-done.3
  301.8 3.5 reshape.1239
  311.0 5.5 fusion.163
  320.2 178.1 %all-gather.16.cloned.1.call-done = bf16[2048,8192]{1,0:T(8,128)(2,1)} async-done(((bf16[64,8192]{1,0:T(8,128)(2,1)}), bf16[2048,8192]{1,0:T(8,128)(2,1)}) %all-gather.16.cloned.1.call-update) | async-done | bytes 33554448 | tf_op jit(solution)/shard_map/all_gather | solution.py:246
  498.3 13.1 fusion.164
  514.1 180.1 %all-gather.18.cloned.1.call-done = bf16[2048,8192]{1,0:T(8,128)(2,1)} async-done(((bf16[64,8192]{1,0:T(8,128)(2,1)}), bf16[2048,8192]{1,0:T(8,128)(2,1)}) %all-gather.18.cloned.1.call-update) | async-done | bytes 33554448 | tf_op jit(solution)/shard_map/all_gather | solution.py:247
  694.1 13.1 fusion.165
  710.0 180.2 %all-gather.20.cloned.1.call-done = bf16[8192,2048]{1,0:T(8,128)(2,1)} async-done(((bf16[256,2048]{1,0:T(8,128)(2,1)}), bf16[8192,2048]{1,0:T(8,128)(2,1)}) %all-gather.20.cloned.1.call-update) | async-done | bytes 33554448 | tf_op jit(solution)/shard_map/all_gather | solution.py:248
  890.1 18.0 fusion.82
  908.1 8.6 multiply_convert_fusion.1
  918.1 16.0 fusion.167
  934.1 17.1 convolution_add_fusion.11
  953.5 6.4 fusion.155
  962.1 6.4 all-to-all-start.4
  968.9 3.5 copy.163
  972.3 4.6 reshape.1230
  977.0 3.8 all-to-all-done.4
  983.5 60.3 %while.37 = (s32[]{:T(128)}, f32[1,1024,4,64]{1,3,2,0:T(8,128)S(1)}, f32[1,1024,4,64]{1,3,2,0:T(8,128)}, bf16[2,1,512,4,64]{2,4,3,1,0:T(8,128)(2,1)}, s32[2]{0:T...) while((s32[]{:T(128)}, ...), condition=%wide.region_9.10_spmd.clone, body=%wide.region_7.9_spmd.clone.sunk | while | flops 1376778752 | bytes 132979592 | solution.py:156
  985.3 4.6 fusion.251
  991.9 5.8 multiply_reduce_fusion.3
  997.9 3.7 multiply_convert_fusion.6
  1001.6 3.3 fusion.253
  1005.0 4.7 fusion.255
  1009.6 3.6 fusion.254
  1015.0 4.6 fusion.251
  1021.5 5.7 multiply_reduce_fusion.3
  1027.5 3.7 multiply_convert_fusion.6
  1031.3 3.3 fusion.253
  1034.6 4.7 fusion.255
  1039.3 4.6 fusion.254
  1046.1 7.2 all-to-all-start.6
  1054.3 3.3 copy.167
  1057.6 4.6 reshape.1234
  1066.3 7.0 all-to-all-start.7
  1086.3 6.7 all-to-all-start.5
  1100.6 5.0 all-to-all-done.5
  1112.9 4.5 reshape.1226
  1120.6 4.5 reshape.1232
  1128.3 4.6 reshape.1236
  1136.3 3.1 copy.157
  1139.4 5.1 reshape.1224
  1154.9 13.9 fusion.166
  1172.3 6.4 fusion.168
  1183.8 58.0 %reduce-scatter.38.cloned.1.call-done = f32[64,128]{1,0:T(8,128)} async-done(((f32[2048,128]{1,0:T(8,128)}), f32[64,128]{1,0:T(8,128)}) %reduce-scatter.38.cloned.1.call-update) | async-done | bytes 32784
  1243.5 130.6 %reduce-scatter.32.cloned.1.call-done = f32[32,64]{1,0:T(8,128)} async-done(((f32[1024,64]{1,0:T(8,128)}), f32[32,64]{1,0:T(8,128)}) %reduce-scatter.32.cloned.1.call-update) | async-done | bytes 8208
  1375.6 131.9 %reduce-scatter.30.cloned.1.call-done = f32[64,64]{1,0:T(8,128)} async-done(((f32[2048,64]{1,0:T(8,128)}), f32[64,64]{1,0:T(8,128)}) %reduce-scatter.30.cloned.1.call-update) | async-done | bytes 16400
  1509.0 131.7 %reduce-scatter.36.cloned.1.call-done = f32[64,64]{1,0:T(8,128)} async-done(((f32[2048,64]{1,0:T(8,128)}), f32[64,64]{1,0:T(8,128)}) %reduce-scatter.36.cloned.1.call-update) | async-done | bytes 16400
  1642.4 131.9 %reduce-scatter.40.cloned.1.call-done = f32[64,64]{1,0:T(8,128)} async-done(((f32[2048,64]{1,0:T(8,128)}), f32[64,64]{1,0:T(8,128)}) %reduce-scatter.40.cloned.1.call-update) | async-done | bytes 16400
  1775.9 134.0 %reduce-scatter.28.cloned.1.call-done = f32[64,192]{1,0:T(8,128)} async-done(((f32[2048,192]{1,0:T(8,128)}), f32[64,192]{1,0:T(8,128)}) %reduce-scatter.28.cloned.1.call-update) | async-done | bytes 49168
  1911.6 134.1 %reduce-scatter.26.cloned.1.call-done = f32[4,256,16]{1,2,0:T(8,128)} async-done(((f32[4,8192,16]{1,2,0:T(8,128)}), f32[4,256,16]{1,2,0:T(8,128)}) %reduce-scatter.26.cloned.1.call-update) | async-done | bytes 65552 | tf_op jit(solution)/shard_map/reduce_scatter | solution.py:384
  2045.7 141.9 %reduce-scatter.24.cloned.1.call-done = f32[4,16,512]{2,1,0:T(8,128)} async-done(((f32[4,16,16384]{2,1,0:T(8,128)}), f32[4,16,512]{2,1,0:T(8,128)}) %reduce-scatter.24.cloned.1.call-update) | async-done | bytes 131088 | tf_op jit(solution)/shard_map/reduce_scatter | solution.py:383
  (317 shorter events, 140.6 us)
Async XLA Ops:
  7.2 504.2 %copy-start = (bf16[4,16,16384]{2,1,0:T(8,128)(2,1)S(1)}, bf16[4,16,16384]{2,1,0:T(8,128)(2,1)}, u32[]{:S(2)}) copy-start(bf16[4,16,16384]{2,1,0:T(8,128)(2,1)} %param.45) | copy-start | bytes 6291460
  7.2 7.2 copy-start.3
  7.2 7.2 copy-start.32
  7.2 60.6 %all-gather.10.cloned.1.call-start = ((), (), s32[]{:S(2)}) async-start(), calls=%async_computation.18 | async-start | bytes 2162688 | tf_op jit(solution)/shard_map/all_gather | solution.py:207
  8.0 120.3 %all-gather.12.cloned.1.call-start = ((), (), s32[]{:S(2)}) async-start(), calls=%async_computation.19 | async-start | bytes 2162688 | tf_op jit(solution)/shard_map/all_gather | solution.py:208
  8.7 204.4 %all-gather.8.cloned.1.call-start = ((), (), s32[]{:S(2)}) async-start(), calls=%async_computation.17 | async-start | bytes 8650752 | tf_op jit(solution)/shard_map/all_gather | solution.py:206
  9.4 301.6 %all-gather.14.cloned.1.call-start = ((), (), s32[]{:S(2)}) async-start(), calls=%async_computation.20 | async-start | bytes 8650752 | tf_op jit(solution)/shard_map/all_gather | solution.py:209
  10.0 488.3 %all-gather.16.cloned.1.call-start = ((), (), s32[]{:S(2)}) async-start(), calls=%async_computation.21 | async-start | bytes 34603008 | tf_op jit(solution)/shard_map/all_gather | solution.py:246
  10.6 683.5 %all-gather.18.cloned.1.call-start = ((), (), s32[]{:S(2)}) async-start(), calls=%async_computation.22 | async-start | bytes 34603008 | tf_op jit(solution)/shard_map/all_gather | solution.py:247
  11.2 879.0 %all-gather.20.cloned.1.call-start = ((), (), s32[]{:S(2)}) async-start(), calls=%async_computation.23 | async-start | bytes 34603008 | tf_op jit(solution)/shard_map/all_gather | solution.py:248
  13.8 63.0 %copy-start.47 = (f32[128]{0:T(128)}, f32[128]{0:T(128)S(1)}, u32[]{:S(2)}) copy-start(f32[128]{0:T(128)S(1)} %fusion.143) | copy-start | bytes 1540
  15.7 61.2 %copy-start.41 = (bf16[1,128,48]{1,2,0:T(8,128)(2,1)}, bf16[1,128,48]{1,2,0:T(8,128)(2,1)S(1)}, u32[]{:S(2)}) copy-start(bf16[1,128,48]{1,2,0:T(8,128)(2,1)S(1)} %fusion.65) | copy-start | bytes 36868
  16.4 59.5 %copy-start.36 = (f32[128,32]{0,1:T(8,128)}, f32[128,32]{0,1:T(8,128)S(1)}, u32[]{:S(2)}) copy-start(f32[128,32]{0,1:T(8,128)S(1)} %get-tuple-element.307) | copy-start | bytes 49156
  16.4 204.0 %copy-start.30 = (f32[128,32]{0,1:T(8,128)}, f32[128,32]{0,1:T(8,128)S(1)}, u32[]{:S(2)}) copy-start(f32[128,32]{0,1:T(8,128)S(1)} %get-tuple-element.308) | copy-start | bytes 49156
  71.0 59.5 %all-to-all-start.1 = ((bf16[1,128,32,64]{1,3,0,2:T(8,128)(2,1)}), bf16[1,128,32,64]{1,3,0,2:T(8,128)(2,1)S(1)}, u32[]{:S(2)}, u32[]{:S(2)}) async-start(bf16[1,128,32,64]{1,3,0,2:T(8,128)(2,1)} %bitcast.26), calls=%async_computation.1 | async-start | bytes 1048576 | tf_op jit(solution)/shard_map/all_to_all | solution.py:235
  130.5 82.6 %copy-start.26 = (bf16[1,128,32,64]{1,3,0,2:T(8,128)(2,1)}, bf16[1,128,32,64]{1,3,0,2:T(8,128)(2,1)S(1)}, u32[]{:S(2)}) copy-start(bf16[1,128,32,64]{1,3,0,2:T(8,128)(2,1)S(1)} %all-to-all-done.1) | copy-start | bytes 1572868
  131.5 91.1 %all-to-all-start.2 = ((bf16[1,128,32,64]{1,3,0,2:T(8,128)(2,1)}), bf16[1,128,32,64]{1,3,0,2:T(8,128)(2,1)}, u32[]{:S(2)}, u32[]{:S(2)}) async-start(bf16[1,128,32,64]{1,3,0,2:T(8,128)(2,1)} %bitcast.32), calls=%async_computation.2 | async-start | bytes 1048576 | tf_op jit(solution)/shard_map/all_to_all | solution.py:236
  217.9 8.6 copy-start.56
  222.6 26.5 %all-to-all-start = ((bf16[1,128,32,64]{1,3,0,2:T(8,128)(2,1)}), bf16[1,128,32,64]{1,3,0,2:T(8,128)(2,1)S(1)}, u32[]{:S(2)}, u32[]{:S(2)}) async-start(bf16[1,128,32,64]{1,3,0,2:T(8,128)(2,1)} %maximum_bitcast_fusion.1), calls=%async_computation | async-start | bytes 1048576 | tf_op jit(solution)/shard_map/all_to_all | solution.py:234
  276.4 25.4 %all-to-all-start.3 = ((bf16[8,2,16384]{2,1,0:T(2,128)(2,1)}), bf16[8,2,16384]{2,1,0:T(2,128)(2,1)}, u32[]{:S(2)}, u32[]{:S(2)}) async-start(bf16[8,2,16384]{2,1,0:T(2,128)(2,1)} %reshape.1238), calls=%async_computation.3 | async-start | bytes 1048576 | tf_op jit(solution)/shard_map/all_to_all | solution.py:239
  283.1 625.0 %copy-start.51 = (bf16[128,16]{0,1:T(8,128)(2,1)}, bf16[128,16]{0,1:T(8,128)(2,1)S(1)}, u32[]{:S(2)}) copy-start(bf16[128,16]{0,1:T(8,128)(2,1)S(1)} %convolution_convert_fusion.9) | copy-start | bytes 12292
  311.0 7.0 copy-start.46
  320.1 387.1 %copy-start.38 = (bf16[1,128,32]{1,2,0:T(8,128)(2,1)}, bf16[1,128,32]{1,2,0:T(8,128)(2,1)S(1)}, u32[]{:S(2)}) copy-start(bf16[1,128,32]{1,2,0:T(8,128)(2,1)S(1)} %fusion.66) | copy-start | bytes 24580
  916.8 17.3 copy-start.14
  934.1 17.1 copy-start.10
  934.1 18.8 copy-start.24
  953.2 6.7 copy-start.6
  953.5 15.0 copy-start.20
  962.1 18.7 all-to-all-start.4
  968.5 202.2 %reduce-scatter.34.cloned.1.call-start = ((), (), s32[]{:S(2)}) async-start(), calls=%async_computation.29 | async-start | bytes 1081344
  968.5 85.7 %copy-start.49 = (f32[4]{0:T(128)}, f32[4]{0:T(128)S(1)}, u32[]{:S(2)}) copy-start(f32[4]{0:T(128)S(1)} %compare_convert_fusion.1) | copy-start | bytes 52
  972.3 11.2 copy-start.16
  991.9 5.8 slice-start
  991.9 6.0 slice-start.1
  1001.6 8.0 copy-start.2
  1021.5 6.0 slice-start.1
  1031.3 8.0 copy-start.2
  1043.8 10.1 copy-start.18
  1046.1 20.2 all-to-all-start.6
  1053.4 188.5 %reduce-scatter.38.cloned.1.call-start = ((), (), s32[]{:S(2)}) async-start(), calls=%async_computation.31 | async-start | bytes 1081344
  1062.2 13.4 copy-start.25
  1062.2 13.6 copy-start.7
  1062.2 13.6 copy-start.43
  1066.3 20.0 all-to-all-start.7
  1075.6 8.6 copy-start.44
  1079.7 15.6 copy-start.31
  1079.8 15.6 copy-start.34
  1086.3 19.3 all-to-all-start.5
  1093.0 281.0 %reduce-scatter.32.cloned.1.call-start = ((), (), s32[]{:S(2)}) async-start(), calls=%async_computation.28 | async-start | bytes 540672
  1100.6 6.9 copy-start.35
  1107.7 399.8 %reduce-scatter.30.cloned.1.call-start = ((), (), s32[]{:S(2)}) async-start(), calls=%async_computation.27 | async-start | bytes 1081344
  1117.5 523.3 %reduce-scatter.36.cloned.1.call-start = ((), (), s32[]{:S(2)}) async-start(), calls=%async_computation.30 | async-start | bytes 1081344
  1125.2 649.1 %reduce-scatter.40.cloned.1.call-start = ((), (), s32[]{:S(2)}) async-start(), calls=%async_computation.32 | async-start | bytes 1081344
  1128.3 7.4 copy-start.5
  1128.3 7.4 copy-start.33
  1128.3 7.5 copy-start.48
  1128.3 7.8 copy-start.50
  1133.8 776.1 %reduce-scatter.28.cloned.1.call-start = ((), (), s32[]{:S(2)}) async-start(), calls=%async_computation.26 | async-start | bytes 2162688
  1144.6 901.2 %reduce-scatter.26.cloned.1.call-start = ((), (), s32[]{:S(2)}) async-start(), calls=%async_computation.25 | async-start | bytes 2162688 | tf_op jit(solution)/shard_map/reduce_scatter | solution.py:384
  1152.3 1035.4 %reduce-scatter.24.cloned.1.call-start = ((), (), s32[]{:S(2)}) async-start(), calls=%async_computation.24 | async-start | bytes 4325376 | tf_op jit(solution)/shard_map/reduce_scatter | solution.py:383
  1154.9 13.9 copy-start.11
  1154.9 13.9 copy-start.45
  1172.3 6.5 copy-start.21
  1180.4 1007.3 %copy-start.1 = (bf16[4,16,16384]{2,1,0:T(8,128)(2,1)S(1)}, bf16[4,16,16384]{2,1,0:T(8,128)(2,1)}, u32[]{:S(2)}) copy-start(bf16[4,16,16384]{2,1,0:T(8,128)(2,1)} %param.45) | copy-start | bytes 6291460
  (24 other events, 72.7 us)
Sparse Core Ops, SparseCore 0:
  11.0 56.7 all-gather.9
  70.8 57.4 all-gather.11
  131.2 81.8 all-gather.7
  216.0 85.1 all-gather.13
  304.0 194.2 all-gather.15
  501.1 192.9 all-gather.17
  697.1 192.9 all-gather.19
  977.1 131.2 reduce-scatter.33
  1110.7 131.1 reduce-scatter.37
  1244.0 130.0 reduce-scatter.31
  1376.4 131.0 reduce-scatter.29
  1509.5 131.1 reduce-scatter.35
  1643.1 131.1 reduce-scatter.39
  1776.4 133.4 reduce-scatter.27
  1912.7 132.9 reduce-scatter.25
  2048.4 139.1 reduce-scatter.23
where the time goes:
time: 2210 us; the launch traced here: 2190 us
  waiting for transfers between devices  1750 us (79%)
  matrix products  221 us (10%)
  local copies, waits for them, and re-layouts  107 us (5%)
  starting transfers between devices  47.5 us (2%)
  other arithmetic  31.8 us (1%)
    unnamed x23, waiting for transfers between devices  723 us
    all_gather x1, waiting for transfers between devices, local(): lax.all_gather(down_weight, ('dp', 'seq'), axis=0, tiled=True)  180 us
    all_gather x1, waiting for transfers between devices, local(): lax.all_gather(up_weight, ('dp', 'seq'), axis=0, tiled=True)  180 us
    all_gather x1, waiting for transfers between devices, local(): lax.all_gather(gate_weight, ('dp', 'seq'), axis=0, tiled=True)  178 us
    reduce_scatter x1, waiting for transfers between devices, local(): lax.psum_scatter(spread(g_gu_out), ('dp', 'seq'), scatter_dimension=2, ti...  142 us
    reduce_scatter x1, waiting for transfers between devices, local(): lax.psum_scatter(spread(g_down_in), ('dp', 'seq'), scatter_dimension=1, t...  134 us
    unnamed x145, local copies, waits for them, and re-layouts  81.3 us
    all_gather x1, waiting for transfers between devices, local(): lax.all_gather(query_weight, ('dp', 'seq'), axis=0, tiled=True)  76.2 us
  transfers between devices with their start and end apart: 24, of which 19 were waited for; matrix products, arithmetic and copies ran while one was open for 13% of the time, Pallas kernels for 0%

commit v1 on v0

v1 whole, which is shorter than its diff:
```python
import math

import jax
import jax.numpy as jnp
from jax import lax
from jax.sharding import PartitionSpec as P

NH = 32
KVH = 8
HD = 64

EPSILON = 1e-05
RESIDUAL_SCALE = 0.22
SCORE_SCALE = 1.0 / 64.0
ROPE_BASE = 10000000.0
BF16 = jnp.bfloat16
F32 = jnp.float32


def mm(a, b):
    return jnp.dot(a, b, preferred_element_type=F32)


def mm_t(a, b):
    return lax.dot_general(a, b, (((1,), (1,)), ((), ())), preferred_element_type=F32)


def t_mm(a, b):
    return lax.dot_general(a, b, (((0,), (0,)), ((), ())), preferred_element_type=F32)


def rms_scale(values, gain):
    mean_square = jnp.mean(values * values, axis=-1, keepdims=True)
    return values * lax.rsqrt(mean_square + EPSILON) * gain


def rms_back(values, gain, grad):
    r = lax.rsqrt(jnp.mean(values * values, axis=-1, keepdims=True) + EPSILON)
    z = grad * gain
    return r * z - r * r * r * values * jnp.mean(z * values, axis=-1, keepdims=True)


def angle_tables(positions, head_size):
    steps = jnp.arange(head_size // 2).astype(F32)
    frequency = jnp.exp(steps * (-2.0 * math.log(ROPE_BASE) / head_size))
    angles = positions[:, None] * frequency[None, :]
    return (jnp.cos(angles), jnp.sin(angles))


def rotate(values, cos_table, sin_table):
    half_width = values.shape[-1] // 2
    first_half = values[..., :half_width]
    second_half = values[..., half_width:]
    cos_part = cos_table[:, None, :]
    sin_part = sin_table[:, None, :]
    return jnp.concatenate(
        [
            first_half * cos_part - second_half * sin_part,
            second_half * cos_part + first_half * sin_part,
        ],
        axis=-1,
    )


def masked_scores(query_block, keys, seg_block, segments, start_row):
    key_pos = jnp.arange(keys.shape[0], dtype=jnp.int32)
    query_pos = start_row + jnp.arange(query_block.shape[0], dtype=jnp.int32)
    scores = jnp.einsum("qhd,kd->hqk", query_block, keys, preferred_element_type=F32) * SCORE_SCALE
    allowed = (key_pos[None, :] <= query_pos[:, None]) & (seg_block[:, None] == segments[None, :])
    return jnp.where(allowed[None], scores, -1e30)


def attend_forward(query, keys, values, segments):
    length, heads, head_size = query.shape
    rows = min(512, length)

    def one_block(index):
        start = index * rows
        query_block = lax.dynamic_slice_in_dim(query, start, rows, 0)
        seg_block = lax.dynamic_slice_in_dim(segments, start, rows, 0)
        scores = masked_scores(query_block, keys, seg_block, segments, start)
        row_max = jnp.max(scores, axis=-1, keepdims=True)
        weights = jnp.exp(scores - row_max)
        totals = jnp.sum(weights, axis=-1, keepdims=True)
        low = (weights / totals).astype(BF16)
        output = jnp.einsum("hqk,kd->qhd", low, values, preferred_element_type=F32)
        return (output.astype(BF16), (row_max + jnp.log(totals))[..., 0])

    outputs, log_totals = lax.map(one_block, jnp.arange(length // rows, dtype=jnp.int32))
    return (outputs.reshape(length, heads * head_size), log_totals)


def attend_backward(query, keys, values, segments, log_totals, grad):
    length, heads, head_size = query.shape
    rows = min(512, length)

    def one_block(carry, index):
        grad_keys, grad_values = carry
        start = index * rows
        query_block = lax.dynamic_slice_in_dim(query, start, rows, 0)
        seg_block = lax.dynamic_slice_in_dim(segments, start, rows, 0)
        grad_block = lax.dynamic_slice_in_dim(grad, start, rows, 0)
        scores = masked_scores(query_block, keys, seg_block, segments, start)
        weights = jnp.exp(scores - log_totals[index][..., None])
        grad_weights = jnp.einsum("qhd,kd->hqk", grad_block, values, preferred_element_type=F32)
        row_dot = jnp.sum(weights * grad_weights, axis=-1, keepdims=True)
        grad_scores = (weights * (grad_weights - row_dot)).astype(BF16)
        grad_query = jnp.einsum("hqk,kd->qhd", grad_scores, keys, preferred_element_type=F32)
        grad_keys = grad_keys + jnp.einsum(
            "hqk,qhd->kd", grad_scores, query_block, preferred_element_type=F32
        )
        grad_values = grad_values + jnp.einsum(
            "hqk,qhd->kd", weights.astype(BF16), grad_block, preferred_element_type=F32
        )
        return ((grad_keys, grad_values), (grad_query * SCORE_SCALE).astype(BF16))

    zero = jnp.zeros(keys.shape, F32)
    (grad_keys, grad_values), grad_query = lax.scan(
        one_block, (zero, zero), jnp.arange(length // rows, dtype=jnp.int32)
    )
    return (grad_query.reshape(length, heads, head_size), grad_keys * SCORE_SCALE, grad_values)


def make_local(dp_size, seq_size):
    devices = dp_size * seq_size
    heads = NH // seq_size
    kv_repeat = max(1, seq_size // KVH)

    def local(
        hidden,
        token_document_numbers,
        sequence_adapter_index,
        cotangent,
        attention_norm_gain,
        feedforward_norm_gain,
        query_weight,
        key_weight,
        value_weight,
        attention_output_weight,
        gate_weight,
        up_weight,
        down_weight,
        adapter_query_key_value_input,
        adapter_query_output,
        adapter_key_value_output,
        adapter_projection_input,
        adapter_projection_output,
        adapter_gate_up_input,
        adapter_gate_up_output,
        adapter_down_input,
        adapter_down_output,
    ):
        tokens, width = hidden.shape[1:]
        length = tokens * seq_size
        rows = query_weight.shape[0]
        key_width = key_weight.shape[1]
        ff_width = gate_weight.shape[1]
        ff_block = ff_width // devices
        rank = adapter_projection_input.shape[2]
        adapters = adapter_projection_input.shape[0]
        me = lax.axis_index("seq")
        q_width = heads * HD

        def across(piece):
            return lax.all_to_all(piece, "seq", split_axis=0, concat_axis=0, tiled=True)

        def gather_dp(block):
            return lax.all_gather(block, "dp", axis=0, tiled=True)

        def gather_seq(block):
            return lax.all_gather(block, "seq", axis=0, tiled=True)

        def scatter_seq(total):
            return lax.psum_scatter(total, "seq", scatter_dimension=0, tiled=True)

        def by_owner(columns):
            return columns.reshape(columns.shape[0], dp_size, seq_size, ff_block)

        hidden_own = hidden[0].astype(F32)
        hidden_all = gather_seq(hidden[0])
        segments = gather_seq(token_document_numbers[0])
        kv = jnp.stack([key_weight.reshape(rows, KVH, HD), value_weight.reshape(rows, KVH, HD)], 2)
        kv = jnp.repeat(kv.reshape(rows, KVH, 2 * HD), kv_repeat, axis=1)
        qkv = jnp.concatenate([query_weight.reshape(rows, seq_size, q_width), kv], axis=2)
        qkv = across(jnp.swapaxes(qkv, 0, 1)).reshape(seq_size * rows, q_width + 2 * HD)
        qkv = gather_dp(qkv)
        gate_up = jnp.concatenate([by_owner(gate_weight), by_owner(up_weight)], axis=1)
        gate_up = across(jnp.transpose(gate_up, (2, 0, 1, 3)))
        gate_up = gather_dp(gate_up.reshape(seq_size * rows, 2 * dp_size * ff_block))
        down = gather_dp(down_weight)
        out_full = lax.all_gather(attention_output_weight, ("dp", "seq"), axis=0, tiled=True)
        ff_own = dp_size * ff_block

        adapter = sequence_adapter_index[0]
        qkv_in = adapter_query_key_value_input[adapter]
        q_out = lax.dynamic_slice_in_dim(adapter_query_output[adapter], me * q_width, q_width, 1)
        kv_out = adapter_key_value_output[adapter]
        kv_start = (me // kv_repeat) * HD
        k_out = lax.dynamic_slice_in_dim(kv_out, kv_start, HD, 1)
        v_out = lax.dynamic_slice_in_dim(kv_out, key_width + kv_start, HD, 1)
        o_in = adapter_projection_input[adapter]
        o_out = adapter_projection_output[adapter]
        gu_in = adapter_gate_up_input[adapter]
        gu_all = adapter_gate_up_output[adapter].reshape(rank, 2, dp_size, seq_size, ff_block)
        gu_out = lax.dynamic_index_in_dim(gu_all, me, 3, keepdims=False)
        g_out, u_out = gu_out[:, 0].reshape(rank, ff_own), gu_out[:, 1].reshape(rank, ff_own)
        down_all = adapter_down_input[adapter].reshape(dp_size, seq_size, ff_block, rank)
        down_in = lax.dynamic_index_in_dim(down_all, me, 1, keepdims=False).reshape(ff_own, rank)
        down_out = adapter_down_output[adapter]

        norm_one = rms_scale(hidden_all.astype(F32), attention_norm_gain).astype(BF16)
        low_qkv = mm(norm_one, qkv_in).astype(BF16)
        pre = mm(norm_one, qkv)
        query_pre = pre[:, :q_width] + mm(low_qkv[:, :rank], q_out)
        key_pre = pre[:, q_width : q_width + HD] + mm(low_qkv[:, rank : 2 * rank], k_out)
        value_pre = pre[:, q_width + HD :] + mm(low_qkv[:, 2 * rank :], v_out)
        cos_table, sin_table = angle_tables(jnp.arange(length, dtype=jnp.int32).astype(F32), HD)
        query = rotate(query_pre.reshape(length, heads, HD), cos_table, sin_table).astype(BF16)
        keys = rotate(key_pre.reshape(length, 1, HD), cos_table, sin_table).astype(BF16)[:, 0]
        values = value_pre.astype(BF16)
        attn_heads, log_totals = attend_forward(query, keys, values, segments)
        attn = lax.all_gather(attn_heads, "seq", axis=1, tiled=True)
        low_out = mm(attn, o_in).astype(BF16)
        branch = mm(attn, out_full) + mm(low_out, o_out)
        middle = hidden_all.astype(F32) + RESIDUAL_SCALE * branch
        own_row = me * tokens
        middle_own = lax.dynamic_slice_in_dim(middle, own_row, tokens, 0)
        norm_two = rms_scale(middle, feedforward_norm_gain).astype(BF16)
        low_gu = mm(norm_two, gu_in).astype(BF16)
        wide = mm(norm_two, gate_up)
        gate = wide[:, :ff_own] + mm(low_gu[:, :rank], g_out)
        up_proj = wide[:, ff_own:] + mm(low_gu[:, rank:], u_out)
        sigma = jax.nn.sigmoid(gate)
        activation = (gate * sigma * up_proj).astype(BF16)
        low_down = mm(activation, down_in).astype(BF16)
        ffn = scatter_seq((mm(activation, down) + mm(low_down, down_out)).astype(BF16))
        mixed = (middle_own + RESIDUAL_SCALE * ffn.astype(F32)).astype(BF16)

        grad_ffn = gather_seq((RESIDUAL_SCALE * cotangent[0].astype(F32)).astype(BF16))
        grad_low_down = mm_t(grad_ffn, down_out).astype(BF16)
        grad_act = mm_t(grad_ffn, down) + mm_t(grad_low_down, down_in)
        grad_gate = (grad_act * up_proj * sigma * (1.0 + gate * (1.0 - sigma))).astype(BF16)
        grad_up = (grad_act * gate * sigma).astype(BF16)
        grad_low_gu = jnp.concatenate([mm_t(grad_gate, g_out), mm_t(grad_up, u_out)], axis=1)
        grad_low_gu = grad_low_gu.astype(BF16)
        grad_norm_two = scatter_seq(
            (
                mm_t(jnp.concatenate([grad_gate, grad_up], axis=1), gate_up)
                + mm_t(grad_low_gu, gu_in)
            ).astype(BF16)
        )
        grad_middle = cotangent[0].astype(F32) + rms_back(
            middle_own, feedforward_norm_gain, grad_norm_two.astype(F32)
        )
        grad_branch = (RESIDUAL_SCALE * grad_middle).astype(BF16)
        grad_low_out = mm_t(grad_branch, o_out).astype(BF16)
        grad_attn = (mm_t(grad_branch, out_full) + mm_t(grad_low_out, o_in)).astype(BF16)
        grad_heads = lax.all_to_all(
            jnp.swapaxes(grad_attn.reshape(tokens, seq_size, q_width), 0, 1),
            "seq",
            split_axis=0,
            concat_axis=0,
            tiled=True,
        ).reshape(length, heads, HD)
        grad_q, grad_k, grad_v = attend_backward(
            query, keys, values, segments, log_totals, grad_heads
        )
        grad_query = rotate(grad_q.astype(F32), cos_table, -sin_table)
        grad_query = grad_query.reshape(length, q_width).astype(BF16)
        grad_key = rotate(grad_k[:, None], cos_table, -sin_table)[:, 0].astype(BF16)
        grad_value = grad_v.astype(BF16)
        grad_low_qkv = jnp.concatenate(
            [mm_t(grad_query, q_out), mm_t(grad_key, k_out), mm_t(grad_value, v_out)], axis=1
        ).astype(BF16)
        grad_qkv = jnp.concatenate([grad_query, grad_key, grad_value], axis=1)
        grad_norm_one = scatter_seq((mm_t(grad_qkv, qkv) + mm_t(grad_low_qkv, qkv_in)).astype(BF16))
        grad_hidden = grad_middle + rms_back(
            hidden_own, attention_norm_gain, grad_norm_one.astype(F32)
        )

        attn_own = lax.dynamic_slice_in_dim(attn, own_row, tokens, 0)
        low_out_own = lax.dynamic_slice_in_dim(low_out, own_row, tokens, 0)
        partial = jnp.concatenate(
            [
                t_mm(norm_one, grad_low_qkv),
                t_mm(attn_own, grad_low_out),
                t_mm(grad_branch, low_out_own),
                t_mm(norm_two, grad_low_gu),
                t_mm(grad_ffn, low_down),
            ],
            axis=1,
        ).reshape(dp_size, seq_size, rows, 8 * rank)
        own_q = t_mm(grad_query, low_qkv[:, :rank])
        own_k = t_mm(grad_key, low_qkv[:, rank : 2 * rank])
        own_v = t_mm(grad_value, low_qkv[:, 2 * rank :])
        own_g = t_mm(grad_gate, low_gu[:, :rank]).reshape(dp_size, ff_block, rank)
        own_u = t_mm(grad_up, low_gu[:, rank:]).reshape(dp_size, ff_block, rank)
        own_d = t_mm(activation, grad_low_down).reshape(dp_size, ff_block, rank)

        def placed(block, total, start, axis):
            empty = list(block.shape)
            empty[axis] = total
            return lax.dynamic_update_slice_in_dim(jnp.zeros(empty, F32), block, start, axis)

        def by_target(whole):
            return whole.reshape(dp_size, seq_size, -1)

        full_q = placed(own_q, width, me * q_width, 0)
        full_kv = jnp.concatenate(
            [placed(own_k, key_width, kv_start, 0), placed(own_v, key_width, kv_start, 0)], axis=0
        )
        spot = [placed(v[:, None], seq_size, me, 1) for v in (own_g, own_u, own_d)]
        full_gu = jnp.concatenate([spot[0].reshape(ff_width, rank), spot[1].reshape(ff_width, rank)])
        pieces = [by_target(v) for v in (partial, full_q, full_kv, full_gu, spot[2])]
        send = jnp.concatenate(pieces, axis=2)
        send = jnp.swapaxes(send, 0, 1).reshape(seq_size, -1)
        mine = lax.psum_scatter(send, "seq", scatter_dimension=0, tiled=True)
        mine = lax.all_to_all(
            mine.reshape(dp_size, -1), "dp", split_axis=0, concat_axis=0, tiled=True
        )
        owners = lax.all_gather(sequence_adapter_index, "dp", axis=0, tiled=True)
        numbers = jnp.arange(adapters, dtype=jnp.int32)
        chooser = (owners[:, None] == numbers[None, :]).astype(F32)
        mine = jnp.einsum("sa,si->ai", chooser, mine, precision=lax.Precision.HIGHEST)
        sizes = [v.shape[2] for v in pieces]
        cuts = [sum(sizes[:i]) for i in range(1, len(sizes))]
        got, got_q, got_kv, got_gu, got_d = jnp.split(mine, cuts, axis=1)
        got = got.reshape(adapters, rows, 8 * rank)

        def turned(flat):
            return jnp.swapaxes(flat.reshape(adapters, -1, rank), 1, 2)

        return (
            mixed[None],
            grad_hidden.astype(BF16)[None],
            got[:, :, : 3 * rank],
            turned(got_q),
            turned(got_kv),
            got[:, :, 3 * rank : 4 * rank],
            jnp.swapaxes(got[:, :, 4 * rank : 5 * rank], 1, 2),
            got[:, :, 5 * rank : 7 * rank],
            turned(got_gu),
            got_d.reshape(adapters, ff_block, rank),
            jnp.swapaxes(got[:, :, 7 * rank :], 1, 2),
        )

    return local


def solution(mesh):
    both = ("dp", "seq")
    tokens = P("dp", "seq", None)
    weight = P(both, None)
    in_specs = (
        (tokens, P("dp", "seq"), P("dp"), tokens, P(), P()) + (weight,) * 7 + (P(),) * 9
    )
    by_row, by_column = P(None, both, None), P(None, None, both)
    out_specs = (
        tokens,
        tokens,
        by_row,
        by_column,
        by_column,
        by_row,
        by_column,
        by_row,
        by_column,
        by_row,
        by_column,
    )
    local = make_local(mesh.shape["dp"], mesh.shape["seq"])
    return jax.shard_map(local, mesh=mesh, in_specs=in_specs, out_specs=out_specs, check_vma=False)
```

time: 2210 us -> 839 us (0.38)
  waiting for transfers between devices: 1750 us -> 382 us
  blocking collectives: 19.4 us -> 101 us
  matrix products: 221 us -> 172 us
  starting transfers between devices: 47.5 us -> 13 us
    unnamed x23 -> x12, waiting for transfers between devices: 723 us -> 66.2 us
    all_gather x6, waiting for transfers between devices: 716 us -> 158 us  [the longest x3 109 us: gather_dp(): return lax.all_gather(block, 'dp', axis=0, tiled=True)]
    reduce_scatter x2 -> x3, waiting for transfers between devices: 276 us -> 80.1 us  [scatter_seq(): return lax.psum_scatter(total, 'seq', scatter_dimension=0, tiled=True)]
    all_to_all x0 -> x2, blocking collectives: none -> 81.3 us  [across(): return lax.all_to_all(piece, 'seq', split_axis=0, concat_axis=0, tiled=True)]
    all_gather x1, waiting for transfers between devices: 0.02 us -> 77.7 us  [local(): lax.all_gather(attention_output_weight, ('dp', 'seq'), axis=0, tiled=True)]
    dot_general x61 -> x53, matrix products: 221 us -> 164 us  [the longest x15 57.1 us: mm(): return jnp.dot(a, b, preferred_element_type=F32)]
    unnamed x145 -> x141, local copies, waits for them, and re-layouts: 81.3 us -> 36 us
    all_to_all x8 -> x2, starting transfers between devices: 47 us -> 12.2 us  [the longest x1 8.46 us: local(): lax.all_to_all(jnp.swapaxes(grad_attn.reshape(tokens, seq_size, q_width),...]
  transfers between devices with their start and end apart: 24 -> 13, of which waited for: 19 -> 10; matrix products, arithmetic and copies ran while one was open for 13% -> 20% of each run, Pallas kernels for 0% -> 0%
where the time goes in v1:
time: 839 us; the launch traced here: 829 us
  waiting for transfers between devices  382 us (46%)
  matrix products  172 us (21%)
  local copies, waits for them, and re-layouts  103 us (12%)
  blocking collectives  101 us (12%)
  other arithmetic  34.9 us (4%)
  between operations  15.9 us (2%)
  starting transfers between devices  13 us (2%)
    all_gather x3, waiting for transfers between devices, gather_dp(): return lax.all_gather(block, 'dp', axis=0, tiled=True)  109 us
    all_to_all x2, blocking collectives, across(): return lax.all_to_all(piece, 'seq', split_axis=0, concat_axis=0, tiled=True)  81.3 us
    reduce_scatter x3, waiting for transfers between devices, scatter_seq(): return lax.psum_scatter(total, 'seq', scatter_dimension=0, tiled=True)  80.1 us
    all_gather x1, waiting for transfers between devices, local(): lax.all_gather(attention_output_weight, ('dp', 'seq'), axis=0, tiled=True)  77.7 us
    unnamed x12, waiting for transfers between devices  66.2 us
    dot_general x15, matrix products, mm(): return jnp.dot(a, b, preferred_element_type=F32)  57.1 us
    dot_general x15, matrix products, mm_t(): lax.dot_general(a, b, (((1,), (1,)), ((), ())), preferred_element_type=F32)  49.2 us
    all_gather x1, waiting for transfers between devices, local(): attn = lax.all_gather(attn_heads, 'seq', axis=1, tiled=True)  37.4 us
  transfers between devices with their start and end apart: 13, of which 10 were waited for; matrix products, arithmetic and copies ran while one was open for 20% of the time, Pallas kernels for 0%

profile of v1, /device:TPU:8, one launch (start us, length us, event | category | flops | bytes accessed | tf_op | source)
XLA Modules:
  0.0 828.6 jit_solution(10794050840830408316)
XLA Ops:
  12.0 23.4 %all_to_all.27 = bf16[8,64,384]{2,1,0:T(8,128)(2,1)} all-to-all(bf16[8,64,384]{2,1,0:T(8,128)(2,1)S(1)} %copy.149), channel_id=1, replica_groups=mesh['dp'=4,'seq'=8] {'seq'}, dimensions={0} | all-to-all | bytes 786432 | tf_op jit(solution)/shard_map/all_to_all | solution.py:165
  37.7 11.8 %all-gather.1 = s32[1,1024]{1,0:T(1,128)S(1)} all-gather(s32[1,128]{1,0:T(1,128)S(1)} %copy-done.54), channel_id=3, replica_groups=mesh['dp'=4,'seq'=8] {'seq'}, dimensions={1}, use_global_device_ids=true | all-gather | bytes 4608 | tf_op jit(solution)/shard_map/all_gather | solution.py:171
  50.7 10.8 %all-gather.22.cloned.1.call-done = bf16[1,1024,2048]{2,1,0:T(8,128)(2,1)} async-done(((bf16[1,128,2048]{2,1,0:T(8,128)(2,1)}), bf16[1,1024,2048]{2,1,0:T(8,128)(2,1)}) %all-gather.22.cloned.1.call-update) | async-done | bytes 4194320 | tf_op jit(solution)/shard_map/all_gather | solution.py:171
  61.5 3.2 fusion.48
  70.2 26.3 %all-gather.10.cloned.1.call-done = bf16[2048,384]{1,0:T(8,128)(2,1)} async-done(((bf16[512,384]{1,0:T(8,128)(2,1)}), bf16[2048,384]{1,0:T(8,128)(2,1)}) %all-gather.10.cloned.1.call-update) | async-done | bytes 1572880 | tf_op jit(solution)/shard_map/all_gather | solution.py:168
  96.5 4.5 fusion.169
  105.0 18.1 %while.27 = (s32[]{:T(128)}, bf16[2,512,4,64]{1,3,2,0:T(8,128)(2,1)S(1)}, f32[2,4,512]{2,1,0:T(4,128)S(1)}, s32[2]{0:T(128)S(1)}, s32[1024]{0:T(1024)S(1)}, /*in...) while((s32[]{:T(128)}, ...), condition=%wide.region_4.5_spmd, body=%wide.region_1.4_spmd.sunk | while | flops 563739136 | bytes 28129476 | solution.py:89
  108.5 2.4 fusion.241
  111.0 3.1 fusion.242
  117.5 2.4 fusion.241
  120.0 3.1 fusion.242
  129.3 57.9 %all_to_all.28 = bf16[8,64,8,256]{3,2,1,0:T(8,128)(2,1)S(1)} all-to-all(bf16[8,64,8,256]{3,2,1,0:T(8,128)(2,1)S(1)} %maximum_bitcast_fusion), channel_id=1, replica_groups=mesh['dp'=4,'seq'=8] {'seq'}, dimensions={0} | all-to-all | bytes 4194304 | tf_op jit(solution)/shard_map/all_to_all | solution.py:165
  191.1 3.4 convolution_convert_fusion.7
  194.4 18.0 %all-gather.18.cloned.1.call-done = bf16[1024,2048]{1,0:T(8,128)(2,1)} async-done(((bf16[256,2048]{1,0:T(8,128)(2,1)}), bf16[1024,2048]{1,0:T(8,128)(2,1)}) %all-gather.18.cloned.1.call-update) | async-done | bytes 4194320 | tf_op jit(solution)/shard_map/all_gather | solution.py:168
  212.4 7.6 fusion.173
  220.0 2.7 convolution_add_fusion.1
  222.7 37.4 %all-gather.12.cloned.1.call-done = bf16[1024,2048]{0,1:T(8,128)(2,1)} async-done(((bf16[1024,256]{0,1:T(8,128)(2,1)}), bf16[1024,2048]{0,1:T(8,128)(2,1)}) %all-gather.12.cloned.1.call-update) | async-done | bytes 4194320 | tf_op jit(solution)/shard_map/all_gather | solution.py:222
  260.1 2.9 convolution_convert_fusion.4
  263.0 77.7 %all-gather.14.cloned.1.call-done = bf16[2048,2048]{1,0:T(8,128)(2,1)} async-done(((bf16[64,2048]{1,0:T(8,128)(2,1)}), bf16[2048,2048]{1,0:T(8,128)(2,1)}) %all-gather.14.cloned.1.call-update) | async-done | bytes 8388624 | tf_op jit(solution)/shard_map/all_gather | solution.py:191
  340.7 13.1 %fusion.170 = f32[1024,2048]{1,0:T(8,128)S(1)} fusion(bf16[1024,2048]{0,1:T(8,128)(2,1)} %all-gather.12.cloned.1.call-done, bf16[2048,2048]{1,0:T(8,128)(2,1)} %all-gather.14.cloned.1.call-done), kind=kOutput, calls=%fused_computation.275 | convolution fusion | flops 8589934592 | bytes 20971520 | tf_op jit(solution)/shard_map/dot_general | solution.py:21
  353.8 3.3 multiply_reduce_fusion
  357.9 2.4 copy-done.7
  363.6 65.1 %all-gather.16.cloned.1.call-done = bf16[2048,2048]{1,0:T(8,128)(2,1)} async-done(((bf16[512,2048]{1,0:T(8,128)(2,1)}), bf16[2048,2048]{1,0:T(8,128)(2,1)}) %all-gather.16.cloned.1.call-update) | async-done | bytes 8388624 | tf_op jit(solution)/shard_map/all_gather | solution.py:168
  428.7 12.6 %fusion.171 = f32[1024,2048]{1,0:T(8,128)S(1)} fusion(bf16[1024,2048]{1,0:T(8,128)(2,1)} %copy-done.3, bf16[2048,2048]{1,0:T(8,128)(2,1)} %all-gather.16.cloned.1.call-done), kind=kOutput, calls=%fused_computation.276 | convolution fusion | flops 8589934592 | bytes 20971520 | tf_op jit(solution)/shard_map/dot_general | solution.py:21
  443.5 2.8 multiply_convert_fusion.2
  447.7 12.1 %fusion.51 = f32[1024,2048]{1,0:T(8,128)S(1)} fusion(bf16[2048,2048]{1,0:T(8,128)(2,1)} %all-gather.16.cloned.1.call-done, bf16[1024,1024]{1,0:T(8,128)(2,1)S(1)} %get-tuple-element.270, bf16[1024,1024]{1,0:T(8,128)(2,1)S(1)} %get-tuple-element.268), kind=kOutput, calls=%fused_computation.71 | convolution fusion | flops 8598323200 | bytes 20971520 | tf_op jit(solution)/shard_map/dot_general | solution.py:25
  459.8 3.3 add_convert_fusion.1
  463.8 6.5 fusion.172
  470.3 3.3 add_convert_fusion.2
  473.7 2.5 fusion.123
  476.2 2.5 broadcast.297.clone.1
  479.6 2.8 copy.188
  482.4 2.6 fusion.120
  485.0 2.5 broadcast.297.clone
  488.4 3.5 copy.190
  491.9 17.4 %reduce-scatter.6.cloned.1.call-done = bf16[128,2048]{1,0:T(8,128)(2,1)} async-done(((bf16[1024,2048]{1,0:T(8,128)(2,1)}), bf16[128,2048]{1,0:T(8,128)(2,1)}) %reduce-scatter.6.cloned.1.call-update) | async-done | bytes 524304 | tf_op jit(solution)/shard_map/reduce_scatter | solution.py:174
  511.0 48.8 %reduce-scatter.4.cloned.1.call-done = bf16[128,2048]{1,0:T(8,128)(2,1)} async-done(((bf16[1024,2048]{1,0:T(8,128)(2,1)}), bf16[128,2048]{1,0:T(8,128)(2,1)}) %reduce-scatter.4.cloned.1.call-update) | async-done | bytes 524304 | tf_op jit(solution)/shard_map/reduce_scatter | solution.py:174
  559.9 2.7 convert_add_fusion.1
  563.6 6.3 fusion.165
  571.9 8.5 %all-to-all-start.2 = ((bf16[8,128,256]{2,1,0:T(8,128)(2,1)}), bf16[8,128,256]{2,1,0:T(8,128)(2,1)}, u32[]{:S(2)}, u32[]{:S(2)}) async-start(bf16[8,128,256]{2,1,0:T(8,128)(2,1)} %bitcast.285), calls=%async_computation.4 | async-start | bytes 1048576 | tf_op jit(solution)/shard_map/all_to_all | solution.py:258
  581.5 4.7 copy.170
  586.2 8.7 %reshape.488 = f32[4,8,8192]{2,1,0:T(8,128)} reshape(f32[16384,16]{1,0:T(8,128)} %copy.170) | data formatting | bytes 2097152 | tf_op jit(solution)/shard_map/reshape | solution.py:306
  594.9 2.5 fusion.174
  597.4 2.5 broadcast.297.clone.2
  600.7 5.4 reshape.489
  608.6 59.3 %while.28 = (s32[]{:T(128)}, f32[1024,64]{0,1:T(8,128)S(1)}, f32[1024,64]{0,1:T(8,128)}, bf16[2,512,4,64]{1,3,2,0:T(8,128)(2,1)}, s32[2]{0:T(128)S(1)}, /*index=...) while((s32[]{:T(128)}, f32[1024,64]{0,1:T(8,128)S(1)}, ...), condition=%wide.region_13.14_spmd.clone, body=%wide.region_11.13_spmd.clone.sunk | while | flops 1375730176 | bytes 109779816 | solution.py:118
  610.9 4.6 fusion.251
  617.5 5.4 fusion.253
  623.4 2.4 fusion.254
  629.9 3.1 fusion.255
  633.0 5.5 fusion.256
  640.3 4.6 fusion.251
  646.9 5.4 fusion.253
  652.8 2.4 fusion.254
  659.3 3.1 fusion.255
  662.4 5.5 fusion.256
  684.8 2.5 reshape_reshape.3
  700.8 4.4 add_convert_fusion
  705.2 64.4 %all-reduce.4.cloned.1.call-done = f32[8,88064]{1,0:T(8,128)} async-done(((f32[8,88064]{1,0:T(8,128)}), f32[8,88064]{1,0:T(8,128)}) %all-reduce.4.cloned.1.call-update) | async-done | bytes 2818064
  769.6 3.4 constant_dynamic-slice_fusion.7
  773.0 3.8 all-to-all-start.3
  778.2 7.9 all-reduce
  804.0 13.9 %reduce-scatter.8.cloned.1.call-done = bf16[128,2048]{1,0:T(8,128)(2,1)} async-done(((bf16[1024,2048]{1,0:T(8,128)(2,1)}), bf16[128,2048]{1,0:T(8,128)(2,1)}) %reduce-scatter.8.cloned.1.call-update) | async-done | bytes 524304 | tf_op jit(solution)/shard_map/reduce_scatter | solution.py:174
  819.4 2.5 fusion.71
  (304 shorter events, 114.0 us)
Async XLA Ops:
  7.2 182.1 %copy-start = (bf16[4,16,16384]{2,1,0:T(8,128)(2,1)S(1)}, bf16[4,16,16384]{2,1,0:T(8,128)(2,1)}, u32[]{:S(2)}) copy-start(bf16[4,16,16384]{2,1,0:T(8,128)(2,1)} %param.45) | copy-start | bytes 6291460
  7.2 28.3 %copy-start.19 = (bf16[1,128,2048]{2,1,0:T(8,128)(2,1)S(1)}, bf16[1,128,2048]{2,1,0:T(8,128)(2,1)}, u32[]{:S(2)}) copy-start(bf16[1,128,2048]{2,1,0:T(8,128)(2,1)} %param.29) | copy-start | bytes 1572868
  7.2 30.5 %copy-start.54 = (s32[1,128]{1,0:T(1,128)S(1)}, s32[1,128]{1,0:T(1,128)}, u32[]{:S(2)}) copy-start(s32[1,128]{1,0:T(1,128)} %param.27) | copy-start | bytes 1540
  7.2 54.3 %all-gather.22.cloned.1.call-start = ((), (), s32[]{:S(2)}) async-start(), calls=%async_computation.16 | async-start | bytes 4718592 | tf_op jit(solution)/shard_map/all_gather | solution.py:171
  8.0 88.5 %all-gather.10.cloned.1.call-start = ((), (), s32[]{:S(2)}) async-start(), calls=%async_computation.7 | async-start | bytes 1966080 | tf_op jit(solution)/shard_map/all_gather | solution.py:168
  12.0 52.7 %copy-start.47 = (f32[2048]{0:T(1024)S(1)}, f32[2048]{0:T(1024)}, u32[]{:S(2)}) copy-start(f32[2048]{0:T(1024)} %param.30) | copy-start | bytes 24580
  35.4 155.7 %all-gather.20.cloned.1.call-start = ((), (), s32[]{:S(2)}) async-start(), calls=%async_computation.13 | async-start | bytes 4718592 | tf_op jit(solution)/shard_map/all_gather | solution.py:171
  36.4 176.1 %all-gather.18.cloned.1.call-start = ((), (), s32[]{:S(2)}) async-start(), calls=%async_computation.11 | async-start | bytes 5242880 | tf_op jit(solution)/shard_map/all_gather | solution.py:168
  37.0 223.1 %all-gather.12.cloned.1.call-start = ((), (), s32[]{:S(2)}) async-start(), calls=%async_computation.8 | async-start | bytes 4718592 | tf_op jit(solution)/shard_map/all_gather | solution.py:222
  37.0 65.0 %copy-start.50 = (f32[1024]{0:T(1024)}, f32[1024]{0:T(1024)S(1)}, u32[]{:S(2)}) copy-start(f32[1024]{0:T(1024)S(1)} %iota_convert_fusion) | copy-start | bytes 12292
  37.0 65.0 %copy-start.52 = (f32[32]{0:T(128)}, f32[32]{0:T(128)S(1)}, u32[]{:S(2)}) copy-start(f32[32]{0:T(128)S(1)} %multiply_exponential_fusion) | copy-start | bytes 388
  50.7 54.0 %copy-start.22 = (f32[1024,32]{0,1:T(8,128)}, f32[1024,32]{0,1:T(8,128)S(1)}, u32[]{:S(2)}) copy-start(f32[1024,32]{0,1:T(8,128)S(1)} %get-tuple-element.288) | copy-start | bytes 393220
  61.5 3.4 copy-start.8
  70.2 33.4 %copy-start.25 = (bf16[1024,48]{0,1:T(8,128)(2,1)}, bf16[1024,48]{0,1:T(8,128)(2,1)S(1)}, u32[]{:S(2)}) copy-start(bf16[1024,48]{0,1:T(8,128)(2,1)S(1)} %convolution_convert_fusion) | copy-start | bytes 294916
  123.1 4.7 copy-start.11
  123.1 4.7 copy-start.44
  124.5 216.1 %all-gather.14.cloned.1.call-start = ((), (), s32[]{:S(2)}) async-start(), calls=%async_computation.9 | async-start | bytes 8650752 | tf_op jit(solution)/shard_map/all_gather | solution.py:191
  125.1 303.6 %all-gather.16.cloned.1.call-start = ((), (), s32[]{:S(2)}) async-start(), calls=%async_computation.10 | async-start | bytes 10485760 | tf_op jit(solution)/shard_map/all_gather | solution.py:168
  189.2 320.1 %reduce-scatter.6.cloned.1.call-start = ((), (), s32[]{:S(2)}) async-start(), calls=%async_computation.14 | async-start | bytes 4718592 | tf_op jit(solution)/shard_map/reduce_scatter | solution.py:174
  263.0 90.8 %copy-start.40 = (bf16[1024,16]{0,1:T(8,128)(2,1)}, bf16[1024,16]{0,1:T(8,128)(2,1)S(1)}, u32[]{:S(2)}) copy-start(bf16[1024,16]{0,1:T(8,128)(2,1)S(1)} %convolution_convert_fusion.4) | copy-start | bytes 98308
  340.7 13.1 %copy-start.9 = (bf16[1,1024,2048]{2,1,0:T(8,128)(2,1)S(1)}, bf16[1,1024,2048]{2,1,0:T(8,128)(2,1)}, u32[]{:S(2)}) copy-start(bf16[1,1024,2048]{2,1,0:T(8,128)(2,1)} %all-gather.22.cloned.1.call-done) | copy-start | bytes 12582916
  353.8 3.3 copy-start.46
  357.1 3.3 copy-start.7
  357.1 5.2 copy-start.43
  446.3 13.4 %copy-start.14 = (bf16[1024,1024]{1,0:T(8,128)(2,1)}, bf16[1024,1024]{1,0:T(8,128)(2,1)S(1)}, u32[]{:S(2)}) copy-start(bf16[1024,1024]{1,0:T(8,128)(2,1)S(1)} %get-tuple-element.270) | copy-start | bytes 6291460
  446.3 13.4 %copy-start.15 = (bf16[1024,1024]{1,0:T(8,128)(2,1)}, bf16[1024,1024]{1,0:T(8,128)(2,1)S(1)}, u32[]{:S(2)}) copy-start(bf16[1024,1024]{1,0:T(8,128)(2,1)S(1)} %get-tuple-element.268) | copy-start | bytes 6291460
  446.4 17.4 %copy-start.13 = (bf16[1024,1024]{1,0:T(8,128)(2,1)}, bf16[1024,1024]{1,0:T(8,128)(2,1)S(1)}, u32[]{:S(2)}) copy-start(bf16[1024,1024]{1,0:T(8,128)(2,1)S(1)} %get-tuple-element.269) | copy-start | bytes 6291460
  447.7 12.1 %copy-start.27 = (bf16[1024,16]{0,1:T(8,128)(2,1)}, bf16[1024,16]{0,1:T(8,128)(2,1)S(1)}, u32[]{:S(2)}) copy-start(bf16[1024,16]{0,1:T(8,128)(2,1)S(1)} %convolution_convert_fusion.6) | copy-start | bytes 98308
  463.1 96.8 %reduce-scatter.4.cloned.1.call-start = ((), (), s32[]{:S(2)}) async-start(), calls=%async_computation.12 | async-start | bytes 4718592 | tf_op jit(solution)/shard_map/reduce_scatter | solution.py:174
  463.8 6.5 copy-start.29
  487.5 72.3 %copy-start.20 = (bf16[1,128,2048]{2,1,0:T(8,128)(2,1)S(1)}, bf16[1,128,2048]{2,1,0:T(8,128)(2,1)}, u32[]{:S(2)}) copy-start(bf16[1,128,2048]{2,1,0:T(8,128)(2,1)} %param.29) | copy-start | bytes 1572868
  571.9 34.2 %all-to-all-start.2 = ((bf16[8,128,256]{2,1,0:T(8,128)(2,1)}), bf16[8,128,256]{2,1,0:T(8,128)(2,1)}, u32[]{:S(2)}, u32[]{:S(2)}) async-start(bf16[8,128,256]{2,1,0:T(8,128)(2,1)} %bitcast.285), calls=%async_computation.4 | async-start | bytes 1048576 | tf_op jit(solution)/shard_map/all_to_all | solution.py:258
  580.4 189.2 %all-reduce.4.cloned.1.call-start = ((), (), s32[]{:S(2)}) async-start(), calls=%async_computation.17 | async-start | bytes 5636096
  599.9 8.7 %copy-start.12 = (bf16[1024,4,64]{0,2,1:T(8,128)(2,1)S(1)}, bf16[1024,4,64]{0,2,1:T(8,128)(2,1)}, u32[]{:S(2)}) copy-start(bf16[1024,4,64]{0,2,1:T(8,128)(2,1)} %copy-done.11) | copy-start | bytes 1572868
  599.9 8.7 %copy-start.45 = (f32[2,4,512]{2,1,0:T(4,128)S(1)}, f32[2,4,512]{2,1,0:T(4,128)}, u32[]{:S(2)}) copy-start(f32[2,4,512]{2,1,0:T(4,128)} %copy-done.44) | copy-start | bytes 49156
  608.6 60.3 %copy-start.26 = (bf16[1024,48]{0,1:T(8,128)(2,1)S(1)}, bf16[1024,48]{0,1:T(8,128)(2,1)}, u32[]{:S(2)}) copy-start(bf16[1024,48]{0,1:T(8,128)(2,1)} %copy-done.25) | copy-start | bytes 294916
  608.6 62.0 %copy-start.51 = (f32[1024]{0:T(1024)S(1)}, f32[1024]{0:T(1024)}, u32[]{:S(2)}) copy-start(f32[1024]{0:T(1024)} %copy-done.50) | copy-start | bytes 12292
  608.6 62.0 %copy-start.53 = (f32[32]{0:T(128)S(1)}, f32[32]{0:T(128)}, u32[]{:S(2)}) copy-start(f32[32]{0:T(128)} %copy-done.52) | copy-start | bytes 388
  617.4 5.4 slice-start
  617.4 5.9 slice-start.1
  646.9 5.4 slice-start
  646.9 5.9 slice-start.1
  667.9 6.8 copy-start.23
  673.3 4.7 copy-start.6
  673.3 3.7 copy-start.35
  673.3 3.7 copy-start.38
  675.8 6.2 copy-start.4
  675.8 6.2 copy-start.28
  678.0 4.8 copy-start.41
  679.6 3.2 copy-start.10
  679.6 3.2 copy-start.30
  684.8 11.0 %copy-start.16 = (f32[4,8,8192]{2,1,0:T(8,128)S(1)}, f32[4,8,8192]{2,1,0:T(8,128)}, u32[]{:S(2)}) copy-start(f32[4,8,8192]{2,1,0:T(8,128)} %reshape.488) | copy-start | bytes 3145732
  687.3 9.5 %copy-start.18 = (f32[4,8,4096]{2,1,0:T(8,128)S(1)}, f32[4,8,4096]{2,1,0:T(8,128)}, u32[]{:S(2)}) copy-start(f32[4,8,4096]{2,1,0:T(8,128)} %reshape.489) | copy-start | bytes 1572868
  690.8 7.0 copy-start.56
  690.8 7.6 copy-start.32
  691.7 6.7 copy-start.36
  691.7 6.7 copy-start.33
  694.3 4.1 copy-start.39
  694.3 4.1 copy-start.42
  697.7 120.2 %reduce-scatter.8.cloned.1.call-start = ((), (), s32[]{:S(2)}) async-start(), calls=%async_computation.15 | async-start | bytes 4718592 | tf_op jit(solution)/shard_map/reduce_scatter | solution.py:174
  705.2 71.6 %copy-start.55 = (u32[32]{0:T(128)S(1)}, u32[32]{0:T(128)}, u32[]{:S(2)}) copy-start(u32[32]{0:T(128)} %constant.173) | copy-start | bytes 388
  773.0 44.9 %copy-start.48 = (f32[2048]{0:T(1024)S(1)}, f32[2048]{0:T(1024)}, u32[]{:S(2)}) copy-start(f32[2048]{0:T(1024)} %param.30) | copy-start | bytes 24580
  773.0 13.0 %all-to-all-start.3 = ((f32[4,1,22016]{2,1,0:T(1,128)}), f32[4,1,22016]{2,1,0:T(1,128)S(1)}, u32[]{:S(2)}, u32[]{:S(2)}) async-start(f32[4,1,22016]{2,1,0:T(1,128)} %bitcast.47), calls=%async_computation.6 | async-start | bytes 704512 | tf_op jit(solution)/shard_map/all_to_all | solution.py:318
  789.3 32.6 %copy-start.1 = (bf16[4,16,16384]{2,1,0:T(8,128)(2,1)S(1)}, bf16[4,16,16384]{2,1,0:T(8,128)(2,1)}, u32[]{:S(2)}) copy-start(bf16[4,16,16384]{2,1,0:T(8,128)(2,1)} %param.45) | copy-start | bytes 6291460
  (11 other events, 21.5 us)
Sparse Core Ops, SparseCore 0:
  9.7 51.7 all-gather.21
  63.3 33.1 all-gather.9
  98.6 51.0 all-gather.19
  151.4 60.9 all-gather.17
  214.5 45.5 all-gather.11
  262.9 77.6 all-gather.13
  342.5 86.1 all-gather.15
  463.2 46.1 reduce-scatter.5
  511.7 48.1 reduce-scatter.3
  697.8 71.7 all-reduce.3
  771.9 45.9 reduce-scatter.7

commit v2 on v1

--- a/solution.py
+++ b/solution.py
@@ -1,8 +1,11 @@
+import functools
 import math
 
 import jax
 import jax.numpy as jnp
 from jax import lax
+from jax.experimental import pallas as pl
+from jax.experimental.pallas import tpu as pltpu
 from jax.sharding import PartitionSpec as P
 
 NH = 32
@@ -121,10 +124,500 @@
     return (grad_query.reshape(length, heads, head_size), grad_keys * SCORE_SCALE, grad_values)
 
 
+MESH = pl.DeviceIdType.MESH
+
+
+def remote(src, dst, send_sem, recv_sem, device):
+    return pltpu.make_async_remote_copy(
+        src_ref=src,
+        dst_ref=dst,
+        send_sem=send_sem,
+        recv_sem=recv_sem,
+        device_id=device,
+        device_id_type=MESH,
+    )
+
+
+class Place:
+    def __init__(self, seq_size):
+        self.d = lax.axis_index("dp")
+        self.s = lax.axis_index("seq")
+        self.seq_size = seq_size
+        self.chips = seq_size // 2
+        self.z = self.s // 2
+        self.c = self.s % 2
+        self.dx = self.d + 1 - 2 * (self.d % 2)
+        self.dy = lax.rem(self.d + 2, 4)
+        self.dd = lax.rem(self.dx + 2, 4)
+        self.sib = self.s + 1 - 2 * self.c
+
+    def seq(self, s):
+        return (self.d, s)
+
+    def dp(self, d):
+        return (d, self.s)
+
+    def peer(self, step):
+        return lax.rem(self.s + step, self.seq_size)
+
+    def greet(self, seq_steps, dp_peers):
+        barrier = pltpu.get_barrier_semaphore()
+        for step in seq_steps:
+            pl.semaphore_signal(
+                barrier, 1, device_id=self.seq(self.peer(step)), device_id_type=MESH
+            )
+        for d in dp_peers:
+            pl.semaphore_signal(barrier, 1, device_id=self.dp(d), device_id_type=MESH)
+        pl.semaphore_wait(barrier, len(seq_steps) + len(dp_peers))
+
+
+class Chain:
+    def __init__(self, place, own, slot, sems):
+        self.p, self.own, self.slot = place, own, slot
+        self.up, self.down, self.side, self.got = (sems.at[i] for i in range(4))
+
+    def _up(self, src, i):
+        return remote(src, self.slot(i), self.up.at[i], self.got.at[i], self.p.seq(self.p.s + 2))
+
+    def _down(self, src, i):
+        return remote(src, self.slot(i), self.down.at[i], self.got.at[i], self.p.seq(self.p.s - 2))
+
+    def _side(self, src, i):
+        return remote(src, self.slot(i), self.side.at[i], self.got.at[i], self.p.seq(self.p.sib))
+
+    def start(self):
+        p = self.p
+
+        @pl.when(p.z < p.chips - 1)
+        def _():
+            self._up(self.own, p.s).start()
+
+        @pl.when(p.z > 0)
+        def _():
+            self._down(self.own, p.s).start()
+
+        self._side(self.own, p.s).start()
+
+    def step(self, k):
+        p = self.p
+        low, high = p.s - 2 * k, p.s + 2 * k
+
+        @pl.when(p.z >= k)
+        def _():
+            self._side(self.slot(low), low).wait_recv()
+
+            @pl.when(p.z < p.chips - 1)
+            def _():
+                self._up(self.slot(low), low).start()
+
+            self._side(self.slot(low), low).start()
+
+        @pl.when(p.z + k < p.chips)
+        def _():
+            self._side(self.slot(high), high).wait_recv()
+
+            @pl.when(p.z > 0)
+            def _():
+                self._down(self.slot(high), high).start()
+
+            self._side(self.slot(high), high).start()
+
+    def side_recv(self, z):
+        other = 2 * z + 1 - self.p.c
+        self._side(self.slot(other), other).wait_recv()
+
+    def finish(self):
+        p = self.p
+
+        @pl.when(p.z < p.chips - 1)
+        def _():
+            self._up(self.own, p.s).wait_send()
+
+        @pl.when(p.z > 0)
+        def _():
+            self._down(self.own, p.s).wait_send()
+
+        self._side(self.own, p.s).wait_send()
+        for k in range(1, p.chips):
+            low, high = p.s - 2 * k, p.s + 2 * k
+
+            @pl.when(p.z >= k)
+            def _():
+                @pl.when(p.z < p.chips - 1)
+                def _():
+                    self._up(self.slot(low), low).wait_send()
+
+                self._side(self.slot(low), low).wait_send()
+
+            @pl.when(p.z + k < p.chips)
+            def _():
+                @pl.when(p.z > 0)
+                def _():
+                    self._down(self.slot(high), high).wait_send()
+
+                self._side(self.slot(high), high).wait_send()
+
+
+class Plane:
+    def __init__(self, place, block, half, sems):
+        self.p, self.block, self.half, self.sems = place, block, half, sems
+
+    def _copy(self, ref, i, d):
+        return remote(ref, ref, self.sems.at[0, i], self.sems.at[1, i], self.p.dp(d))
+
+    def _all(self):
+        p = self.p
+        return (
+            (self.block(p.d), p.dx),
+            (self.block(p.d), p.dy),
+            (self.half(p.dx, 0), p.dy),
+            (self.half(p.dy, 1), p.dx),
+        )
+
+    def start(self):
+        for i, (ref, d) in enumerate(self._all()[:2]):
+            self._copy(ref, i, d).start()
+
+    def forward(self):
+        p = self.p
+        everything = self._all()
+        for i, came in ((0, p.dx), (1, p.dy)):
+            self._copy(self.block(came), i, came).wait_recv()
+            ref, d = everything[2 + i]
+            self._copy(ref, 2 + i, d).start()
+
+    def recv(self):
+        p = self.p
+        self._copy(self.half(p.dd, 0), 2, p.dy).wait_recv()
+        self._copy(self.half(p.dd, 1), 3, p.dx).wait_recv()
+
+    def finish(self):
+        for i, (ref, d) in enumerate(self._all()):
+            self._copy(ref, i, d).wait_send()
+
+
+class Spread:
+    def __init__(self, place, pairs, whole, send_sem, recv_sem):
+        self.p, self.pairs, self.whole = place, pairs, whole
+        self.send_sem, self.recv_sem = send_sem, recv_sem
+
+    def start(self):
+        p = self.p
+        for step in (1, 2, 3, 4, 5, 6, 7):
+            j = p.peer(step)
+            for src, dst in self.pairs(j):
+                remote(src, dst, self.send_sem, self.recv_sem, p.seq(j)).start()
+
+    def recv(self):
+        p = self.p
+        for whole in self.whole:
+            remote(whole, whole, self.send_sem, self.recv_sem, p.seq(p.sib)).wait_recv()
+
+    def finish(self):
+        p = self.p
+        for whole in self.whole:
+            remote(whole, whole, self.send_sem, self.recv_sem, p.seq(p.sib)).wait_send()
+
+
+PIECES = 4
+
+
+def gather_kernel(
+    seq_size,
+    hidden,
+    cotangent,
+    documents,
+    adapter_row,
+    query_w,
+    kv_w,
+    out_w,
+    gate_w,
+    up_w,
+    down_w,
+    hidden_all,
+    cotangent_all,
+    documents_all,
+    adapters_all,
+    qkv_all,
+    out_all,
+    gu_all,
+    down_all,
+    chain_sems,
+    plane_sems,
+    local_sems,
+    spread_sems,
+    small_sems,
+    side_sems,
+    hidden_v,
+    cotangent_v,
+    out_v,
+    down_v,
+    qkv_v,
+    gu_v,
+):
+    p = Place(seq_size)
+    d, s, z, c = p.d, p.s, p.z, p.c
+    rows = query_w.shape[0]
+    part = down_w.shape[0]
+    half_rows = seq_size * rows // 2
+
+    landing = pl.ds(pl.multiple_of(rows * s, rows), rows)
+    q_width = query_w.shape[1] // seq_size
+
+    def column_block(number, size):
+        return pl.ds(pl.multiple_of(number * size, size), size)
+
+    stage = [
+        (hidden, hidden_v),
+        (cotangent, cotangent_v),
+        (out_w, out_v),
+        (down_w, down_v),
+        (query_w.at[:, column_block(s, q_width)], qkv_v.at[:, pl.ds(0, q_width)]),
+        (kv_w.at[s], qkv_v.at[:, pl.ds(q_width, kv_w.shape[2])]),
+    ]
+    for i in range(8):
+        matrix = (gate_w, up_w)[i // 4]
+        block = matrix.at[:, column_block(seq_size * (i % 4) + s, part)]
+        stage.append((block, gu_v.at[:, pl.ds(part * i, part)]))
+    stage = [
+        pltpu.make_async_copy(src, dst, local_sems.at[0, i]) for i, (src, dst) in enumerate(stage)
+    ]
+    keep = [
+        pltpu.make_async_copy(src, dst, local_sems.at[1, i])
+        for i, (src, dst) in enumerate(
+            (
+                (hidden_v, hidden_all.at[s]),
+                (cotangent_v, cotangent_all.at[s]),
+                (out_v, out_all.at[d, z, c]),
+                (down_v, down_all.at[d]),
+                (qkv_v, qkv_all.at[d, landing]),
+                (gu_v, gu_all.at[d, landing]),
+                (documents, documents_all.at[s]),
+                (adapter_row, adapters_all.at[d]),
+            )
+        )
+    ]
+    for copy in stage:
+        copy.start()
+    p.greet(range(1, seq_size), (p.dx, p.dy, p.dd))
+
+    hid = Chain(p, hidden, lambda i: hidden_all.at[i], chain_sems.at[0])
+    cot = Chain(p, cotangent, lambda i: cotangent_all.at[i], chain_sems.at[1])
+    out = Chain(p, out_w, lambda i: out_all.at[d, i // 2, i % 2], chain_sems.at[2])
+
+    def qkv_pairs(j):
+        width = query_w.shape[1] // seq_size
+        columns = pl.ds(pl.multiple_of(width * j, width), width)
+        return (
+            (query_w.at[:, columns], qkv_all.at[d, landing, pl.ds(0, width)]),
+            (kv_w.at[j], qkv_all.at[d, landing, pl.ds(width, kv_w.shape[2])]),
+        )
+
+    def gu_pairs(piece):
+        matrix = (gate_w, up_w)[piece // 2]
+
+        def pairs(j):
+            found = []
+            for block in (2 * (piece % 2), 2 * (piece % 2) + 1):
+                columns = pl.ds(pl.multiple_of(part * (seq_size * block + j), part), part)
+                at = part * (4 * (piece // 2) + block)
+                found.append((matrix.at[:, columns], gu_all.at[d, landing, pl.ds(at, part)]))
+            return found
+
+        return pairs
+
+    others = pl.ds(0, rows * (seq_size - 1))
+    qkv = Spread(
+        p, qkv_pairs, [qkv_all.at[d, others]], spread_sems.at[0, 0], spread_sems.at[0, 1]
+    )
+    gu = []
+    gu_planes = []
+    for i in range(PIECES):
+        cut = pl.ds(2 * part * i, 2 * part)
+        gu.append(
+            Spread(
+                p, gu_pairs(i), [gu_all.at[d, others, cut]], spread_sems.at[1 + i, 0], spread_sems.at[1 + i, 1],
+            )
+        )
+        gu_planes.append(
+            Plane(
+                p,
+                lambda e, cut=cut: gu_all.at[e, :, cut],
+                lambda e, h, cut=cut: gu_all.at[e, pl.ds(half_rows * h, half_rows), cut],
+                plane_sems.at[3 + i],
+            )
+        )
+    qkv_plane = Plane(
+        p,
+        lambda e: qkv_all.at[e],
+        lambda e, h: qkv_all.at[e, pl.ds(half_rows * h, half_rows)],
+        plane_sems.at[0],
+    )
+    down = Plane(
+        p,
+        lambda e: down_w if e is d else down_all.at[e],
+        lambda e, h: down_all.at[e, pl.ds(part // 2 * h, part // 2)],
+        plane_sems.at[1],
+    )
+    half_chips = p.chips // 2
+    out_plane = Plane(
+        p,
+        lambda e: out_all.at[e, :, c],
+        lambda e, h: out_all.at[e, pl.ds(half_chips * h, half_chips), c],
+        plane_sems.at[2],
+    )
+
+    def documents_copy(step):
+        return remote(
+            documents, documents_all.at[s], small_sems.at[0, step], small_sems.at[1, 0], p.seq(p.peer(step))
+        )
+
+    def adapters_copy(i, e):
+        return remote(
+            adapter_row, adapters_all.at[d], small_sems.at[2, i], small_sems.at[3, 0], p.dp(e)
+        )
+
+    def side_copy(i, e):
+        ref = out_all.at[e, :, c]
+        return remote(ref, ref, side_sems.at[0, i], side_sems.at[1, i], p.seq(p.sib))
+
+    def side_wait(i, e):
+        ref = out_all.at[e, :, 1 - c]
+        remote(ref, ref, side_sems.at[0, i], side_sems.at[1, i], p.seq(p.sib)).wait_recv()
+
+    for step in range(1, seq_size):
+        documents_copy(step).start()
+    for i, e in enumerate((p.dx, p.dy, p.dd)):
+        adapters_copy(i, e).start()
+    qkv.start()
+    hid.start()
+    for i, e in enumerate((p.dx, p.dy)):
+        remote(
+            down_w, down_all.at[d], down.sems.at[0, i], down.sems.at[1, i], p.dp(e)
+        ).start()
+    for copy in stage:
+        copy.wait()
+    for copy in keep:
+        copy.start()
+    for copy in keep:
+        copy.wait()
+    qkv.recv()
+    qkv_plane.start()
+    hid.step(1)
+    gu[0].start()
+    down.forward()
+    qkv_plane.forward()
+    hid.step(2)
+    gu[1].start()
+    gu[0].recv()
+    gu_planes[0].start()
+    hid.step(3)
+    gu[2].start()
+    qkv_plane.recv()
+    out.start()
+    gu[1].recv()
+    gu_planes[1].start()
+    gu_planes[0].forward()
+    gu[3].start()
+    out.step(1)
+    gu[2].recv()
+    gu_planes[2].start()
+    gu_planes[1].forward()
+    out.step(2)
+    cot.start()
+    gu[3].recv()
+    gu_planes[3].start()
+    gu_planes[2].forward()
+    out.step(3)
+    out_plane.start()
+    cot.step(1)
+    gu_planes[3].forward()
+    cot.step(2)
+    out_plane.forward()
+    side_copy(0, p.dx).start()
+    side_copy(1, p.dy).start()
+    cot.step(3)
+    out_plane.recv()
+    side_copy(2, p.dd).start()
+    for i in range(4):
+        gu_planes[i].recv()
+    down.recv()
+    for chain in (hid, out, cot):
+        for other in range(p.chips):
+            chain.side_recv(other)
+        chain.finish()
+    side_wait(0, p.dx)
+    side_wait(1, p.dy)
+    side_wait(2, p.dd)
+    remote(
+        documents_all.at[pl.ds(0, seq_size - 1)], documents_all.at[pl.ds(0, seq_size - 1)],
+        small_sems.at[0, 0], small_sems.at[1, 0], p.seq(p.sib),
+    ).wait_recv()
+    remote(
+        adapters_all.at[pl.ds(0, 3)], adapters_all.at[pl.ds(0, 3)],
+        small_sems.at[2, 3], small_sems.at[3, 0], p.dp(p.dx),
+    ).wait_recv()
+    for step in range(1, seq_size):
+        documents_copy(step).wait_send()
+    for i, e in enumerate((p.dx, p.dy, p.dd)):
+        adapters_copy(i, e).wait_send()
+        side_copy(i, e).wait_send()
+    for group in [qkv, *gu, qkv_plane, down, out_plane, *gu_planes]:
+        group.finish()
+
+
+def gather_all(
+    seq_size, hidden, cotangent, documents, adapter_row, query_w, kv_w, out_w, gate_w, up_w, down_w
+):
+    tokens, width = hidden.shape
+    rows = query_w.shape[0]
+    part = down_w.shape[0]
+    chips = seq_size // 2
+    qkv_width = query_w.shape[1] // seq_size + kv_w.shape[2]
+
+    def shape(*dims, dtype=BF16):
+        return jax.ShapeDtypeStruct(dims, dtype)
+
+    anywhere = pl.BlockSpec(memory_space=pl.ANY)
+    return pl.pallas_call(
+        functools.partial(gather_kernel, seq_size),
+        out_shape=(
+            shape(seq_size, tokens, width),
+            shape(seq_size, tokens, width),
+            shape(seq_size, 8, tokens, dtype=jnp.int32),
+            shape(4, 8, 128, dtype=jnp.int32),
+            shape(4, seq_size * rows, qkv_width),
+            shape(4, chips, 2, rows, width),
+            shape(4, seq_size * rows, 8 * part),
+            shape(4, part, width),
+        ),
+        in_specs=[anywhere] * 10,
+        out_specs=(anywhere,) * 8,
+        scratch_shapes=[
+            pltpu.SemaphoreType.DMA((3, 4, seq_size)),
+            pltpu.SemaphoreType.DMA((3 + PIECES, 2, 4)),
+            pltpu.SemaphoreType.DMA((2, 14)),
+            pltpu.SemaphoreType.DMA((1 + PIECES, 2)),
+            pltpu.SemaphoreType.DMA((4, seq_size)),
+            pltpu.SemaphoreType.DMA((2, 3)),
+            pltpu.VMEM((tokens, width), BF16),
+            pltpu.VMEM((tokens, width), BF16),
+            pltpu.VMEM((rows, width), BF16),
+            pltpu.VMEM((part, width), BF16),
+            pltpu.VMEM((rows, qkv_width), BF16),
+            pltpu.VMEM((rows, 8 * part), BF16),
+        ],
+        compiler_params=pltpu.CompilerParams(collective_id=0, has_side_effects=True),
+        cost_estimate=pl.CostEstimate(flops=0, bytes_accessed=2 * 30 * 2**20, transcendentals=0),
+        name="gather_all",
+    )(hidden, cotangent, documents, adapter_row, query_w, kv_w, out_w, gate_w, up_w, down_w)
+
+
 def make_local(dp_size, seq_size):
     devices = dp_size * seq_size
     heads = NH // seq_size
     kv_repeat = max(1, seq_size // KVH)
+    kernels = dp_size == 4 and seq_size == 8
 
     def local(
         hidden,
@@ -177,18 +670,46 @@
             return columns.reshape(columns.shape[0], dp_size, seq_size, ff_block)
 
         hidden_own = hidden[0].astype(F32)
-        hidden_all = gather_seq(hidden[0])
-        segments = gather_seq(token_document_numbers[0])
-        kv = jnp.stack([key_weight.reshape(rows, KVH, HD), value_weight.reshape(rows, KVH, HD)], 2)
-        kv = jnp.repeat(kv.reshape(rows, KVH, 2 * HD), kv_repeat, axis=1)
-        qkv = jnp.concatenate([query_weight.reshape(rows, seq_size, q_width), kv], axis=2)
-        qkv = across(jnp.swapaxes(qkv, 0, 1)).reshape(seq_size * rows, q_width + 2 * HD)
-        qkv = gather_dp(qkv)
-        gate_up = jnp.concatenate([by_owner(gate_weight), by_owner(up_weight)], axis=1)
-        gate_up = across(jnp.transpose(gate_up, (2, 0, 1, 3)))
-        gate_up = gather_dp(gate_up.reshape(seq_size * rows, 2 * dp_size * ff_block))
-        down = gather_dp(down_weight)
-        out_full = lax.all_gather(attention_output_weight, ("dp", "seq"), axis=0, tiled=True)
+        if kernels:
+            kv = jnp.concatenate(
+                [key_weight.reshape(rows, KVH, HD), value_weight.reshape(rows, KVH, HD)], axis=2
+            )
+            gathered = gather_all(
+                seq_size,
+                hidden[0],
+                cotangent[0],
+                jnp.broadcast_to(token_document_numbers, (8, tokens)),
+                jnp.broadcast_to(sequence_adapter_index[:, None], (8, 128)),
+                query_weight,
+                jnp.swapaxes(kv, 0, 1),
+                attention_output_weight,
+                gate_weight,
+                up_weight,
+                down_weight,
+            )
+            hidden_all = gathered[0].reshape(length, width)
+            cotangent_all = gathered[1].reshape(length, width)
+            segments = gathered[2][:, 0].reshape(length)
+            owners = gathered[3][:, 0, 0]
+            qkv = gathered[4].reshape(width, -1)
+            out_full = gathered[5].reshape(width, width)
+            gate_up = gathered[6].reshape(width, -1)
+            down = gathered[7].reshape(dp_size * ff_block, width)
+        else:
+            hidden_all = gather_seq(hidden[0])
+            segments = gather_seq(token_document_numbers[0])
+            kv = jnp.stack([key_weight.reshape(rows, KVH, HD), value_weight.reshape(rows, KVH, HD)], 2)
+            kv = jnp.repeat(kv.reshape(rows, KVH, 2 * HD), kv_repeat, axis=1)
+            qkv = jnp.concatenate([query_weight.reshape(rows, seq_size, q_width), kv], axis=2)
+            qkv = across(jnp.swapaxes(qkv, 0, 1)).reshape(seq_size * rows, q_width + 2 * HD)
+            qkv = gather_dp(qkv)
+            gate_up = jnp.concatenate([by_owner(gate_weight), by_owner(up_weight)], axis=1)
+            gate_up = across(jnp.transpose(gate_up, (2, 0, 1, 3)))
+            gate_up = gather_dp(gate_up.reshape(seq_size * rows, 2 * dp_size * ff_block))
+            down = gather_dp(down_weight)
+            out_full = lax.all_gather(attention_output_weight, ("dp", "seq"), axis=0, tiled=True)
+            cotangent_all = gather_seq(cotangent[0])
+            owners = lax.all_gather(sequence_adapter_index, "dp", axis=0, tiled=True)
         ff_own = dp_size * ff_block
 
         adapter = sequence_adapter_index[0]
@@ -236,7 +757,7 @@
         ffn = scatter_seq((mm(activation, down) + mm(low_down, down_out)).astype(BF16))
         mixed = (middle_own + RESIDUAL_SCALE * ffn.astype(F32)).astype(BF16)
 
-        grad_ffn = gather_seq((RESIDUAL_SCALE * cotangent[0].astype(F32)).astype(BF16))
+        grad_ffn = (RESIDUAL_SCALE * cotangent_all.astype(F32)).astype(BF16)
         grad_low_down = mm_t(grad_ffn, down_out).astype(BF16)
         grad_act = mm_t(grad_ffn, down) + mm_t(grad_low_down, down_in)
         grad_gate = (grad_act * up_proj * sigma * (1.0 + gate * (1.0 - sigma))).astype(BF16)
@@ -318,7 +839,6 @@
         mine = lax.all_to_all(
             mine.reshape(dp_size, -1), "dp", split_axis=0, concat_axis=0, tiled=True
         )
-        owners = lax.all_gather(sequence_adapter_index, "dp", axis=0, tiled=True)
         numbers = jnp.arange(adapters, dtype=jnp.int32)
         chooser = (owners[:, None] == numbers[None, :]).astype(F32)
         mine = jnp.einsum("sa,si->ai", chooser, mine, precision=lax.Precision.HIGHEST)

time: 839 us -> 719 us (0.86)
  waiting for transfers between devices: 382 us -> 186 us
  Pallas kernels: 0 us -> 161 us
  blocking collectives: 101 us -> 0 us
  other arithmetic: 34.9 us -> 47.2 us
    all_gather x6 -> x0, waiting for transfers between devices: 198 us -> none  [the longest x3 109 us: gather_dp(): return lax.all_gather(block, 'dp', axis=0, tiled=True)]
    pallas_call x0 -> x1, Pallas kernels: none -> 161 us  [gather_all(): pl.pallas_call(functools.partial(gather_kernel, seq_size), out_shape=(sha...]
    all_to_all x2 -> x0, blocking collectives: 81.3 us -> none  [across(): return lax.all_to_all(piece, 'seq', split_axis=0, concat_axis=0, tiled=True)]
    all_gather x1 -> x0, blocking collectives: 11.8 us -> none  [gather_seq(): return lax.all_gather(block, 'seq', axis=0, tiled=True)]
    convert_element_type x1 -> x2, other arithmetic: 1.02 us -> 10.7 us  [local(): rms_scale(hidden_all.astype(F32), attention_norm_gain).astype(BF16)]
    unnamed x141 -> x132, local copies, waits for them, and re-layouts: 36 us -> 30.7 us
    unnamed x12 -> x6, waiting for transfers between devices: 66.2 us -> 63.7 us
  transfers between devices with their start and end apart: 13 -> 7, of which waited for: 10 -> 6; matrix products, arithmetic and copies ran while one was open for 20% -> 15% of each run, Pallas kernels for 0% -> 0%
where the time goes in v2:
time: 719 us; the launch traced here: 705 us
  waiting for transfers between devices  186 us (26%)
  matrix products  176 us (24%)
  Pallas kernels  161 us (22%)
  local copies, waits for them, and re-layouts  99.4 us (14%)
  other arithmetic  47.2 us (7%)
  between operations  16.1 us (2%)
  starting transfers between devices  12.3 us (2%)
    pallas_call x1, Pallas kernels, gather_all(): pl.pallas_call(functools.partial(gather_kernel, seq_size), out_shape=(sha...  161 us
    reduce_scatter x3, waiting for transfers between devices, scatter_seq(): return lax.psum_scatter(total, 'seq', scatter_dimension=0, tiled=True)  79.5 us
    unnamed x6, waiting for transfers between devices  63.7 us
    dot_general x15, matrix products, mm(): return jnp.dot(a, b, preferred_element_type=F32)  62.7 us
    dot_general x15, matrix products, mm_t(): lax.dot_general(a, b, (((1,), (1,)), ((), ())), preferred_element_type=F32)  44.6 us
    all_gather x1, waiting for transfers between devices, local(): attn = lax.all_gather(attn_heads, 'seq', axis=1, tiled=True)  38.2 us
    unnamed x132, local copies, waits for them, and re-layouts  30.7 us
    reshape x4, local copies, waits for them, and re-layouts, by_target(): return whole.reshape(dp_size, seq_size, -1)  15.6 us
  transfers between devices with their start and end apart: 7, of which 6 were waited for; matrix products, arithmetic and copies ran while one was open for 15% of the time, Pallas kernels for 0%

profile of v2, /device:TPU:8, one launch (start us, length us, event | category | flops | bytes accessed | tf_op | source)
XLA Modules:
  0.0 704.6 jit_solution(110968320117265410)
XLA Ops:
  12.7 161.0 %gather_all.1 = (bf16[8,128,2048]{2,1,0:T(8,128)(2,1)}, bf16[8,128,2048]{2,1,0:T(8,128)(2,1)}, s32[8,8,128]{2,1,0:T(8,128)}, s32[4,8,128]{2,1,0:T(8,128)}, bf16[...) custom-call(bf16[128,2048]{1,0:T(8,128)(2,1)} %bitcast.350, ...), custom_call_target="tpu_custom_call" | custom-call | bytes 62914560 | tf_op jit(solution)/shard_map/gather_all/pallas_call | solution.py:582
  173.7 3.1 fusion.48
  177.4 5.3 fusion.50
  182.7 5.7 fusion.171
  188.4 3.6 convolution_convert_fusion
  199.1 18.2 %while.27 = (s32[]{:T(128)}, bf16[2,512,4,64]{1,3,2,0:T(8,128)(2,1)S(1)}, f32[2,4,512]{2,1,0:T(4,128)S(1)}, s32[2]{0:T(128)S(1)}, s32[1024]{0:T(1024)S(1)}, /*in...) while((s32[]{:T(128)}, ...), condition=%wide.region_4.5_spmd, body=%wide.region_1.4_spmd.sunk | while | flops 563739136 | bytes 28129484 | solution.py:92
  202.7 2.4 fusion.243
  205.2 3.1 fusion.244
  211.7 2.4 fusion.243
  214.2 3.1 fusion.244
  220.6 3.4 multiply_convert_fusion
  225.2 2.5 copy-done.54
  227.7 4.5 fusion.175
  232.2 2.7 convolution_add_fusion.1
  234.9 38.2 %all-gather.2.cloned.1.call-done = bf16[1024,2048]{0,1:T(8,128)(2,1)} async-done(((bf16[1024,256]{0,1:T(8,128)(2,1)}), bf16[1024,2048]{0,1:T(8,128)(2,1)}) %all-gather.2.cloned.1.call-update) | async-done | bytes 4194320 | tf_op jit(solution)/shard_map/all_gather | solution.py:743
  273.1 14.3 %fusion.172 = f32[1024,2048]{1,0:T(8,128)S(1)} fusion(bf16[1024,2048]{0,1:T(8,128)(2,1)} %all-gather.2.cloned.1.call-done, bf16[2048,2048]{1,0:T(8,128)(2,1)} %bitcast.345), kind=kOutput, calls=%fused_computation.277 | convolution fusion | flops 8589934592 | bytes 20971520 | tf_op jit(solution)/shard_map/dot_general | solution.py:24
  289.6 3.2 multiply_reduce_fusion
  293.7 2.4 copy-done.8
  296.1 12.8 %fusion.173 = f32[1024,2048]{1,0:T(8,128)S(1)} fusion(bf16[1024,2048]{1,0:T(8,128)(2,1)S(1)} %multiply_convert_fusion.1, bf16[2048,2048]{1,0:T(8,128)(2,1)} %bitcast.395), kind=kOutput, calls=%fused_computation.278 | convolution fusion | flops 8589934592 | bytes 20971520 | tf_op jit(solution)/shard_map/dot_general | solution.py:24
  314.1 4.8 multiply_convert_fusion.3
  319.6 12.8 %fusion.53 = f32[1024,2048]{1,0:T(8,128)S(1)} fusion(bf16[2048,2048]{1,0:T(8,128)(2,1)} %bitcast.396, bf16[1024,1024]{1,0:T(8,128)(2,1)S(1)} %get-tuple-element.304, bf16[1024,1024]{1,0:T(8,128)(2,1)S(1)} %get-tuple-element.302), kind=kOutput, calls=%fused_computation.75 | convolution fusion | flops 8598323200 | bytes 20971520 | tf_op jit(solution)/shard_map/dot_general | solution.py:28
  333.0 3.3 add_convert_fusion.1
  337.0 6.5 fusion.174
  343.5 3.4 add_convert_fusion.2
  347.6 5.4 fusion.52
  353.9 2.4 broadcast.330.clone.1
  357.2 2.8 copy.176
  360.1 2.6 fusion.121
  362.6 2.4 broadcast.330.clone
  365.9 3.6 copy.178
  369.4 13.4 %reduce-scatter.6.cloned.1.call-done = bf16[128,2048]{1,0:T(8,128)(2,1)} async-done(((bf16[1024,2048]{1,0:T(8,128)(2,1)}), bf16[128,2048]{1,0:T(8,128)(2,1)}) %reduce-scatter.6.cloned.1.call-update) | async-done | bytes 524304 | tf_op jit(solution)/shard_map/reduce_scatter | solution.py:667
  384.5 48.9 %reduce-scatter.4.cloned.1.call-done = bf16[128,2048]{1,0:T(8,128)(2,1)} async-done(((bf16[1024,2048]{1,0:T(8,128)(2,1)}), bf16[128,2048]{1,0:T(8,128)(2,1)}) %reduce-scatter.4.cloned.1.call-update) | async-done | bytes 524304 | tf_op jit(solution)/shard_map/reduce_scatter | solution.py:667
  433.5 2.7 subtract_add_fusion
  436.2 6.3 fusion.167
  445.5 8.4 %all-to-all-start = ((bf16[8,128,256]{2,1,0:T(8,128)(2,1)}), bf16[8,128,256]{2,1,0:T(8,128)(2,1)}, u32[]{:S(2)}, u32[]{:S(2)}) async-start(bf16[8,128,256]{2,1,0:T(8,128)(2,1)} %bitcast.280), calls=%async_computation.2 | async-start | bytes 1048576 | tf_op jit(solution)/shard_map/all_to_all | solution.py:779
  455.0 4.9 copy.158
  459.8 8.7 %reshape.537 = f32[4,8,8192]{2,1,0:T(8,128)} reshape(f32[16384,16]{1,0:T(8,128)} %copy.158) | data formatting | bytes 2097152 | tf_op jit(solution)/shard_map/reshape | solution.py:827
  468.5 2.5 fusion.176
  471.0 2.5 broadcast.330.clone.2
  474.4 5.4 reshape.538
  482.2 58.9 %while.28 = (s32[]{:T(128)}, f32[1024,64]{0,1:T(8,128)S(1)}, f32[1024,64]{0,1:T(8,128)}, bf16[2,512,4,64]{1,3,2,0:T(8,128)(2,1)}, s32[2]{0:T(128)S(1)}, /*index=...) while((s32[]{:T(128)}, f32[1024,64]{0,1:T(8,128)S(1)}, ...), condition=%wide.region_13.14_spmd.clone, body=%wide.region_11.13_spmd.clone.sunk | while | flops 1375730176 | bytes 109779824 | solution.py:121
  484.1 4.6 fusion.253
  490.7 5.4 fusion.255
  496.6 2.4 fusion.256
  503.1 3.1 fusion.257
  506.2 5.4 fusion.258
  513.5 4.6 fusion.253
  520.1 5.4 fusion.255
  526.0 2.4 fusion.256
  532.5 3.1 fusion.257
  535.6 5.5 fusion.258
  552.6 3.8 convolution_dynamic-update-slice_fusion
  562.9 2.7 copy.151
  565.6 2.4 reshape_reshape.3
  568.0 2.3 constant_dynamic-update-slice_fusion.4
  575.1 2.3 fusion.77
  577.5 4.4 add_convert_fusion
  581.9 63.6 %all-reduce.3.cloned.1.call-done = f32[8,88064]{1,0:T(8,128)} async-done(((f32[8,88064]{1,0:T(8,128)}), f32[8,88064]{1,0:T(8,128)}) %all-reduce.3.cloned.1.call-update) | async-done | bytes 2818064
  645.5 3.4 constant_dynamic-slice_fusion.7
  648.9 3.8 all-to-all-start.1
  653.6 4.9 all-to-all-done.1
  661.7 2.3 copy.168
  676.4 17.2 %reduce-scatter.8.cloned.1.call-done = bf16[128,2048]{1,0:T(8,128)(2,1)} async-done(((bf16[1024,2048]{1,0:T(8,128)(2,1)}), bf16[128,2048]{1,0:T(8,128)(2,1)}) %reduce-scatter.8.cloned.1.call-update) | async-done | bytes 524304 | tf_op jit(solution)/shard_map/reduce_scatter | solution.py:667
  695.1 2.5 fusion.72
  (275 shorter events, 96.9 us)
Async XLA Ops:
  7.2 211.6 %copy-start = (bf16[4,16,16384]{2,1,0:T(8,128)(2,1)S(1)}, bf16[4,16,16384]{2,1,0:T(8,128)(2,1)}, u32[]{:S(2)}) copy-start(bf16[4,16,16384]{2,1,0:T(8,128)(2,1)} %param.45) | copy-start | bytes 6291460
  7.2 265.9 %all-gather.2.cloned.1.call-start = ((), (), s32[]{:S(2)}) async-start(), calls=%async_computation.5 | async-start | bytes 4718592 | tf_op jit(solution)/shard_map/all_gather | solution.py:743
  7.3 187.2 %copy-start.49 = (f32[1024]{0:T(1024)}, f32[1024]{0:T(1024)S(1)}, u32[]{:S(2)}) copy-start(f32[1024]{0:T(1024)S(1)} %iota_convert_fusion) | copy-start | bytes 12292
  7.3 187.2 %copy-start.52 = (f32[32]{0:T(128)}, f32[32]{0:T(128)S(1)}, u32[]{:S(2)}) copy-start(f32[32]{0:T(128)S(1)} %multiply_exponential_fusion) | copy-start | bytes 388
  12.7 164.7 %copy-start.41 = (f32[2048]{0:T(1024)S(1)}, f32[2048]{0:T(1024)}, u32[]{:S(2)}) copy-start(f32[2048]{0:T(1024)} %param.30) | copy-start | bytes 24580
  191.9 7.0 copy-start.24
  193.2 5.8 copy-start.22
  217.3 6.6 copy-start.9
  218.8 164.1 %reduce-scatter.6.cloned.1.call-start = ((), (), s32[]{:S(2)}) async-start(), calls=%async_computation.7 | async-start | bytes 4718592 | tf_op jit(solution)/shard_map/reduce_scatter | solution.py:667
  220.6 3.4 copy-start.48
  224.0 8.3 %copy-start.6 = (bf16[8,128,2048]{2,1,0:T(8,128)(2,1)}, bf16[8,128,2048]{2,1,0:T(8,128)(2,1)S(1)}, u32[]{:S(2)}) copy-start(bf16[8,128,2048]{2,1,0:T(8,128)(2,1)S(1)} %multiply_convert_fusion) | copy-start | bytes 12582916
  224.0 3.7 copy-start.54
  273.1 14.3 %copy-start.15 = (bf16[1024,2048]{0,1:T(8,128)(2,1)S(1)}, bf16[1024,2048]{0,1:T(8,128)(2,1)}, u32[]{:S(2)}) copy-start(bf16[1024,2048]{0,1:T(8,128)(2,1)} %all-gather.2.cloned.1.call-done) | copy-start | bytes 12582916
  287.4 2.2 copy-start.3
  289.6 3.2 copy-start.39
  289.6 3.3 copy-start.47
  292.8 3.3 copy-start.8
  296.1 12.8 %copy-start.4 = (bf16[1024,2048]{1,0:T(8,128)(2,1)}, bf16[1024,2048]{1,0:T(8,128)(2,1)S(1)}, u32[]{:S(2)}) copy-start(bf16[1024,2048]{1,0:T(8,128)(2,1)S(1)} %multiply_convert_fusion.1) | copy-start | bytes 12582916
  296.1 12.8 %copy-start.44 = (bf16[4,2048,32]{1,2,0:T(8,128)(2,1)S(1)}, bf16[4,2048,32]{1,2,0:T(8,128)(2,1)}, u32[]{:S(2)}) copy-start(bf16[4,2048,32]{1,2,0:T(8,128)(2,1)} %param.44) | copy-start | bytes 1572868
  309.0 3.5 copy-start.19
  310.3 3.8 copy-start.17
  318.9 13.5 %copy-start.12 = (bf16[1024,1024]{1,0:T(8,128)(2,1)}, bf16[1024,1024]{1,0:T(8,128)(2,1)S(1)}, u32[]{:S(2)}) copy-start(bf16[1024,1024]{1,0:T(8,128)(2,1)S(1)} %get-tuple-element.304) | copy-start | bytes 6291460
  318.9 13.5 %copy-start.13 = (bf16[1024,1024]{1,0:T(8,128)(2,1)}, bf16[1024,1024]{1,0:T(8,128)(2,1)S(1)}, u32[]{:S(2)}) copy-start(bf16[1024,1024]{1,0:T(8,128)(2,1)S(1)} %get-tuple-element.302) | copy-start | bytes 6291460
  318.9 18.1 %copy-start.11 = (bf16[1024,1024]{1,0:T(8,128)(2,1)}, bf16[1024,1024]{1,0:T(8,128)(2,1)S(1)}, u32[]{:S(2)}) copy-start(bf16[1024,1024]{1,0:T(8,128)(2,1)S(1)} %get-tuple-element.303) | copy-start | bytes 6291460
  333.0 3.3 copy-start.26
  336.3 97.1 %reduce-scatter.4.cloned.1.call-start = ((), (), s32[]{:S(2)}) async-start(), calls=%async_computation.6 | async-start | bytes 4718592 | tf_op jit(solution)/shard_map/reduce_scatter | solution.py:667
  337.0 6.5 copy-start.28
  347.6 5.4 copy-start.14
  365.1 68.4 %copy-start.20 = (bf16[1,128,2048]{2,1,0:T(8,128)(2,1)S(1)}, bf16[1,128,2048]{2,1,0:T(8,128)(2,1)}, u32[]{:S(2)}) copy-start(bf16[1,128,2048]{2,1,0:T(8,128)(2,1)} %param.29) | copy-start | bytes 1572868
  445.5 34.2 %all-to-all-start = ((bf16[8,128,256]{2,1,0:T(8,128)(2,1)}), bf16[8,128,256]{2,1,0:T(8,128)(2,1)}, u32[]{:S(2)}, u32[]{:S(2)}) async-start(bf16[8,128,256]{2,1,0:T(8,128)(2,1)} %bitcast.280), calls=%async_computation.2 | async-start | bytes 1048576 | tf_op jit(solution)/shard_map/all_to_all | solution.py:779
  453.9 191.6 %all-reduce.3.cloned.1.call-start = ((), (), s32[]{:S(2)}) async-start(), calls=%async_computation.9 | async-start | bytes 5636096
  473.5 8.7 %copy-start.10 = (bf16[1024,4,64]{0,2,1:T(8,128)(2,1)S(1)}, bf16[1024,4,64]{0,2,1:T(8,128)(2,1)}, u32[]{:S(2)}) copy-start(bf16[1024,4,64]{0,2,1:T(8,128)(2,1)} %copy-done.9) | copy-start | bytes 1572868
  473.5 8.7 %copy-start.46 = (f32[2,4,512]{2,1,0:T(4,128)S(1)}, f32[2,4,512]{2,1,0:T(4,128)}, u32[]{:S(2)}) copy-start(f32[2,4,512]{2,1,0:T(4,128)} %copy-done.45) | copy-start | bytes 49156
  482.2 59.9 %copy-start.25 = (bf16[1024,48]{0,1:T(8,128)(2,1)S(1)}, bf16[1024,48]{0,1:T(8,128)(2,1)}, u32[]{:S(2)}) copy-start(bf16[1024,48]{0,1:T(8,128)(2,1)} %copy-done.24) | copy-start | bytes 294916
  482.2 61.6 %copy-start.50 = (f32[1024]{0:T(1024)S(1)}, f32[1024]{0:T(1024)}, u32[]{:S(2)}) copy-start(f32[1024]{0:T(1024)} %copy-done.49) | copy-start | bytes 12292
  482.2 61.6 %copy-start.53 = (f32[32]{0:T(128)S(1)}, f32[32]{0:T(128)}, u32[]{:S(2)}) copy-start(f32[32]{0:T(128)} %copy-done.52) | copy-start | bytes 388
  490.6 5.4 slice-start
  490.7 5.9 slice-start.1
  499.0 2.1 copy-start.2
  520.0 5.4 slice-start
  520.1 5.9 slice-start.1
  528.3 2.1 copy-start.2
  541.1 6.7 copy-start.23
  544.4 2.1 copy-start.35
  544.4 2.1 copy-start.37
  547.8 3.1 copy-start.36
  547.8 3.1 copy-start.38
  547.8 4.8 copy-start.32
  549.9 8.6 %copy-start.30 = (bf16[1024,16]{0,1:T(8,128)(2,1)}, bf16[1024,16]{0,1:T(8,128)(2,1)S(1)}, u32[]{:S(2)}) copy-start(bf16[1024,16]{0,1:T(8,128)(2,1)S(1)} %convolution_convert_fusion.9) | copy-start | bytes 98308
  550.0 10.0 %copy-start.27 = (bf16[1024,16]{0,1:T(8,128)(2,1)S(1)}, bf16[1024,16]{0,1:T(8,128)(2,1)}, u32[]{:S(2)}) copy-start(bf16[1024,16]{0,1:T(8,128)(2,1)} %copy-done.26) | copy-start | bytes 98308
  550.9 9.1 %copy-start.5 = (bf16[1024,2048]{1,0:T(8,128)(2,1)S(1)}, bf16[1024,2048]{1,0:T(8,128)(2,1)}, u32[]{:S(2)}) copy-start(bf16[1024,2048]{1,0:T(8,128)(2,1)} %copy-done.4) | copy-start | bytes 12582916
  556.4 5.2 copy-start.7
  556.4 5.2 copy-start.29
  562.9 8.1 %copy-start.34 = (f32[4,8,512]{2,1,0:T(8,128)S(1)}, f32[4,8,512]{2,1,0:T(8,128)}, u32[]{:S(2)}) copy-start(f32[4,8,512]{2,1,0:T(8,128)} %reshape.534) | copy-start | bytes 196612
  562.9 8.7 %copy-start.16 = (f32[4,8,8192]{2,1,0:T(8,128)S(1)}, f32[4,8,8192]{2,1,0:T(8,128)}, u32[]{:S(2)}) copy-start(f32[4,8,8192]{2,1,0:T(8,128)} %reshape.537) | copy-start | bytes 3145732
  562.9 9.8 %copy-start.18 = (f32[4,8,4096]{2,1,0:T(8,128)S(1)}, f32[4,8,4096]{2,1,0:T(8,128)}, u32[]{:S(2)}) copy-start(f32[4,8,4096]{2,1,0:T(8,128)} %reshape.538) | copy-start | bytes 1572868
  568.0 5.6 copy-start.55
  568.0 7.1 %copy-start.31 = (bf16[1024,16]{0,1:T(8,128)(2,1)S(1)}, bf16[1024,16]{0,1:T(8,128)(2,1)}, u32[]{:S(2)}) copy-start(bf16[1024,16]{0,1:T(8,128)(2,1)} %copy-done.30) | copy-start | bytes 98308
  568.0 7.1 %copy-start.33 = (bf16[1024,16]{0,1:T(8,128)(2,1)S(1)}, bf16[1024,16]{0,1:T(8,128)(2,1)}, u32[]{:S(2)}) copy-start(bf16[1024,16]{0,1:T(8,128)(2,1)} %convolution_convert_fusion.2) | copy-start | bytes 98308
  573.5 120.0 %reduce-scatter.8.cloned.1.call-start = ((), (), s32[]{:S(2)}) async-start(), calls=%async_computation.8 | async-start | bytes 4718592 | tf_op jit(solution)/shard_map/reduce_scatter | solution.py:667
  575.1 2.4 copy-start.21
  648.9 44.6 %copy-start.43 = (f32[2048]{0:T(1024)S(1)}, f32[2048]{0:T(1024)}, u32[]{:S(2)}) copy-start(f32[2048]{0:T(1024)} %param.30) | copy-start | bytes 24580
  648.9 9.5 %all-to-all-start.1 = ((f32[4,1,22016]{2,1,0:T(1,128)}), f32[4,1,22016]{2,1,0:T(1,128)S(1)}, u32[]{:S(2)}, u32[]{:S(2)}) async-start(f32[4,1,22016]{2,1,0:T(1,128)} %bitcast.50), calls=%async_computation.4 | async-start | bytes 704512 | tf_op jit(solution)/shard_map/all_to_all | solution.py:839
  661.7 35.9 %copy-start.1 = (bf16[4,16,16384]{2,1,0:T(8,128)(2,1)S(1)}, bf16[4,16,16384]{2,1,0:T(8,128)(2,1)}, u32[]{:S(2)}) copy-start(bf16[4,16,16384]{2,1,0:T(8,128)(2,1)} %param.45) | copy-start | bytes 6291460
  (4 other events, 3.9 us)
Sparse Core Ops, SparseCore 0:
  218.9 54.1 all-gather.1
  336.5 46.3 reduce-scatter.5
  385.2 48.2 reduce-scatter.3
  573.7 71.8 all-reduce.2
  647.7 45.8 reduce-scatter.7

commit v3 on v2

--- a/solution.py
+++ b/solution.py
@@ -613,6 +613,505 @@
     )(hidden, cotangent, documents, adapter_row, query_w, kv_w, out_w, gate_w, up_w, down_w)
 
 
+def dot_nn(a, b):
+    return lax.dot_general(a, b, (((1,), (0,)), ((), ())), preferred_element_type=F32)
+
+
+def dot_nt(a, b):
+    return lax.dot_general(a, b, (((1,), (1,)), ((), ())), preferred_element_type=F32)
+
+
+class ChainSum:
+    def __init__(self, place, part, side_in, up_in, down_in, sems):
+        self.p, self.part = place, part
+        self.side_in, self.up_in, self.down_in = side_in, up_in, down_in
+        self.sems = sems
+
+    def _side(self, z):
+        p = self.p
+        return remote(
+            self.part.at[2 * z + 1 - p.c], self.side_in.at[z],
+            self.sems.at[0, z], self.sems.at[1, z], p.seq(p.sib),
+        )
+
+    def _up(self, z):
+        p = self.p
+        return remote(
+            self.part.at[2 * z + p.c], self.up_in.at[z],
+            self.sems.at[2, z], self.sems.at[3, z], p.seq(p.s + 2),
+        )
+
+    def _down(self, z):
+        p = self.p
+        return remote(
+            self.part.at[2 * z + p.c], self.down_in.at[z],
+            self.sems.at[4, z], self.sems.at[5, z], p.seq(p.s - 2),
+        )
+
+    def _add(self, z, incoming):
+        slot = 2 * z + self.p.c
+        rows = self.part.shape[1]
+
+        @pl.loop(0, rows // 16)
+        def _(i):
+            cut = pl.ds(pl.multiple_of(i * 16, 16), 16)
+            total = self.part[slot, cut].astype(F32) + incoming[z, cut].astype(F32)
+            self.part[slot, cut] = total.astype(BF16)
+
+    def side_start(self, z):
+        self._side(z).start()
+
+    def side_add(self, z):
+        self._side(z).wait_recv()
+        self._add(z, self.side_in)
+
+    def step(self, k):
+        p = self.p
+
+        @pl.when(p.z + k < p.chips)
+        def _():
+            to = p.z + k
+            self.side_add(to)
+
+            @pl.when(p.z > 0)
+            def _():
+                self._up(to).wait_recv()
+                self._add(to, self.up_in)
+
+            self._up(to).start()
+
+        @pl.when(p.z >= k)
+        def _():
+            to = p.z - k
+            self.side_add(to)
+
+            @pl.when(p.z < p.chips - 1)
+            def _():
+                self._down(to).wait_recv()
+                self._add(to, self.down_in)
+
+            self._down(to).start()
+
+    def last(self):
+        p = self.p
+        self.side_add(p.z)
+
+        @pl.when(p.z > 0)
+        def _():
+            self._up(p.z).wait_recv()
+            self._add(p.z, self.up_in)
+
+        @pl.when(p.z < p.chips - 1)
+        def _():
+            self._down(p.z).wait_recv()
+            self._add(p.z, self.down_in)
+
+    def finish(self):
+        p = self.p
+        for z in range(p.chips):
+            self._side(z).wait_send()
+        for k in range(1, p.chips):
+
+            @pl.when(p.z + k < p.chips)
+            def _():
+                self._up(p.z + k).wait_send()
+
+            @pl.when(p.z >= k)
+            def _():
+                self._down(p.z - k).wait_send()
+
+
+def swap_halves(values):
+    lane = lax.broadcasted_iota(jnp.int32, values.shape, 1)
+    return jnp.where(
+        lane % HD < HD // 2,
+        pltpu.roll(values, values.shape[1] - HD // 2, 1),
+        pltpu.roll(values, HD // 2, 1),
+    )
+
+
+def mask_bias(seg_col, seg_row, start, size):
+    length = start + size
+    key_pos = lax.broadcasted_iota(jnp.int32, (length, size), 0)
+    query_pos = start + lax.broadcasted_iota(jnp.int32, (length, size), 1)
+    same = seg_col[pl.ds(0, length), 0:1] == seg_row[0:1, pl.ds(start, size)]
+    return jnp.where((key_pos <= query_pos) & same, 0.0, -1e30).astype(F32)
+
+
+QB = 256
+
+
+def back_kernel(
+    seq_size,
+    grad_attn,
+    query,
+    keys2,
+    values2,
+    keys_t,
+    log_totals,
+    seg_row,
+    seg_col,
+    cos_t,
+    sin_t,
+    cos_n,
+    sin_n,
+    qkv_w,
+    qkv_in,
+    low_map,
+    low_qkv_t,
+    norm_one,
+    ffn_part,
+    early_t,
+    gu_grad,
+    down_grad,
+    owners,
+    norm_sum,
+    ffn_sum,
+    share_out,
+    gu_out,
+    down_out,
+    q_out,
+    kv_out,
+    grads,
+    key_z,
+    value_z,
+    key_acc,
+    value_acc,
+    bias,
+    grad_qkv,
+    grad_low,
+    qkv_v,
+    norm_v,
+    ffn_v,
+    ffn_side,
+    ffn_up,
+    ffn_down,
+    sum_v,
+    sum_side,
+    sum_up,
+    sum_down,
+    share,
+    share_in,
+    turned,
+    gu_in,
+    down_in,
+    q_got,
+    kv_got,
+    load_sems,
+    swap_sems,
+    ffn_sems,
+    sum_sems,
+    send_sems,
+    got_sems,
+):
+    p = Place(seq_size)
+    d, s = p.d, p.s
+    length = query.shape[0]
+    chips = p.chips
+    loads = [
+        pltpu.make_async_copy(src, dst, load_sems.at[i])
+        for i, (src, dst) in enumerate(
+            ((ffn_part, ffn_v), (qkv_w, qkv_v), (norm_one, norm_v), (grad_attn.at[s], grads.at[s]))
+        )
+    ]
+    for copy in loads:
+        copy.start()
+    barrier = pltpu.get_barrier_semaphore()
+    everyone = 4 * seq_size
+
+    def place_of(t):
+        return lax.rem(d + t // seq_size, 4), lax.rem(s + lax.rem(t, seq_size), seq_size)
+
+    @pl.loop(1, everyone)
+    def _(t):
+        pl.semaphore_signal(barrier, 1, device_id=place_of(t), device_id_type=MESH)
+
+    pl.semaphore_wait(barrier, everyone - 1)
+
+    def swap_copy(step):
+        return remote(
+            grad_attn.at[p.peer(step)], grads.at[s], swap_sems.at[0, step], swap_sems.at[1, 0],
+            p.seq(p.peer(step)),
+        )
+
+    for step in range(1, seq_size):
+        swap_copy(step).start()
+
+    def deliver(src, dst, td, ts, i, wait):
+        here = (td == d) & (ts == s)
+
+        @pl.when(jnp.logical_not(here))
+        def _():
+            copy = remote(src, dst, send_sems.at[i], got_sems.at[i], (td, ts))
+            if wait:
+                copy.wait_send()
+            else:
+                copy.start()
+
+        if not wait:
+
+            @pl.when(here)
+            def _():
+                pltpu.make_async_copy(src, dst, got_sems.at[i]).start()
+
+    def ready(buffer, i):
+        remote(buffer, buffer, send_sems.at[i], got_sems.at[i], p.seq(p.sib)).wait_recv()
+
+    block = gu_grad.shape[1] // 8
+
+    def deliver_wide(wait):
+        side = pl.ds(pl.multiple_of(block * lax.rem(s, 2), block), block)
+        for e in range(4):
+            for upper in range(2):
+                deliver(
+                    gu_grad.at[:, pl.ds((4 * upper + e) * block, block)],
+                    gu_in.at[d, :, side],
+                    2 * upper + e // 2,
+                    lax.rem(e, 2) * (seq_size // 2) + s // 2,
+                    0,
+                    wait,
+                )
+            deliver(down_grad.at[:, pl.ds(e * block, block)], down_in.at[d], e, s, 1, wait)
+
+    def deliver_heads(wait):
+        for i in range(4):
+            m = 4 * s + i
+            deliver(
+                turned.at[pl.ds(HD * i, HD)], q_got.at[d], m // seq_size, lax.rem(m, seq_size), 2, wait
+            )
+        for i in range(4):
+            m = 2 * seq_size * (i // 2) + 2 * s + i % 2
+            deliver(
+                turned.at[pl.ds(4 * HD + HD // 2 * i, HD // 2)],
+                kv_got.at[d],
+                m // seq_size,
+                lax.rem(m, seq_size),
+                3,
+                wait,
+            )
+
+    def deliver_share(wait):
+        rows = share.shape[0] // everyone
+
+        @pl.loop(0, everyone)
+        def _(t):
+            td, ts = place_of(t)
+            start = pl.multiple_of((td * seq_size + ts) * rows, rows)
+            deliver(share.at[pl.ds(start, rows)], share_in.at[d, s], td, ts, 4, wait)
+
+    ffn = ChainSum(p, ffn_v, ffn_side, ffn_up, ffn_down, ffn_sems)
+    total = ChainSum(p, sum_v, sum_side, sum_up, sum_down, sum_sems)
+
+    low_lane = lax.broadcasted_iota(jnp.int32, (length, 2 * HD), 1) < HD
+    zero = jnp.zeros((length, 2 * HD), BF16)
+    key_z[0] = jnp.where(low_lane, keys2[...], zero)
+    key_z[1] = jnp.where(low_lane, zero, keys2[...])
+    value_z[0] = jnp.where(low_lane, values2[...], zero)
+    value_z[1] = jnp.where(low_lane, zero, values2[...])
+    key_acc[...] = jnp.zeros_like(key_acc)
+    value_acc[...] = jnp.zeros_like(value_acc)
+    for copy in loads:
+        copy.wait()
+    for z in range(chips):
+        ffn.side_start(z)
+    remote(
+        grads.at[pl.ds(0, seq_size - 1)], grads.at[pl.ds(0, seq_size - 1)],
+        swap_sems.at[0, 0], swap_sems.at[1, 0], p.seq(p.sib),
+    ).wait_recv()
+    deliver_wide(False)
+    ffn.step(3)
+
+    def query_block(i):
+        start = i * QB
+        span = pl.ds(0, start + QB)
+        rows = pl.ds(start, QB)
+        bias[span, :] = mask_bias(seg_col, seg_row, start, QB)
+        slots = QB // grads.shape[1]
+
+        for m in range(2):
+            pair = pl.ds(2 * HD * m, 2 * HD)
+            query_pair = query[rows, pair]
+            grad_pair = grads[pl.ds(slots * i, slots), :, pair].reshape(QB, 2 * HD)
+            turned_q = []
+            for e in range(2):
+                h = 2 * m + e
+                scores = dot_nt(key_z[e, span, :], query_pair)
+                weights = jnp.exp(scores * SCORE_SCALE + bias[span, :] - log_totals[h : h + 1, rows])
+                grad_weights = dot_nt(value_z[e, span, :], grad_pair)
+                row_dot = jnp.sum(weights * grad_weights, axis=0, keepdims=True)
+                grad_scores = (weights * (grad_weights - row_dot)).astype(BF16)
+                key_acc[e, span, :] += dot_nn(grad_scores, query_pair)
+                value_acc[e, span, :] += dot_nn(weights.astype(BF16), grad_pair)
+                grad_q = dot_nn(keys_t[:, span], grad_scores) * SCORE_SCALE
+                first, second = grad_q[: HD // 2], grad_q[HD // 2 :]
+                cos_part, sin_part = cos_t[:, rows], sin_t[:, rows]
+                turned_q.append(first * cos_part + second * sin_part)
+                turned_q.append(second * cos_part - first * sin_part)
+            grad_qkv[rows, pair] = jnp.concatenate(turned_q, axis=0).T.astype(BF16)
+
+    query_block(0)
+    query_block(1)
+    query_block(2)
+    ffn.step(2)
+    query_block(3)
+
+    def folded(acc):
+        merged = jnp.where(low_lane, acc[0], acc[1])
+        return merged + pltpu.roll(merged, HD, 1)
+
+    grad_key = folded(key_acc) * SCORE_SCALE
+    grad_key = grad_key * cos_n[...] - swap_halves(grad_key) * sin_n[...]
+    grad_qkv[:, pl.ds(4 * HD, 2 * HD)] = jnp.where(low_lane, grad_key, folded(value_acc)).astype(BF16)
+    grad_low[...] = dot_nt(grad_qkv[...], low_map[...]).astype(BF16)
+    grad_low_t = dot_nt(low_map[...], grad_qkv[...]).astype(BF16)
+    ffn.step(1)
+
+    tokens = sum_v.shape[1]
+
+    def fill(slot):
+        rows = pl.ds(pl.multiple_of(slot * tokens, tokens), tokens)
+        left, low = grad_qkv[rows, :], grad_low[rows, :]
+        for j in range(4):
+            cut = pl.ds(512 * j, 512)
+            sum_v[slot, :, cut] = (
+                dot_nt(left, qkv_v[cut, :]) + dot_nt(low, qkv_in[cut, :])
+            ).astype(BF16)
+
+    for k in (3, 2, 1, 0):
+
+        def give(to):
+            fill(2 * to)
+            fill(2 * to + 1)
+            total.side_start(to)
+
+        @pl.when(p.z + k < chips)
+        def _():
+            give(p.z + k)
+
+        if k:
+
+            @pl.when(p.z >= k)
+            def _():
+                give(p.z - k)
+
+            total.step(k)
+        if k == 2:
+            outer = dot_nn(low_qkv_t[...], grad_qkv[...])
+            outer = jnp.concatenate([outer, jnp.zeros((80, outer.shape[1]), F32)], axis=0)
+            turned[...] = outer.T
+            deliver_heads(False)
+            for j in range(8):
+                cut = pl.ds(256 * j, 256)
+                piece = jnp.concatenate(
+                    [dot_nn(grad_low_t, norm_v[:, cut]), early_t[:, cut]], axis=0
+                )
+                share[cut, :] = piece.T.astype(BF16)
+            deliver_share(False)
+    ffn.last()
+    ffn_sum[...] = ffn_v[s].astype(F32)
+    for buffer, i in ((gu_in, 0), (down_in, 1), (q_got, 2), (kv_got, 3), (share_in, 4)):
+        ready(buffer, i)
+
+    def by_adapter(out, value):
+        values = [value(e) for e in range(4)]
+        for a in range(4):
+            chosen = jnp.zeros_like(values[0])
+            for e in range(4):
+                chosen = jnp.where(owners[e, 0:1, 0:1] == a, values[e], chosen)
+            out[a] = chosen
+
+    by_adapter(gu_out, lambda e: gu_in[e])
+    by_adapter(down_out, lambda e: down_in[e])
+    by_adapter(q_out, lambda e: q_got[e])
+    by_adapter(kv_out, lambda e: kv_got[e])
+    by_adapter(share_out, lambda e: jnp.sum(share_in[e].astype(F32), axis=0))
+    total.last()
+    norm_sum[...] = sum_v[s].astype(F32)
+    for step in range(1, seq_size):
+        swap_copy(step).wait_send()
+    deliver_wide(True)
+    deliver_heads(True)
+    deliver_share(True)
+    ffn.finish()
+    total.finish()
+
+
+def back_all(seq_size, ins):
+    (grad_attn, query, keys2) = ins[:3]
+    _, tokens, width_q = grad_attn.shape
+    length = query.shape[0]
+    width = ins[16].shape[1]
+    qkv_width = ins[12].shape[1]
+    chips = seq_size // 2
+    rows = width // (4 * seq_size)
+    rank = ins[19].shape[0]
+    block = ins[19].shape[1] // 8
+
+    def shape(*dims):
+        return jax.ShapeDtypeStruct(dims, F32)
+
+    vmem = pl.BlockSpec(memory_space=pltpu.VMEM)
+    anywhere = pl.BlockSpec(memory_space=pl.ANY)
+    far = (0, 12, 16, 17)
+    outs = (
+        shape(tokens, width),
+        shape(tokens, width),
+        shape(4, rows, 128),
+        shape(4, rank, 2 * block),
+        shape(4, rank, block),
+        shape(4, HD, 128),
+        shape(4, HD // 2, 128),
+    )
+    many = (seq_size, tokens, width)
+    few = (chips, tokens, width)
+    return pl.pallas_call(
+        functools.partial(back_kernel, seq_size),
+        out_shape=outs,
+        in_specs=[anywhere if i in far else vmem for i in range(len(ins))],
+        out_specs=(vmem,) * len(outs),
+        scratch_shapes=[
+            pltpu.VMEM(grad_attn.shape, BF16),
+            pltpu.VMEM((2, length, 2 * HD), BF16),
+            pltpu.VMEM((2, length, 2 * HD), BF16),
+            pltpu.VMEM((2, length, 2 * HD), F32),
+            pltpu.VMEM((2, length, 2 * HD), F32),
+            pltpu.VMEM((length, QB), F32),
+            pltpu.VMEM((length, qkv_width), BF16),
+            pltpu.VMEM((length, 3 * rank), BF16),
+            pltpu.VMEM(ins[12].shape, BF16),
+            pltpu.VMEM((length, width), BF16),
+            pltpu.VMEM(many, BF16),
+            pltpu.VMEM(few, BF16),
+            pltpu.VMEM(few, BF16),
+            pltpu.VMEM(few, BF16),
+            pltpu.VMEM(many, BF16),
+            pltpu.VMEM(few, BF16),
+            pltpu.VMEM(few, BF16),
+            pltpu.VMEM(few, BF16),
+            pltpu.VMEM((width, 128), BF16),
+            pltpu.VMEM((4, seq_size, rows, 128), BF16),
+            pltpu.VMEM((qkv_width, 128), F32),
+            pltpu.VMEM((4, rank, 2 * block), F32),
+            pltpu.VMEM((4, rank, block), F32),
+            pltpu.VMEM((4, HD, 128), F32),
+            pltpu.VMEM((4, HD // 2, 128), F32),
+            pltpu.SemaphoreType.DMA((4,)),
+            pltpu.SemaphoreType.DMA((2, seq_size)),
+            pltpu.SemaphoreType.DMA((6, chips)),
+            pltpu.SemaphoreType.DMA((6, chips)),
+            pltpu.SemaphoreType.DMA((5,)),
+            pltpu.SemaphoreType.DMA((5,)),
+        ],
+        compiler_params=pltpu.CompilerParams(
+            collective_id=1, has_side_effects=True, vmem_limit_bytes=60 * 2**20
+        ),
+        cost_estimate=pl.CostEstimate(
+            flops=10 * 10**9, bytes_accessed=20 * 2**20, transcendentals=4 * 2**20
+        ),
+        name="attend_back",
+    )(*ins)
+
+
 def make_local(dp_size, seq_size):
     devices = dp_size * seq_size
     heads = NH // seq_size
@@ -754,8 +1253,7 @@
         sigma = jax.nn.sigmoid(gate)
         activation = (gate * sigma * up_proj).astype(BF16)
         low_down = mm(activation, down_in).astype(BF16)
-        ffn = scatter_seq((mm(activation, down) + mm(low_down, down_out)).astype(BF16))
-        mixed = (middle_own + RESIDUAL_SCALE * ffn.astype(F32)).astype(BF16)
+        ffn_part = (mm(activation, down) + mm(low_down, down_out)).astype(BF16)
 
         grad_ffn = (RESIDUAL_SCALE * cotangent_all.astype(F32)).astype(BF16)
         grad_low_down = mm_t(grad_ffn, down_out).astype(BF16)
@@ -776,6 +1274,79 @@
         grad_branch = (RESIDUAL_SCALE * grad_middle).astype(BF16)
         grad_low_out = mm_t(grad_branch, o_out).astype(BF16)
         grad_attn = (mm_t(grad_branch, out_full) + mm_t(grad_low_out, o_in)).astype(BF16)
+        attn_own = lax.dynamic_slice_in_dim(attn, own_row, tokens, 0)
+        low_out_own = lax.dynamic_slice_in_dim(low_out, own_row, tokens, 0)
+        if kernels:
+            early = jnp.concatenate(
+                [
+                    t_mm(grad_low_out, attn_own),
+                    t_mm(low_out_own, grad_branch),
+                    t_mm(grad_low_gu, norm_two),
+                    t_mm(low_down, grad_ffn),
+                ],
+                axis=0,
+            )
+            gu_grad = jnp.concatenate(
+                [t_mm(low_gu[:, :rank], grad_gate), t_mm(low_gu[:, rank:], grad_up)], axis=1
+            )
+            none_q = jnp.zeros((rank, q_width), BF16)
+            none_h = jnp.zeros((rank, HD), BF16)
+            low_map = jnp.concatenate(
+                [
+                    jnp.concatenate([q_out, none_h, none_h], axis=1),
+                    jnp.concatenate([none_q, k_out, none_h], axis=1),
+                    jnp.concatenate([none_q, none_h, v_out], axis=1),
+                ],
+                axis=0,
+            )
+            sums = back_all(
+                seq_size,
+                (
+                    jnp.swapaxes(grad_attn.reshape(tokens, seq_size, q_width), 0, 1),
+                    query.reshape(length, q_width),
+                    jnp.concatenate([keys, keys], axis=1),
+                    jnp.concatenate([values, values], axis=1),
+                    keys.T,
+                    jnp.swapaxes(log_totals, 0, 1).reshape(heads, length),
+                    segments[None],
+                    jnp.broadcast_to(segments[:, None], (length, 128)),
+                    cos_table.T,
+                    sin_table.T,
+                    jnp.tile(cos_table, (1, 4)),
+                    jnp.tile(jnp.concatenate([-sin_table, sin_table], axis=1), (1, 2)),
+                    qkv,
+                    qkv_in,
+                    low_map,
+                    low_qkv.T,
+                    norm_one,
+                    ffn_part.reshape(seq_size, tokens, width),
+                    early,
+                    gu_grad,
+                    t_mm(grad_low_down, activation),
+                    gathered[3],
+                ),
+            )
+            norm_sum, ffn_sum, share, gu_got, down_got, q_got, kv_got = sums
+            mixed = (middle_own + RESIDUAL_SCALE * ffn_sum).astype(BF16)
+            grad_hidden = grad_middle + rms_back(hidden_own, attention_norm_gain, norm_sum)
+            lower = lax.axis_index("dp") < dp_size // 2
+            kv_got = jnp.where(lower, kv_got[:, :, rank : 2 * rank], kv_got[:, :, 2 * rank : 3 * rank])
+            share_t = jnp.swapaxes(share, 1, 2)
+            return (
+                mixed[None],
+                grad_hidden.astype(BF16)[None],
+                share[:, :, : 3 * rank],
+                jnp.swapaxes(q_got[:, :, :rank], 1, 2),
+                jnp.swapaxes(kv_got, 1, 2),
+                share[:, :, 3 * rank : 4 * rank],
+                share_t[:, 4 * rank : 5 * rank],
+                share[:, :, 5 * rank : 7 * rank],
+                gu_got,
+                jnp.swapaxes(down_got, 1, 2),
+                share_t[:, 7 * rank :],
+            )
+        ffn = lax.psum_scatter(ffn_part, "seq", scatter_dimension=0, tiled=True)
+        mixed = (middle_own + RESIDUAL_SCALE * ffn.astype(F32)).astype(BF16)
         grad_heads = lax.all_to_all(
             jnp.swapaxes(grad_attn.reshape(tokens, seq_size, q_width), 0, 1),
             "seq",
@@ -799,8 +1370,6 @@
             hidden_own, attention_norm_gain, grad_norm_one.astype(F32)
         )
 
-        attn_own = lax.dynamic_slice_in_dim(attn, own_row, tokens, 0)
-        low_out_own = lax.dynamic_slice_in_dim(low_out, own_row, tokens, 0)
         partial = jnp.concatenate(
             [
                 t_mm(norm_one, grad_low_qkv),

time: 719 us -> 564 us (0.78)
  waiting for transfers between devices: 186 us -> 54.1 us
  Pallas kernels: 161 us -> 275 us
  matrix products: 176 us -> 114 us
  local copies, waits for them, and re-layouts: 99.4 us -> 46.6 us
  starting transfers between devices: 12.3 us -> 0.08 us
    pallas_call x0 -> x1, Pallas kernels: none -> 114 us  [back_all(): pl.pallas_call(functools.partial(back_kernel, seq_size), out_shape=outs,...]
    reduce_scatter x3 -> x1, waiting for transfers between devices: 79.5 us -> 14.4 us  [scatter_seq(): return lax.psum_scatter(total, 'seq', scatter_dimension=0, tiled=True)]
    unnamed x6 -> x2, waiting for transfers between devices: 63.7 us -> 0.03 us
    dot_general x9 -> x0, matrix products: 32.7 us -> none  [the longest x2 10.9 us: one_block(): jnp.einsum('hqk,qhd->kd', weights.astype(BF16), grad_block, preferred_ele...]
    reshape x11 -> x0, local copies, waits for them, and re-layouts: 26.3 us -> none  [the longest x4 15.6 us: by_target(): return whole.reshape(dp_size, seq_size, -1)]
    all_to_all x2 -> x0, starting transfers between devices: 12.1 us -> none  [the longest x1 8.35 us: local(): lax.all_to_all(jnp.swapaxes(grad_attn.reshape(tokens, seq_size, q_width),...]
    unnamed x132 -> x130, local copies, waits for them, and re-layouts: 30.7 us -> 19.9 us
    convert_element_type x6 -> x1, other arithmetic: 10 us -> 0.04 us  [local(): rotate(query_pre.reshape(length, heads, HD), cos_table, sin_table)]
  transfers between devices with their start and end apart: 7 -> 2, of which waited for: 6 -> 2; matrix products, arithmetic and copies ran while one was open for 15% -> 8% of each run, Pallas kernels for 0% -> 0%
where the time goes in v3:
time: 564 us; the launch traced here: 555 us
  Pallas kernels  275 us (49%)
  matrix products  114 us (20%)
  waiting for transfers between devices  54.1 us (10%)
  other arithmetic  48.2 us (9%)
  local copies, waits for them, and re-layouts  46.6 us (8%)
  between operations  15.9 us (3%)
    pallas_call x1, Pallas kernels, gather_all(): pl.pallas_call(functools.partial(gather_kernel, seq_size), out_shape=(sha...  161 us
    pallas_call x1, Pallas kernels, back_all(): pl.pallas_call(functools.partial(back_kernel, seq_size), out_shape=outs,...  114 us
    dot_general x15, matrix products, mm(): return jnp.dot(a, b, preferred_element_type=F32)  57.6 us
    all_gather x1, waiting for transfers between devices, local(): attn = lax.all_gather(attn_heads, 'seq', axis=1, tiled=True)  39.6 us
    dot_general x10, matrix products, mm_t(): lax.dot_general(a, b, (((1,), (1,)), ((), ())), preferred_element_type=F32)  37.9 us
    unnamed x130, local copies, waits for them, and re-layouts  19.9 us
    reduce_scatter x1, waiting for transfers between devices, scatter_seq(): return lax.psum_scatter(total, 'seq', scatter_dimension=0, tiled=True)  14.4 us
  transfers between devices with their start and end apart: 2, of which 2 were waited for; matrix products, arithmetic and copies ran while one was open for 8% of the time, Pallas kernels for 0%

profile of v3, /device:TPU:8, one launch (start us, length us, event | category | flops | bytes accessed | tf_op | source)
XLA Modules:
  0.0 555.1 jit_solution(8620155436254596675)
XLA Ops:
  11.5 1.2 broadcast_in_dim.47.documents
  12.7 161.0 %gather_all.1 = (bf16[8,128,2048]{2,1,0:T(8,128)(2,1)}, bf16[8,128,2048]{2,1,0:T(8,128)(2,1)}, s32[8,8,128]{2,1,0:T(8,128)}, s32[4,8,128]{2,1,0:T(8,128)}, bf16[...) custom-call(bf16[128,2048]{1,0:T(8,128)(2,1)} %bitcast.223, ...), custom_call_target="tpu_custom_call" | custom-call | bytes 62914560 | tf_op jit(solution)/shard_map/gather_all/pallas_call | solution.py:582
  173.8 7.7 %fusion.14 = (f32[8,128]{1,0:T(8,128)S(1)}, bf16[8,128,2048]{2,1,0:T(8,128)(2,1)}) fusion(bf16[8,128,2048]{2,1,0:T(8,128)(2,1)} %get-tuple-element.74, bf16[8,128,2048]{2,1,0:T(8,128)(2,1)} %get-tuple-element.79), kind=kLoop, calls=%fused_computation.25 | loop fusion | flops 12581888 | bytes 12587008 | tf_op jit(solution)/shard_map/reduce_sum | solution.py:36
  183.0 3.3 fusion.16
  186.3 1.4 convolution_convert_fusion
  187.7 1.9 fusion.97
  191.3 1.2 fusion.65
  192.6 1.2 fusion.57
  195.2 1.6 convolution_add_fusion.2
  197.7 1.3 fusion.24
  199.9 1.3 slice_bitcast_fusion.1
  201.2 1.6 fusion.93
  202.8 1.0 multiply_subtract_fusion
  204.0 21.8 %while.12 = (s32[]{:T(128)}, bf16[2,512,4,64]{1,3,2,0:T(8,128)(2,1)}, f32[2,4,512]{2,1,0:T(4,128)}, s32[2]{0:T(128)S(1)}, s32[1024]{0:T(1024)S(1)}, /*index=5*/s...) while((s32[]{:T(128)}, ...), condition=%wide.region_4.5_spmd, body=%wide.region_1.4_spmd.sunk | while | flops 563739136 | bytes 32979288 | solution.py:92
  206.0 2.5 bitcast_reduce_fusion.2
  208.5 2.4 fusion.150
  211.0 3.1 fusion.151
  216.8 2.5 bitcast_reduce_fusion.2
  219.3 2.4 fusion.150
  221.8 3.1 fusion.151
  225.7 1.6 copy.78
  228.7 1.1 constant_dynamic-slice_fusion.2
  230.2 3.4 convolution_convert_fusion.6
  233.6 6.6 %fusion.99 = f32[1024,1024]{0,1:T(8,128)S(1)} fusion(bf16[1024,2048]{1,0:T(8,128)(2,1)S(1)} %bitcast.217, bf16[1024,2048]{1,0:T(8,128)(2,1)} %bitcast.261), kind=kOutput, calls=%fused_computation.183 | convolution fusion | flops 4294967296 | bytes 12582912 | tf_op jit(solution)/shard_map/dot_general | solution.py:28
  240.2 2.7 convolution_add_fusion.1
  242.9 39.6 %all-gather.2.cloned.1.call-done = bf16[1024,2048]{0,1:T(8,128)(2,1)} async-done(((bf16[1024,256]{0,1:T(8,128)(2,1)}), bf16[1024,2048]{0,1:T(8,128)(2,1)}) %all-gather.2.cloned.1.call-update) | async-done | bytes 4194320 | tf_op jit(solution)/shard_map/all_gather | solution.py:1242
  282.5 14.0 %fusion.98 = f32[1024,2048]{1,0:T(8,128)S(1)} fusion(bf16[1024,2048]{0,1:T(8,128)(2,1)} %all-gather.2.cloned.1.call-done, bf16[2048,2048]{1,0:T(8,128)(2,1)} %bitcast.221), kind=kOutput, calls=%fused_computation.182 | convolution fusion | flops 8589934592 | bytes 20971520 | tf_op jit(solution)/shard_map/dot_general | solution.py:24
  296.6 1.6 convolution_convert_fusion.5
  298.8 3.2 multiply_reduce_fusion
  302.8 2.5 copy-done.3
  305.3 15.2 %fusion.100 = f32[1024,2048]{0,1:T(8,128)} fusion(bf16[1024,2048]{1,0:T(8,128)(2,1)S(1)} %multiply_convert_fusion, bf16[2048,2048]{1,0:T(8,128)(2,1)} %bitcast.259), kind=kOutput, calls=%fused_computation.184 | convolution fusion | flops 8589934592 | bytes 20971520 | tf_op jit(solution)/shard_map/dot_general | solution.py:24
  320.5 1.3 convolution_convert_fusion.1
  321.9 3.5 slice_add_fusion
  325.4 1.2 copy-done.14
  326.6 2.7 multiply_convert_fusion.2
  329.7 12.6 %fusion.19 = f32[1024,2048]{1,0:T(8,128)S(1)} fusion(bf16[2048,2048]{1,0:T(8,128)(2,1)} %bitcast.260, bf16[1024,1024]{0,1:T(8,128)(2,1)S(1)} %get-tuple-element.177, bf16[1024,1024]{0,1:T(8,128)(2,1)S(1)} %get-tuple-element.176), kind=kOutput, calls=%fused_computation.37 | convolution fusion | flops 8598323200 | bytes 20971520 | tf_op jit(solution)/shard_map/dot_general | solution.py:28
  343.4 3.3 add_convert_fusion.1
  349.5 1.8 copy.87.keys2
  354.3 1.0 copy.88.cos_n
  356.8 1.2 multiply_sine_fusion
  358.1 5.4 fusion.18.norm_one
  365.9 1.3 fusion.103.down_grad
  369.6 4.7 fusion.101
  374.3 4.6 add_convert_fusion
  378.9 14.4 %reduce-scatter.2.cloned.1.call-done = bf16[128,2048]{1,0:T(8,128)(2,1)} async-done(((bf16[1024,2048]{1,0:T(8,128)(2,1)}), bf16[128,2048]{1,0:T(8,128)(2,1)}) %reduce-scatter.2.cloned.1.call-update) | async-done | bytes 524304 | tf_op jit(solution)/shard_map/reduce_scatter | solution.py:1166
  393.3 1.6 multiply_reduce_fusion.2
  395.0 1.7 subtract_add_fusion
  396.8 1.1 convolution_convert_fusion.7
  397.8 1.6 fusion.77
  399.4 6.3 %fusion.94 = f32[128,2048]{1,0:T(8,128)S(1)} fusion(bf16[2048,2048]{1,0:T(8,128)(2,1)} %bitcast.222, f32[128,2048]{1,0:T(8,128)S(1)} %subtract_add_fusion), kind=kOutput, calls=%fused_computation.178 | convolution fusion | flops 1074266112 | bytes 10485760 | tf_op jit(solution)/shard_map/dot_general | solution.py:28
  405.7 1.2 fusion.23
  407.1 1.0 copy.85
  408.1 1.3 fusion.34
  409.4 1.8 pad_maximum_fusion.early_t
  412.2 113.8 %attend_back.1 = (f32[128,2048]{1,0:T(8,128)}, f32[128,2048]{1,0:T(8,128)}, f32[4,64,128]{2,1,0:T(8,128)}, f32[4,16,512]{2,1,0:T(8,128)}, f32[4,16,256]{2,1,0:T(...) custom-call(bf16[8,128,256]{2,1,0:T(8,128)(2,1)} %bitcast.239, bf16[1024,256]{1,0:T(8,128)(2,1)} %copy.86.query, ...), custom_call_target="tpu_custom_call" | custom-call | flops 10000000000 | bytes 20971520 | tf_op jit(solution)/shard_map/attend_back/pallas_call | solution.py:1067
  526.0 1.1 slice.100
  528.1 1.7 fusion.26
  530.3 2.5 fusion.32
  533.6 1.6 copy.94
  535.2 1.6 copy.96
  539.9 1.0 select_bitcast_fusion
  542.3 2.6 fusion.33
  545.0 1.6 copy.122
  546.6 1.5 copy.123
  (214 shorter events, 38.4 us)
Async XLA Ops:
  7.2 221.1 %copy-start = (bf16[4,16,16384]{2,1,0:T(8,128)(2,1)S(1)}, bf16[4,16,16384]{2,1,0:T(8,128)(2,1)}, u32[]{:S(2)}) copy-start(bf16[4,16,16384]{2,1,0:T(8,128)(2,1)} %param.43) | copy-start | bytes 6291460
  7.2 275.3 %all-gather.2.cloned.1.call-start = ((), (), s32[]{:S(2)}) async-start(), calls=%async_computation.1 | async-start | bytes 4718592 | tf_op jit(solution)/shard_map/all_gather | solution.py:1242
  7.3 185.3 %copy-start.48 = (f32[1024]{0:T(1024)}, f32[1024]{0:T(1024)S(1)}, u32[]{:S(2)}) copy-start(f32[1024]{0:T(1024)S(1)} %iota_convert_fusion) | copy-start | bytes 12292
  7.3 185.3 %copy-start.55 = (f32[32]{0:T(128)}, f32[32]{0:T(128)S(1)}, u32[]{:S(2)}) copy-start(f32[32]{0:T(128)S(1)} %multiply_exponential_fusion) | copy-start | bytes 388
  173.7 9.2 %copy-start.40 = (f32[2048]{0:T(1024)S(1)}, f32[2048]{0:T(1024)}, u32[]{:S(2)}) copy-start(f32[2048]{0:T(1024)} %param.28) | copy-start | bytes 24580
  183.0 3.3 copy-start.20
  186.3 1.4 copy-start.58
  187.7 2.8 copy-start.30
  189.6 1.2 copy-start.22
  190.5 9.4 %copy-start.50 = (bf16[16,64]{1,0:T(8,128)(2,1)}, bf16[16,64]{1,0:T(8,128)(2,1)S(1)}, u32[]{:S(2)}) copy-start(bf16[16,64]{1,0:T(8,128)(2,1)S(1)} %get-tuple-element.186) | copy-start | bytes 6148
  192.6 11.4 %copy-start.23 = (f32[1024,32]{0,1:T(8,128)}, f32[1024,32]{0,1:T(8,128)S(1)}, u32[]{:S(2)}) copy-start(f32[1024,32]{0,1:T(8,128)S(1)} %get-tuple-element.194) | copy-start | bytes 393220
  199.1 4.9 copy-start.16
  208.5 2.5 copy-start.59
  208.5 2.5 copy-start.28
  208.5 2.5 copy-start.43
  211.0 3.1 copy-start.60
  219.3 2.5 copy-start.59
  219.3 2.5 copy-start.28
  219.3 2.5 copy-start.43
  221.8 3.1 copy-start.60
  228.2 165.1 %reduce-scatter.2.cloned.1.call-start = ((), (), s32[]{:S(2)}) async-start(), calls=%async_computation.2 | async-start | bytes 4718592 | tf_op jit(solution)/shard_map/reduce_scatter | solution.py:1166
  228.4 5.1 copy-start.6
  230.1 10.1 %copy-start.37 = (bf16[2,8,4,256]{3,1,2,0:T(8,128)(2,1)}, bf16[2,8,4,256]{3,1,2,0:T(8,128)(2,1)S(1)}, u32[]{:S(2)}) copy-start(bf16[2,8,4,256]{3,1,2,0:T(8,128)(2,1)S(1)} %copy.102) | copy-start | bytes 98308
  233.5 6.6 %copy-start.31 = (bf16[1024,16]{0,1:T(8,128)(2,1)}, bf16[1024,16]{0,1:T(8,128)(2,1)S(1)}, u32[]{:S(2)}) copy-start(bf16[1024,16]{0,1:T(8,128)(2,1)S(1)} %convolution_convert_fusion.6) | copy-start | bytes 98308
  282.5 14.0 %copy-start.12 = (bf16[1024,2048]{0,1:T(8,128)(2,1)S(1)}, bf16[1024,2048]{0,1:T(8,128)(2,1)}, u32[]{:S(2)}) copy-start(bf16[1024,2048]{0,1:T(8,128)(2,1)} %all-gather.2.cloned.1.call-done) | copy-start | bytes 12582916
  296.6 2.2 copy-start.2
  298.8 3.2 copy-start.39
  298.8 3.3 copy-start.44
  302.0 3.3 copy-start.3
  305.3 15.2 %copy-start.4 = (bf16[1024,2048]{1,0:T(8,128)(2,1)}, bf16[1024,2048]{1,0:T(8,128)(2,1)S(1)}, u32[]{:S(2)}) copy-start(bf16[1024,2048]{1,0:T(8,128)(2,1)S(1)} %multiply_convert_fusion) | copy-start | bytes 12582916
  305.3 15.2 %copy-start.42 = (bf16[4,2048,32]{1,2,0:T(8,128)(2,1)S(1)}, bf16[4,2048,32]{1,2,0:T(8,128)(2,1)}, u32[]{:S(2)}) copy-start(bf16[4,2048,32]{1,2,0:T(8,128)(2,1)} %param.42) | copy-start | bytes 1572868
  320.5 4.9 copy-start.18
  321.8 4.7 copy-start.14
  329.3 13.1 %copy-start.8 = (bf16[1024,1024]{0,1:T(8,128)(2,1)}, bf16[1024,1024]{0,1:T(8,128)(2,1)S(1)}, u32[]{:S(2)}) copy-start(bf16[1024,1024]{0,1:T(8,128)(2,1)S(1)} %get-tuple-element.177) | copy-start | bytes 6291460
  329.3 13.1 %copy-start.10 = (bf16[1024,1024]{0,1:T(8,128)(2,1)}, bf16[1024,1024]{0,1:T(8,128)(2,1)S(1)}, u32[]{:S(2)}) copy-start(bf16[1024,1024]{0,1:T(8,128)(2,1)S(1)} %get-tuple-element.176) | copy-start | bytes 6291460
  329.7 13.1 %copy-start.33 = (bf16[1024,16]{0,1:T(8,128)(2,1)}, bf16[1024,16]{0,1:T(8,128)(2,1)S(1)}, u32[]{:S(2)}) copy-start(bf16[1024,16]{0,1:T(8,128)(2,1)S(1)} %convolution_convert_fusion.3) | copy-start | bytes 98308
  346.7 0.9 copy-start.21
  346.8 1.9 copy-start.26
  346.8 1.9 copy-start.27
  346.8 5.5 copy-start.25
  346.8 7.4 %copy-start.24 = (f32[1024,32]{0,1:T(8,128)S(1)}, f32[1024,32]{0,1:T(8,128)}, u32[]{:S(2)}) copy-start(f32[1024,32]{0,1:T(8,128)} %copy-done.23) | copy-start | bytes 393220
  346.8 9.2 %copy-start.17 = (bf16[1024,64]{1,0:T(8,128)(2,1)S(1)}, bf16[1024,64]{1,0:T(8,128)(2,1)}, u32[]{:S(2)}) copy-start(bf16[1024,64]{1,0:T(8,128)(2,1)} %copy-done.16) | copy-start | bytes 393220
  346.8 10.0 %copy-start.49 = (f32[1024]{0:T(1024)S(1)}, f32[1024]{0:T(1024)}, u32[]{:S(2)}) copy-start(f32[1024]{0:T(1024)} %copy-done.48) | copy-start | bytes 12292
  346.8 11.3 %copy-start.41 = (f32[2048]{0:T(1024)S(1)}, f32[2048]{0:T(1024)}, u32[]{:S(2)}) copy-start(f32[2048]{0:T(1024)} %param.28) | copy-start | bytes 24580
  348.7 6.6 %copy-start.47 = (bf16[16,256]{1,0:T(8,128)(2,1)S(1)}, bf16[16,256]{1,0:T(8,128)(2,1)}, u32[]{:S(2)}) copy-start(bf16[16,256]{1,0:T(8,128)(2,1)} %copy-done.46) | copy-start | bytes 24580
  348.7 6.6 %copy-start.51 = (bf16[16,64]{1,0:T(8,128)(2,1)S(1)}, bf16[16,64]{1,0:T(8,128)(2,1)}, u32[]{:S(2)}) copy-start(bf16[16,64]{1,0:T(8,128)(2,1)} %copy-done.50) | copy-start | bytes 6148
  348.7 6.6 %copy-start.53 = (bf16[16,64]{1,0:T(8,128)(2,1)S(1)}, bf16[16,64]{1,0:T(8,128)(2,1)}, u32[]{:S(2)}) copy-start(bf16[16,64]{1,0:T(8,128)(2,1)} %copy-done.52) | copy-start | bytes 6148
  348.7 8.1 %copy-start.56 = (f32[32]{0:T(128)S(1)}, f32[32]{0:T(128)}, u32[]{:S(2)}) copy-start(f32[32]{0:T(128)} %copy-done.55) | copy-start | bytes 388
  348.7 9.4 %copy-start.54 = (f32[1024]{0:T(1024)S(1)}, f32[1024]{0:T(1024)}, u32[]{:S(2)}) copy-start(f32[1024]{0:T(1024)} %get-tuple-element.197) | copy-start | bytes 12292
  358.1 5.4 copy-start.11
  358.1 6.1 %copy-start.9 = (bf16[1024,1024]{0,1:T(8,128)(2,1)S(1)}, bf16[1024,1024]{0,1:T(8,128)(2,1)}, u32[]{:S(2)}) copy-start(bf16[1024,1024]{0,1:T(8,128)(2,1)} %copy-done.8) | copy-start | bytes 6291460
  363.5 2.0 copy-start.38
  363.5 2.4 copy-start.32
  363.5 3.7 copy-start.7
  365.5 2.4 copy-start.5
  365.5 2.4 copy-start.34
  365.5 2.4 copy-start.36
  367.2 2.4 copy-start.57
  374.2 19.1 %copy-start.45 = (f32[2048]{0:T(1024)S(1)}, f32[2048]{0:T(1024)}, u32[]{:S(2)}) copy-start(f32[2048]{0:T(1024)} %param.29) | copy-start | bytes 24580
  374.3 20.7 %copy-start.19 = (bf16[1,128,2048]{2,1,0:T(8,128)(2,1)S(1)}, bf16[1,128,2048]{2,1,0:T(8,128)(2,1)}, u32[]{:S(2)}) copy-start(bf16[1,128,2048]{2,1,0:T(8,128)(2,1)} %param.27) | copy-start | bytes 1572868
  406.8 5.4 copy-start.61
  412.2 115.9 %copy-start.13 = (bf16[1,128,2048]{2,1,0:T(8,128)(2,1)S(1)}, bf16[1,128,2048]{2,1,0:T(8,128)(2,1)}, u32[]{:S(2)}) copy-start(bf16[1,128,2048]{2,1,0:T(8,128)(2,1)} %param.24) | copy-start | bytes 1572868
  526.0 6.8 %copy-start.15 = (f32[4,64,128]{2,1,0:T(8,128)S(1)}, f32[4,64,128]{2,1,0:T(8,128)}, u32[]{:S(2)}) copy-start(f32[4,64,128]{2,1,0:T(8,128)} %get-tuple-element.86) | copy-start | bytes 393220
  528.1 19.9 %copy-start.1 = (bf16[4,16,16384]{2,1,0:T(8,128)(2,1)S(1)}, bf16[4,16,16384]{2,1,0:T(8,128)(2,1)}, u32[]{:S(2)}) copy-start(bf16[4,16,16384]{2,1,0:T(8,128)(2,1)} %param.43) | copy-start | bytes 6291460
  (5 other events, 3.4 us)
Sparse Core Ops, SparseCore 0:
  228.3 54.1 all-gather.1
  346.9 46.3 reduce-scatter.1

commit v4 on v3

--- a/solution.py
+++ b/solution.py
@@ -3,6 +3,7 @@
 
 import jax
 import jax.numpy as jnp
+import numpy as np
 from jax import lax
 from jax.experimental import pallas as pl
 from jax.experimental.pallas import tpu as pltpu
@@ -48,6 +49,13 @@
     frequency = jnp.exp(steps * (-2.0 * math.log(ROPE_BASE) / head_size))
     angles = positions[:, None] * frequency[None, :]
     return (jnp.cos(angles), jnp.sin(angles))
+
+
+def fixed_tables(length):
+    steps = np.arange(HD // 2, dtype=np.float32)
+    frequency = np.exp(steps * np.float32(-2.0 * math.log(ROPE_BASE) / HD))
+    angles = np.arange(length, dtype=np.float32)[:, None] * frequency[None, :]
+    return (np.cos(angles), np.sin(angles))
 
 
 def rotate(values, cos_table, sin_table):
@@ -319,10 +327,136 @@
             remote(whole, whole, self.send_sem, self.recv_sem, p.seq(p.sib)).wait_send()
 
 
+def dot_nn(a, b):
+    return lax.dot_general(a, b, (((1,), (0,)), ((), ())), preferred_element_type=F32)
+
+
+def dot_nt(a, b):
+    return lax.dot_general(a, b, (((1,), (1,)), ((), ())), preferred_element_type=F32)
+
+
+class ChainSum:
+    def __init__(self, place, part, side_in, up_in, down_in, sems):
+        self.p, self.part = place, part
+        self.side_in, self.up_in, self.down_in = side_in, up_in, down_in
+        self.sems = sems
+
+    def _side(self, z):
+        p = self.p
+        return remote(
+            self.part.at[2 * z + 1 - p.c], self.side_in.at[z],
+            self.sems.at[0, z], self.sems.at[1, z], p.seq(p.sib),
+        )
+
+    def _up(self, z):
+        p = self.p
+        return remote(
+            self.part.at[2 * z + p.c], self.up_in.at[z],
+            self.sems.at[2, z], self.sems.at[3, z], p.seq(p.s + 2),
+        )
+
+    def _down(self, z):
+        p = self.p
+        return remote(
+            self.part.at[2 * z + p.c], self.down_in.at[z],
+            self.sems.at[4, z], self.sems.at[5, z], p.seq(p.s - 2),
+        )
+
+    def _add(self, z, incoming):
+        slot = 2 * z + self.p.c
+        rows = self.part.shape[1]
+
+        @pl.loop(0, rows // 16)
+        def _(i):
+            cut = pl.ds(pl.multiple_of(i * 16, 16), 16)
+            total = self.part[slot, cut].astype(F32) + incoming[z, cut].astype(F32)
+            self.part[slot, cut] = total.astype(BF16)
+
+    def side_start(self, z):
+        self._side(z).start()
+
+    def side_add(self, z):
+        self._side(z).wait_recv()
+        self._add(z, self.side_in)
+
+    def step(self, k):
+        p = self.p
+
+        @pl.when(p.z + k < p.chips)
+        def _():
+            to = p.z + k
+            self.side_add(to)
+
+            @pl.when(p.z > 0)
+            def _():
+                self._up(to).wait_recv()
+                self._add(to, self.up_in)
+
+            self._up(to).start()
+
+        @pl.when(p.z >= k)
+        def _():
+            to = p.z - k
+            self.side_add(to)
+
+            @pl.when(p.z < p.chips - 1)
+            def _():
+                self._down(to).wait_recv()
+                self._add(to, self.down_in)
+
+            self._down(to).start()
+
+    def last(self):
+        p = self.p
+        self.side_add(p.z)
+
+        @pl.when(p.z > 0)
+        def _():
+            self._up(p.z).wait_recv()
+            self._add(p.z, self.up_in)
+
+        @pl.when(p.z < p.chips - 1)
+        def _():
+            self._down(p.z).wait_recv()
+            self._add(p.z, self.down_in)
+
+    def finish(self):
+        p = self.p
+        for z in range(p.chips):
+            self._side(z).wait_send()
+        for k in range(1, p.chips):
+
+            @pl.when(p.z + k < p.chips)
+            def _():
+                self._up(p.z + k).wait_send()
+
+            @pl.when(p.z >= k)
+            def _():
+                self._down(p.z - k).wait_send()
+
+
+def swap_halves(values):
+    lane = lax.broadcasted_iota(jnp.int32, values.shape, 1)
+    return jnp.where(
+        lane % HD < HD // 2,
+        pltpu.roll(values, values.shape[1] - HD // 2, 1),
+        pltpu.roll(values, HD // 2, 1),
+    )
+
+
+def mask_bias(seg_col, seg_row, start, size):
+    length = start + size
+    key_pos = lax.broadcasted_iota(jnp.int32, (length, size), 0)
+    query_pos = start + lax.broadcasted_iota(jnp.int32, (length, size), 1)
+    same = seg_col[pl.ds(0, length), 0:1] == seg_row[0:1, pl.ds(start, size)]
+    return jnp.where((key_pos <= query_pos) & same, 0.0, -1e30).astype(F32)
+
+
 PIECES = 4
-
-
-def gather_kernel(
+QB = 256
+
+
+def front_kernel(
     seq_size,
     hidden,
     cotangent,
@@ -334,14 +468,29 @@
     gate_w,
     up_w,
     down_w,
+    gain,
+    qkv_in,
+    low_map,
+    cos_n,
+    sin_n,
     hidden_all,
     cotangent_all,
-    documents_all,
     adapters_all,
     qkv_all,
     out_all,
     gu_all,
     down_all,
+    attn_all,
+    norm_all,
+    query,
+    keys2,
+    values2,
+    keys_t,
+    log_totals,
+    seg_row,
+    seg_col,
+    low_t,
+    documents_all,
     chain_sems,
     plane_sems,
     local_sems,
@@ -349,18 +498,24 @@
     small_sems,
     side_sems,
     hidden_v,
+    norm_v,
     cotangent_v,
     out_v,
     down_v,
     qkv_v,
     gu_v,
+    weights_v,
+    key_z,
+    values_t,
+    bias,
+    attn_v,
 ):
     p = Place(seq_size)
     d, s, z, c = p.d, p.s, p.z, p.c
     rows = query_w.shape[0]
     part = down_w.shape[0]
+    tokens = hidden.shape[0]
     half_rows = seq_size * rows // 2
-
     landing = pl.ds(pl.multiple_of(rows * s, rows), rows)
     q_width = query_w.shape[1] // seq_size
 
@@ -368,12 +523,14 @@
         return pl.ds(pl.multiple_of(number * size, size), size)
 
     stage = [
-        (hidden, hidden_v),
+        (hidden, hidden_v.at[s]),
         (cotangent, cotangent_v),
         (out_w, out_v),
         (down_w, down_v),
         (query_w.at[:, column_block(s, q_width)], qkv_v.at[:, pl.ds(0, q_width)]),
         (kv_w.at[s], qkv_v.at[:, pl.ds(q_width, kv_w.shape[2])]),
+        (documents, documents_all.at[s]),
+        (adapter_row, adapters_all.at[d]),
     ]
     for i in range(8):
         matrix = (gate_w, up_w)[i // 4]
@@ -386,14 +543,15 @@
         pltpu.make_async_copy(src, dst, local_sems.at[1, i])
         for i, (src, dst) in enumerate(
             (
-                (hidden_v, hidden_all.at[s]),
                 (cotangent_v, cotangent_all.at[s]),
                 (out_v, out_all.at[d, z, c]),
                 (down_v, down_all.at[d]),
                 (qkv_v, qkv_all.at[d, landing]),
                 (gu_v, gu_all.at[d, landing]),
-                (documents, documents_all.at[s]),
-                (adapter_row, adapters_all.at[d]),
+                (qkv_all, weights_v),
+                (hidden_v, hidden_all),
+                (norm_v, norm_all),
+                (attn_v, attn_all.at[s]),
             )
         )
     ]
@@ -401,16 +559,15 @@
         copy.start()
     p.greet(range(1, seq_size), (p.dx, p.dy, p.dd))
 
-    hid = Chain(p, hidden, lambda i: hidden_all.at[i], chain_sems.at[0])
+    hid = Chain(p, hidden, lambda i: hidden_v.at[i], chain_sems.at[0])
     cot = Chain(p, cotangent, lambda i: cotangent_all.at[i], chain_sems.at[1])
     out = Chain(p, out_w, lambda i: out_all.at[d, i // 2, i % 2], chain_sems.at[2])
+    att = Chain(p, attn_v, lambda i: attn_all.at[i], chain_sems.at[3])
 
     def qkv_pairs(j):
-        width = query_w.shape[1] // seq_size
-        columns = pl.ds(pl.multiple_of(width * j, width), width)
         return (
-            (query_w.at[:, columns], qkv_all.at[d, landing, pl.ds(0, width)]),
-            (kv_w.at[j], qkv_all.at[d, landing, pl.ds(width, kv_w.shape[2])]),
+            (query_w.at[:, column_block(j, q_width)], qkv_all.at[d, landing, pl.ds(0, q_width)]),
+            (kv_w.at[j], qkv_all.at[d, landing, pl.ds(q_width, kv_w.shape[2])]),
         )
 
     def gu_pairs(piece):
@@ -419,9 +576,9 @@
         def pairs(j):
             found = []
             for block in (2 * (piece % 2), 2 * (piece % 2) + 1):
-                columns = pl.ds(pl.multiple_of(part * (seq_size * block + j), part), part)
                 at = part * (4 * (piece // 2) + block)
-                found.append((matrix.at[:, columns], gu_all.at[d, landing, pl.ds(at, part)]))
+                source = matrix.at[:, column_block(seq_size * block + j, part)]
+                found.append((source, gu_all.at[d, landing, pl.ds(at, part)]))
             return found
 
         return pairs
@@ -436,7 +593,8 @@
         cut = pl.ds(2 * part * i, 2 * part)
         gu.append(
             Spread(
-                p, gu_pairs(i), [gu_all.at[d, others, cut]], spread_sems.at[1 + i, 0], spread_sems.at[1 + i, 1],
+                p, gu_pairs(i), [gu_all.at[d, others, cut]], spread_sems.at[1 + i, 0],
+                spread_sems.at[1 + i, 1],
             )
         )
         gu_planes.append(
@@ -455,7 +613,7 @@
     )
     down = Plane(
         p,
-        lambda e: down_w if e is d else down_all.at[e],
+        lambda e: down_all.at[e],
         lambda e, h: down_all.at[e, pl.ds(part // 2 * h, part // 2)],
         plane_sems.at[1],
     )
@@ -469,7 +627,8 @@
 
     def documents_copy(step):
         return remote(
-            documents, documents_all.at[s], small_sems.at[0, step], small_sems.at[1, 0], p.seq(p.peer(step))
+            documents, documents_all.at[s], small_sems.at[0, step], small_sems.at[1, 0],
+            p.seq(p.peer(step)),
         )
 
     def adapters_copy(i, e):
@@ -484,6 +643,75 @@
     def side_wait(i, e):
         ref = out_all.at[e, :, 1 - c]
         remote(ref, ref, side_sems.at[0, i], side_sems.at[1, i], p.seq(p.sib)).wait_recv()
+
+    low_lane = lax.broadcasted_iota(jnp.int32, (tokens, 2 * HD), 1) < HD
+    weights = weights_v.reshape(4 * seq_size * rows, qkv_v.shape[1])
+
+    def process(slot):
+        at = pl.ds(pl.multiple_of(slot * tokens, tokens), tokens)
+        cos_part, sin_part = cos_n[at, :], sin_n[at, :]
+        normed = rms_scale(hidden_v[slot].astype(F32), gain[...]).astype(BF16)
+        norm_v[slot] = normed
+        low = dot_nn(normed, qkv_in[...]).astype(BF16)
+        pre = dot_nn(normed, weights[...]) + dot_nn(low, low_map[...])
+        padded = jnp.concatenate(
+            [low.astype(F32), jnp.zeros((tokens, 128 - low.shape[1]), F32)], axis=1
+        )
+        low_t[:, at] = padded.T[: low.shape[1]].astype(BF16)
+        for m in range(2):
+            pair = pre[:, 2 * HD * m : 2 * HD * (m + 1)]
+            turned = pair * cos_part + swap_halves(pair) * sin_part
+            query[at, pl.ds(2 * HD * m, 2 * HD)] = turned.astype(BF16)
+        pair = pre[:, 4 * HD :]
+        turned = pair * cos_part + swap_halves(pair) * sin_part
+        both = jnp.where(low_lane, turned, pair)
+        crossed = pltpu.roll(both, HD, 1)
+        keys2[at, :] = jnp.where(low_lane, both, crossed).astype(BF16)
+        values2[at, :] = jnp.where(low_lane, crossed, both).astype(BF16)
+        zero = jnp.zeros_like(both)
+        key_z[0, at, :] = jnp.where(low_lane, both, zero).astype(BF16)
+        key_z[1, at, :] = jnp.where(low_lane, zero, crossed).astype(BF16)
+        both_t = both.T
+        keys_t[:, at] = both_t[:HD].astype(BF16)
+        values_t[:, at] = both_t[HD:].astype(BF16)
+
+    def process_distance(k):
+        @pl.when(p.z >= k)
+        def _():
+            hid.side_recv(p.z - k)
+
+            @pl.loop(0, 2)
+            def _(core):
+                process(2 * (p.z - k) + core)
+
+        if k:
+
+            @pl.when(p.z + k < p.chips)
+            def _():
+                hid.side_recv(p.z + k)
+
+                @pl.loop(0, 2)
+                def _(core):
+                    process(2 * (p.z + k) + core)
+
+    def query_block(i):
+        start = i * QB
+        span = pl.ds(0, start + QB)
+        at = pl.ds(start, QB)
+        bias[span, :] = mask_bias(seg_col, seg_row, start, QB)
+
+        for m in range(2):
+            pair = pl.ds(2 * HD * m, 2 * HD)
+            query_pair = query[at, pair]
+            found = []
+            for e in range(2):
+                scores = dot_nt(key_z[e, span, :], query_pair) * SCORE_SCALE + bias[span, :]
+                top = jnp.max(scores, axis=0, keepdims=True)
+                raised = jnp.exp(scores - top)
+                total = jnp.sum(raised, axis=0, keepdims=True)
+                found.append(dot_nn(values_t[:, span], raised.astype(BF16)) / total)
+                log_totals[2 * m + e : 2 * m + e + 1, at] = top + jnp.log(total)
+            attn_v[at, pair] = jnp.concatenate(found, axis=0).T.astype(BF16)
 
     for step in range(1, seq_size):
         documents_copy(step).start()
@@ -491,68 +719,87 @@
         adapters_copy(i, e).start()
     qkv.start()
     hid.start()
-    for i, e in enumerate((p.dx, p.dy)):
-        remote(
-            down_w, down_all.at[d], down.sems.at[0, i], down.sems.at[1, i], p.dp(e)
-        ).start()
     for copy in stage:
         copy.wait()
-    for copy in keep:
-        copy.start()
-    for copy in keep:
-        copy.wait()
+    for i in range(5):
+        keep[i].start()
+    for i in range(5):
+        keep[i].wait()
     qkv.recv()
     qkv_plane.start()
     hid.step(1)
     gu[0].start()
-    down.forward()
+    remote(
+        documents_all.at[pl.ds(0, seq_size - 1)], documents_all.at[pl.ds(0, seq_size - 1)],
+        small_sems.at[0, 0], small_sems.at[1, 0], p.seq(p.sib),
+    ).wait_recv()
+    for slot in range(seq_size):
+        at = pl.ds(tokens * slot, tokens)
+        numbers = documents_all[slot].astype(F32)
+        seg_row[:, at] = numbers
+        seg_col[at, :] = jnp.broadcast_to(numbers[0:1, :], (tokens, tokens)).T
     qkv_plane.forward()
     hid.step(2)
     gu[1].start()
     gu[0].recv()
     gu_planes[0].start()
+    qkv_plane.recv()
+    keep[5].start()
+    keep[5].wait()
+    process_distance(0)
+    process_distance(1)
     hid.step(3)
     gu[2].start()
-    qkv_plane.recv()
     out.start()
     gu[1].recv()
     gu_planes[1].start()
     gu_planes[0].forward()
+    process_distance(2)
+    process_distance(3)
     gu[3].start()
     out.step(1)
+    keep[6].start()
+    keep[7].start()
+    query_block(0)
+    query_block(1)
     gu[2].recv()
     gu_planes[2].start()
     gu_planes[1].forward()
     out.step(2)
-    cot.start()
+    query_block(2)
+    query_block(3)
+    keep[8].start()
+    att.start()
     gu[3].recv()
     gu_planes[3].start()
     gu_planes[2].forward()
     out.step(3)
     out_plane.start()
-    cot.step(1)
+    att.step(1)
+    cot.start()
+    down.start()
     gu_planes[3].forward()
-    cot.step(2)
+    att.step(2)
     out_plane.forward()
     side_copy(0, p.dx).start()
     side_copy(1, p.dy).start()
-    cot.step(3)
+    cot.step(1)
+    att.step(3)
+    cot.step(2)
+    down.forward()
     out_plane.recv()
     side_copy(2, p.dd).start()
+    cot.step(3)
     for i in range(4):
         gu_planes[i].recv()
     down.recv()
-    for chain in (hid, out, cot):
+    for chain in (out, att, cot):
         for other in range(p.chips):
             chain.side_recv(other)
+    for chain in (hid, out, att, cot):
         chain.finish()
-    side_wait(0, p.dx)
-    side_wait(1, p.dy)
-    side_wait(2, p.dd)
-    remote(
-        documents_all.at[pl.ds(0, seq_size - 1)], documents_all.at[pl.ds(0, seq_size - 1)],
-        small_sems.at[0, 0], small_sems.at[1, 0], p.seq(p.sib),
-    ).wait_recv()
+    for i, e in enumerate((p.dx, p.dy, p.dd)):
+        side_wait(i, e)
     remote(
         adapters_all.at[pl.ds(0, 3)], adapters_all.at[pl.ds(0, 3)],
         small_sems.at[2, 3], small_sems.at[3, 0], p.dp(p.dx),
@@ -564,181 +811,78 @@
         side_copy(i, e).wait_send()
     for group in [qkv, *gu, qkv_plane, down, out_plane, *gu_planes]:
         group.finish()
-
-
-def gather_all(
-    seq_size, hidden, cotangent, documents, adapter_row, query_w, kv_w, out_w, gate_w, up_w, down_w
-):
-    tokens, width = hidden.shape
-    rows = query_w.shape[0]
-    part = down_w.shape[0]
+    for i in (6, 7, 8):
+        keep[i].wait()
+
+
+def front_all(seq_size, ins):
+    tokens, width = ins[0].shape
+    rows = ins[4].shape[0]
+    part = ins[9].shape[0]
     chips = seq_size // 2
-    qkv_width = query_w.shape[1] // seq_size + kv_w.shape[2]
+    q_width = ins[4].shape[1] // seq_size
+    qkv_width = q_width + ins[5].shape[2]
+    length = tokens * seq_size
+    low_width = ins[11].shape[1]
 
     def shape(*dims, dtype=BF16):
         return jax.ShapeDtypeStruct(dims, dtype)
 
     anywhere = pl.BlockSpec(memory_space=pl.ANY)
+    vmem = pl.BlockSpec(memory_space=pltpu.VMEM)
+    outs = (
+        shape(seq_size, tokens, width),
+        shape(seq_size, tokens, width),
+        shape(4, 8, 128, dtype=jnp.int32),
+        shape(4, seq_size * rows, qkv_width),
+        shape(4, chips, 2, rows, width),
+        shape(4, seq_size * rows, 8 * part),
+        shape(4, part, width),
+        shape(seq_size, length, q_width),
+        shape(seq_size, tokens, width),
+        shape(length, q_width),
+        shape(length, 2 * HD),
+        shape(length, 2 * HD),
+        shape(HD, length),
+        shape(4, length, dtype=F32),
+        shape(8, length, dtype=F32),
+        shape(length, tokens, dtype=F32),
+        shape(low_width, length),
+    )
     return pl.pallas_call(
-        functools.partial(gather_kernel, seq_size),
-        out_shape=(
-            shape(seq_size, tokens, width),
-            shape(seq_size, tokens, width),
-            shape(seq_size, 8, tokens, dtype=jnp.int32),
-            shape(4, 8, 128, dtype=jnp.int32),
-            shape(4, seq_size * rows, qkv_width),
-            shape(4, chips, 2, rows, width),
-            shape(4, seq_size * rows, 8 * part),
-            shape(4, part, width),
-        ),
-        in_specs=[anywhere] * 10,
-        out_specs=(anywhere,) * 8,
+        functools.partial(front_kernel, seq_size),
+        out_shape=outs,
+        in_specs=[anywhere] * 10 + [vmem] * 5,
+        out_specs=(anywhere,) * 9 + (vmem,) * 8,
         scratch_shapes=[
-            pltpu.SemaphoreType.DMA((3, 4, seq_size)),
+            pltpu.VMEM((seq_size, 8, tokens), jnp.int32),
+            pltpu.SemaphoreType.DMA((4, 4, seq_size)),
             pltpu.SemaphoreType.DMA((3 + PIECES, 2, 4)),
-            pltpu.SemaphoreType.DMA((2, 14)),
+            pltpu.SemaphoreType.DMA((2, 16)),
             pltpu.SemaphoreType.DMA((1 + PIECES, 2)),
             pltpu.SemaphoreType.DMA((4, seq_size)),
             pltpu.SemaphoreType.DMA((2, 3)),
-            pltpu.VMEM((tokens, width), BF16),
+            pltpu.VMEM((seq_size, tokens, width), BF16),
+            pltpu.VMEM((seq_size, tokens, width), BF16),
             pltpu.VMEM((tokens, width), BF16),
             pltpu.VMEM((rows, width), BF16),
             pltpu.VMEM((part, width), BF16),
             pltpu.VMEM((rows, qkv_width), BF16),
             pltpu.VMEM((rows, 8 * part), BF16),
+            pltpu.VMEM((4, seq_size * rows, qkv_width), BF16),
+            pltpu.VMEM((2, length, 2 * HD), BF16),
+            pltpu.VMEM((HD, length), BF16),
+            pltpu.VMEM((length, QB), F32),
+            pltpu.VMEM((length, q_width), BF16),
         ],
-        compiler_params=pltpu.CompilerParams(collective_id=0, has_side_effects=True),
-        cost_estimate=pl.CostEstimate(flops=0, bytes_accessed=2 * 30 * 2**20, transcendentals=0),
-        name="gather_all",
-    )(hidden, cotangent, documents, adapter_row, query_w, kv_w, out_w, gate_w, up_w, down_w)
-
-
-def dot_nn(a, b):
-    return lax.dot_general(a, b, (((1,), (0,)), ((), ())), preferred_element_type=F32)
-
-
-def dot_nt(a, b):
-    return lax.dot_general(a, b, (((1,), (1,)), ((), ())), preferred_element_type=F32)
-
-
-class ChainSum:
-    def __init__(self, place, part, side_in, up_in, down_in, sems):
-        self.p, self.part = place, part
-        self.side_in, self.up_in, self.down_in = side_in, up_in, down_in
-        self.sems = sems
-
-    def _side(self, z):
-        p = self.p
-        return remote(
-            self.part.at[2 * z + 1 - p.c], self.side_in.at[z],
-            self.sems.at[0, z], self.sems.at[1, z], p.seq(p.sib),
-        )
-
-    def _up(self, z):
-        p = self.p
-        return remote(
-            self.part.at[2 * z + p.c], self.up_in.at[z],
-            self.sems.at[2, z], self.sems.at[3, z], p.seq(p.s + 2),
-        )
-
-    def _down(self, z):
-        p = self.p
-        return remote(
-            self.part.at[2 * z + p.c], self.down_in.at[z],
-            self.sems.at[4, z], self.sems.at[5, z], p.seq(p.s - 2),
-        )
-
-    def _add(self, z, incoming):
-        slot = 2 * z + self.p.c
-        rows = self.part.shape[1]
-
-        @pl.loop(0, rows // 16)
-        def _(i):
-            cut = pl.ds(pl.multiple_of(i * 16, 16), 16)
-            total = self.part[slot, cut].astype(F32) + incoming[z, cut].astype(F32)
-            self.part[slot, cut] = total.astype(BF16)
-
-    def side_start(self, z):
-        self._side(z).start()
-
-    def side_add(self, z):
-        self._side(z).wait_recv()
-        self._add(z, self.side_in)
-
-    def step(self, k):
-        p = self.p
-
-        @pl.when(p.z + k < p.chips)
-        def _():
-            to = p.z + k
-            self.side_add(to)
-
-            @pl.when(p.z > 0)
-            def _():
-                self._up(to).wait_recv()
-                self._add(to, self.up_in)
-
-            self._up(to).start()
-
-        @pl.when(p.z >= k)
-        def _():
-            to = p.z - k
-            self.side_add(to)
-
-            @pl.when(p.z < p.chips - 1)
-            def _():
-                self._down(to).wait_recv()
-                self._add(to, self.down_in)
-
-            self._down(to).start()
-
-    def last(self):
-        p = self.p
-        self.side_add(p.z)
-
-        @pl.when(p.z > 0)
-        def _():
-            self._up(p.z).wait_recv()
-            self._add(p.z, self.up_in)
-
-        @pl.when(p.z < p.chips - 1)
-        def _():
-            self._down(p.z).wait_recv()
-            self._add(p.z, self.down_in)
-
-    def finish(self):
-        p = self.p
-        for z in range(p.chips):
-            self._side(z).wait_send()
-        for k in range(1, p.chips):
-
-            @pl.when(p.z + k < p.chips)
-            def _():
-                self._up(p.z + k).wait_send()
-
-            @pl.when(p.z >= k)
-            def _():
-                self._down(p.z - k).wait_send()
-
-
-def swap_halves(values):
-    lane = lax.broadcasted_iota(jnp.int32, values.shape, 1)
-    return jnp.where(
-        lane % HD < HD // 2,
-        pltpu.roll(values, values.shape[1] - HD // 2, 1),
-        pltpu.roll(values, HD // 2, 1),
-    )
-
-
-def mask_bias(seg_col, seg_row, start, size):
-    length = start + size
-    key_pos = lax.broadcasted_iota(jnp.int32, (length, size), 0)
-    query_pos = start + lax.broadcasted_iota(jnp.int32, (length, size), 1)
-    same = seg_col[pl.ds(0, length), 0:1] == seg_row[0:1, pl.ds(start, size)]
-    return jnp.where((key_pos <= query_pos) & same, 0.0, -1e30).astype(F32)
-
-
-QB = 256
+        compiler_params=pltpu.CompilerParams(
+            collective_id=0, has_side_effects=True, vmem_limit_bytes=60 * 2**20
+        ),
+        cost_estimate=pl.CostEstimate(
+            flops=5 * 10**9, bytes_accessed=60 * 2**20, transcendentals=4 * 2**20
+        ),
+        name="attend_front",
+    )(*ins)
 
 
 def back_kernel(
@@ -1169,46 +1313,6 @@
             return columns.reshape(columns.shape[0], dp_size, seq_size, ff_block)
 
         hidden_own = hidden[0].astype(F32)
-        if kernels:
-            kv = jnp.concatenate(
-                [key_weight.reshape(rows, KVH, HD), value_weight.reshape(rows, KVH, HD)], axis=2
-            )
-            gathered = gather_all(
-                seq_size,
-                hidden[0],
-                cotangent[0],
-                jnp.broadcast_to(token_document_numbers, (8, tokens)),
-                jnp.broadcast_to(sequence_adapter_index[:, None], (8, 128)),
-                query_weight,
-                jnp.swapaxes(kv, 0, 1),
-                attention_output_weight,
-                gate_weight,
-                up_weight,
-                down_weight,
-            )
-            hidden_all = gathered[0].reshape(length, width)
-            cotangent_all = gathered[1].reshape(length, width)
-            segments = gathered[2][:, 0].reshape(length)
-            owners = gathered[3][:, 0, 0]
-            qkv = gathered[4].reshape(width, -1)
-            out_full = gathered[5].reshape(width, width)
-            gate_up = gathered[6].reshape(width, -1)
-            down = gathered[7].reshape(dp_size * ff_block, width)
-        else:
-            hidden_all = gather_seq(hidden[0])
-            segments = gather_seq(token_document_numbers[0])
-            kv = jnp.stack([key_weight.reshape(rows, KVH, HD), value_weight.reshape(rows, KVH, HD)], 2)
-            kv = jnp.repeat(kv.reshape(rows, KVH, 2 * HD), kv_repeat, axis=1)
-            qkv = jnp.concatenate([query_weight.reshape(rows, seq_size, q_width), kv], axis=2)
-            qkv = across(jnp.swapaxes(qkv, 0, 1)).reshape(seq_size * rows, q_width + 2 * HD)
-            qkv = gather_dp(qkv)
-            gate_up = jnp.concatenate([by_owner(gate_weight), by_owner(up_weight)], axis=1)
-            gate_up = across(jnp.transpose(gate_up, (2, 0, 1, 3)))
-            gate_up = gather_dp(gate_up.reshape(seq_size * rows, 2 * dp_size * ff_block))
-            down = gather_dp(down_weight)
-            out_full = lax.all_gather(attention_output_weight, ("dp", "seq"), axis=0, tiled=True)
-            cotangent_all = gather_seq(cotangent[0])
-            owners = lax.all_gather(sequence_adapter_index, "dp", axis=0, tiled=True)
         ff_own = dp_size * ff_block
 
         adapter = sequence_adapter_index[0]
@@ -1228,18 +1332,95 @@
         down_in = lax.dynamic_index_in_dim(down_all, me, 1, keepdims=False).reshape(ff_own, rank)
         down_out = adapter_down_output[adapter]
 
-        norm_one = rms_scale(hidden_all.astype(F32), attention_norm_gain).astype(BF16)
-        low_qkv = mm(norm_one, qkv_in).astype(BF16)
-        pre = mm(norm_one, qkv)
-        query_pre = pre[:, :q_width] + mm(low_qkv[:, :rank], q_out)
-        key_pre = pre[:, q_width : q_width + HD] + mm(low_qkv[:, rank : 2 * rank], k_out)
-        value_pre = pre[:, q_width + HD :] + mm(low_qkv[:, 2 * rank :], v_out)
-        cos_table, sin_table = angle_tables(jnp.arange(length, dtype=jnp.int32).astype(F32), HD)
-        query = rotate(query_pre.reshape(length, heads, HD), cos_table, sin_table).astype(BF16)
-        keys = rotate(key_pre.reshape(length, 1, HD), cos_table, sin_table).astype(BF16)[:, 0]
-        values = value_pre.astype(BF16)
-        attn_heads, log_totals = attend_forward(query, keys, values, segments)
-        attn = lax.all_gather(attn_heads, "seq", axis=1, tiled=True)
+        if kernels:
+            kv = jnp.concatenate(
+                [key_weight.reshape(rows, KVH, HD), value_weight.reshape(rows, KVH, HD)], axis=2
+            )
+            none_q = jnp.zeros((rank, q_width), BF16)
+            none_h = jnp.zeros((rank, HD), BF16)
+            low_map = jnp.concatenate(
+                [
+                    jnp.concatenate([q_out, none_h, none_h], axis=1),
+                    jnp.concatenate([none_q, k_out, none_h], axis=1),
+                    jnp.concatenate([none_q, none_h, v_out], axis=1),
+                ],
+                axis=0,
+            )
+            cos_fixed, sin_fixed = fixed_tables(length)
+            (
+                hidden_all,
+                cotangent_all,
+                owners,
+                qkv,
+                out_full,
+                gate_up,
+                down,
+                attn,
+                norm_one,
+                query,
+                keys2,
+                values2,
+                keys_t,
+                log_totals,
+                seg_row,
+                seg_col,
+                low_t,
+            ) = front_all(
+                seq_size,
+                (
+                    hidden[0],
+                    cotangent[0],
+                    jnp.broadcast_to(token_document_numbers, (8, tokens)),
+                    jnp.broadcast_to(sequence_adapter_index[:, None], (8, 128)),
+                    query_weight,
+                    jnp.swapaxes(kv, 0, 1),
+                    attention_output_weight,
+                    gate_weight,
+                    up_weight,
+                    down_weight,
+                    attention_norm_gain[None],
+                    qkv_in,
+                    low_map,
+                    jnp.asarray(np.tile(cos_fixed, (1, 4))),
+                    jnp.asarray(np.tile(np.concatenate([-sin_fixed, sin_fixed], axis=1), (1, 2))),
+                ),
+            )
+            hidden_all = hidden_all.reshape(length, width)
+            cotangent_all = cotangent_all.reshape(length, width)
+            norm_one = norm_one.reshape(length, width)
+            qkv = qkv.reshape(width, -1)
+            out_full = out_full.reshape(width, width)
+            gate_up = gate_up.reshape(width, -1)
+            down = down.reshape(dp_size * ff_block, width)
+            attn = jnp.swapaxes(attn, 0, 1).reshape(length, width)
+        else:
+            hidden_all = gather_seq(hidden[0])
+            segments = gather_seq(token_document_numbers[0])
+            kv = jnp.stack([key_weight.reshape(rows, KVH, HD), value_weight.reshape(rows, KVH, HD)], 2)
+            kv = jnp.repeat(kv.reshape(rows, KVH, 2 * HD), kv_repeat, axis=1)
+            qkv = jnp.concatenate([query_weight.reshape(rows, seq_size, q_width), kv], axis=2)
+            qkv = across(jnp.swapaxes(qkv, 0, 1)).reshape(seq_size * rows, q_width + 2 * HD)
+            qkv = gather_dp(qkv)
+            gate_up = jnp.concatenate([by_owner(gate_weight), by_owner(up_weight)], axis=1)
+            gate_up = across(jnp.transpose(gate_up, (2, 0, 1, 3)))
+            gate_up = gather_dp(gate_up.reshape(seq_size * rows, 2 * dp_size * ff_block))
+            down = gather_dp(down_weight)
+            out_full = lax.all_gather(attention_output_weight, ("dp", "seq"), axis=0, tiled=True)
+            cotangent_all = gather_seq(cotangent[0])
+            owners = lax.all_gather(sequence_adapter_index, "dp", axis=0, tiled=True)
+        if not kernels:
+            norm_one = rms_scale(hidden_all.astype(F32), attention_norm_gain).astype(BF16)
+            low_qkv = mm(norm_one, qkv_in).astype(BF16)
+            pre = mm(norm_one, qkv)
+            query_pre = pre[:, :q_width] + mm(low_qkv[:, :rank], q_out)
+            key_pre = pre[:, q_width : q_width + HD] + mm(low_qkv[:, rank : 2 * rank], k_out)
+            value_pre = pre[:, q_width + HD :] + mm(low_qkv[:, 2 * rank :], v_out)
+            cos_table, sin_table = angle_tables(jnp.arange(length, dtype=jnp.int32).astype(F32), HD)
+            query = rotate(query_pre.reshape(length, heads, HD), cos_table, sin_table).astype(BF16)
+            keys = rotate(key_pre.reshape(length, 1, HD), cos_table, sin_table).astype(BF16)[:, 0]
+            values = value_pre.astype(BF16)
+            attn_heads, log_totals = attend_forward(query, keys, values, segments)
+            attn = lax.all_gather(attn_heads, "seq", axis=1, tiled=True)
         low_out = mm(attn, o_in).astype(BF16)
         branch = mm(attn, out_full) + mm(low_out, o_out)
         middle = hidden_all.astype(F32) + RESIDUAL_SCALE * branch
@@ -1289,41 +1470,31 @@
             gu_grad = jnp.concatenate(
                 [t_mm(low_gu[:, :rank], grad_gate), t_mm(low_gu[:, rank:], grad_up)], axis=1
             )
-            none_q = jnp.zeros((rank, q_width), BF16)
-            none_h = jnp.zeros((rank, HD), BF16)
-            low_map = jnp.concatenate(
-                [
-                    jnp.concatenate([q_out, none_h, none_h], axis=1),
-                    jnp.concatenate([none_q, k_out, none_h], axis=1),
-                    jnp.concatenate([none_q, none_h, v_out], axis=1),
-                ],
-                axis=0,
-            )
             sums = back_all(
                 seq_size,
                 (
                     jnp.swapaxes(grad_attn.reshape(tokens, seq_size, q_width), 0, 1),
-                    query.reshape(length, q_width),
-                    jnp.concatenate([keys, keys], axis=1),
-                    jnp.concatenate([values, values], axis=1),
-                    keys.T,
-                    jnp.swapaxes(log_totals, 0, 1).reshape(heads, length),
-                    segments[None],
-                    jnp.broadcast_to(segments[:, None], (length, 128)),
-                    cos_table.T,
-                    sin_table.T,
-                    jnp.tile(cos_table, (1, 4)),
-                    jnp.tile(jnp.concatenate([-sin_table, sin_table], axis=1), (1, 2)),
+                    query,
+                    keys2,
+                    values2,
+                    keys_t,
+                    log_totals,
+                    seg_row,
+                    seg_col,
+                    jnp.asarray(np.ascontiguousarray(cos_fixed.T)),
+                    jnp.asarray(np.ascontiguousarray(sin_fixed.T)),
+                    jnp.asarray(np.tile(cos_fixed, (1, 4))),
+                    jnp.asarray(np.tile(np.concatenate([-sin_fixed, sin_fixed], axis=1), (1, 2))),
                     qkv,
                     qkv_in,
                     low_map,
-                    low_qkv.T,
+                    low_t,
                     norm_one,
                     ffn_part.reshape(seq_size, tokens, width),
                     early,
                     gu_grad,
                     t_mm(grad_low_down, activation),
-                    gathered[3],
+                    owners,
                 ),
             )
             norm_sum, ffn_sum, share, gu_got, down_got, q_got, kv_got = sums

time: 564 us -> 511 us (0.906)
  Pallas kernels: 275 us -> 311 us
  other arithmetic: 48.2 us -> 18.9 us
  matrix products: 114 us -> 86.4 us
  waiting for transfers between devices: 54.1 us -> 34 us
  local copies, waits for them, and re-layouts: 46.6 us -> 37.2 us
    all_gather x1 -> x0, waiting for transfers between devices: 39.6 us -> none  [local(): attn = lax.all_gather(attn_heads, 'seq', axis=1, tiled=True)]
    pallas_call x1, Pallas kernels: 161 us -> 197 us  [front_all(): pl.pallas_call(functools.partial(front_kernel, seq_size), out_shape=outs,...]
    reduce_scatter x1, waiting for transfers between devices: 14.4 us -> 33.9 us  [scatter_seq(): return lax.psum_scatter(total, 'seq', scatter_dimension=0, tiled=True)]
    dot_general x15 -> x10, matrix products: 57.6 us -> 41.9 us  [mm(): return jnp.dot(a, b, preferred_element_type=F32)]
    reduce_sum x3 -> x0, other arithmetic: 12.6 us -> none  [the longest x1 7.66 us: rms_scale(): mean_square = jnp.mean(values * values, axis=-1, keepdims=True)]
    dot_general x4 -> x0, matrix products: 11.2 us -> none  [the longest x2 6.15 us: one_block(): output = jnp.einsum('hqk,kd->qhd', low, values, preferred_element_type=F32)]
    transpose x0 -> x1, local copies, waits for them, and re-layouts: none -> 6.46 us  [local(): attn = jnp.swapaxes(attn, 0, 1).reshape(length, width)]
    unnamed x130 -> x66, local copies, waits for them, and re-layouts: 19.9 us -> 17.6 us
  transfers between devices with their start and end apart: 2 -> 1, of which waited for: 2 -> 1; matrix products, arithmetic and copies ran while one was open for 8% -> 3% of each run, Pallas kernels for 0% -> 0%
where the time goes in v4:
time: 511 us; the launch traced here: 503 us
  Pallas kernels  311 us (61%)
  matrix products  86.4 us (17%)
  local copies, waits for them, and re-layouts  37.2 us (7%)
  waiting for transfers between devices  34 us (7%)
  other arithmetic  18.9 us (4%)
  between operations  15.6 us (3%)
    pallas_call x1, Pallas kernels, front_all(): pl.pallas_call(functools.partial(front_kernel, seq_size), out_shape=outs,...  197 us
    pallas_call x1, Pallas kernels, back_all(): pl.pallas_call(functools.partial(back_kernel, seq_size), out_shape=outs,...  114 us
    dot_general x10, matrix products, mm(): return jnp.dot(a, b, preferred_element_type=F32)  41.9 us
    reduce_scatter x1, waiting for transfers between devices, scatter_seq(): return lax.psum_scatter(total, 'seq', scatter_dimension=0, tiled=True)  33.9 us
    dot_general x10, matrix products, mm_t(): lax.dot_general(a, b, (((1,), (1,)), ((), ())), preferred_element_type=F32)  33.4 us
    unnamed x66, local copies, waits for them, and re-layouts  17.6 us
    dot_general x7, matrix products, t_mm(): lax.dot_general(a, b, (((0,), (0,)), ((), ())), preferred_element_type=F32)  11.1 us
  transfers between devices with their start and end apart: 1, of which 1 were waited for; matrix products, arithmetic and copies ran while one was open for 3% of the time, Pallas kernels for 0%

profile of v4, /device:TPU:8, one launch (start us, length us, event | category | flops | bytes accessed | tf_op | source)
XLA Modules:
  0.0 503.3 jit_solution(7808500298241176553)
XLA Ops:
  8.0 1.0 reshape.116
  9.1 1.0 reshape.117
  10.1 0.9 constant_dynamic-slice_fusion.3
  11.0 1.0 constant_dynamic-slice_fusion.2
  12.3 1.0 copy.66
  13.8 0.8 maximum_bitcast_fusion.kv_w
  14.5 0.8 dynamic-slice_bitcast_fusion
  15.3 0.8 dynamic-slice_bitcast_fusion.2
  16.1 0.7 fusion.34.low_map
  17.4 0.6 broadcast_in_dim.19.documents
  18.0 197.0 %attend_front.1 = (bf16[8,128,2048]{2,1,0:T(8,128)(2,1)}, bf16[8,128,2048]{2,1,0:T(8,128)(2,1)}, s32[4,8,128]{2,1,0:T(8,128)}, bf16[4,512,384]{2,1,0:T(8,128)(2,...) custom-call(bf16[128,2048]{1,0:T(8,128)(2,1)} %bitcast.142, ...), custom_call_target="tpu_custom_call" | custom-call | flops 5000000000 | bytes 62914560 | tf_op jit(solution)/shard_map/attend_front/pallas_call | solution.py:852
  215.0 6.5 %copy.67 = bf16[1024,8,256]{0,2,1:T(8,128)(2,1)} copy(bf16[1024,8,256]{2,0,1:T(8,128)(2,1)} %bitcast.139) | data formatting | bytes 8388608 | tf_op jit(solution)/shard_map/transpose | solution.py:1395
  221.5 3.4 multiply_convert_fusion.1
  224.9 1.2 convolution_convert_fusion.5
  226.1 2.5 copy-done.22
  228.6 6.5 %fusion.60 = f32[1024,1024]{0,1:T(8,128)} fusion(bf16[1024,2048]{1,0:T(8,128)(2,1)S(1)} %bitcast.128, bf16[1024,2048]{1,0:T(8,128)(2,1)S(1)} %bitcast.168), kind=kOutput, calls=%fused_computation.113 | convolution fusion | flops 4294967296 | bytes 12582912 | tf_op jit(solution)/shard_map/dot_general | solution.py:29
  235.1 1.5 convolution_convert_fusion.4
  236.6 9.4 %fusion.59 = f32[1024,2048]{1,0:T(8,128)S(1)} fusion(bf16[1024,2048]{0,1:T(8,128)(2,1)S(1)} %bitcast.132, bf16[2048,2048]{1,0:T(8,128)(2,1)S(1)} %bitcast.136), kind=kOutput, calls=%fused_computation.112 | convolution fusion | flops 8589934592 | bytes 20971520 | tf_op jit(solution)/shard_map/dot_general | solution.py:25
  246.0 4.0 multiply_reduce_fusion
  250.1 0.8 multiply_convert_fusion
  250.9 2.4 copy-done.2
  253.3 1.3 convolution_convert_fusion
  254.7 13.9 %fusion.61 = f32[1024,2048]{0,1:T(8,128)} fusion(bf16[1024,2048]{1,0:T(8,128)(2,1)S(1)} %multiply_convert_fusion, bf16[2048,2048]{1,0:T(8,128)(2,1)} %bitcast.165), kind=kOutput, calls=%fused_computation.114 | convolution fusion | flops 8589934592 | bytes 20971520 | tf_op jit(solution)/shard_map/dot_general | solution.py:25
  268.5 0.8 convolution_add_fusion.1
  269.3 2.6 copy-done.12
  271.9 0.8 slice_add_fusion
  272.7 2.8 multiply_convert_fusion.2
  276.2 12.4 %fusion = f32[1024,2048]{1,0:T(8,128)S(1)} fusion(bf16[2048,2048]{1,0:T(8,128)(2,1)} %bitcast.166, bf16[1024,1024]{0,1:T(8,128)(2,1)S(1)} %get-tuple-element.98, bf16[1024,1024]{0,1:T(8,128)(2,1)S(1)} %get-tuple-element.97), kind=kOutput, calls=%fused_computation.8 | convolution fusion | flops 8598323200 | bytes 20971520 | tf_op jit(solution)/shard_map/dot_general | solution.py:29
  288.7 3.2 add_convert_fusion.1
  292.0 2.4 fusion.35
  294.3 2.2 fusion.38
  296.6 0.7 pad_maximum_fusion.1.gu_grad
  297.7 1.3 fusion.64.down_grad
  299.0 0.7 fusion.63
  299.6 0.8 fusion.32
  300.5 0.8 copy-done.23
  301.3 4.7 fusion.62
  306.0 3.3 add_convert_fusion
  309.2 33.9 %reduce-scatter.2.cloned.1.call-done = bf16[128,2048]{1,0:T(8,128)(2,1)} async-done(((bf16[1024,2048]{1,0:T(8,128)(2,1)}), bf16[128,2048]{1,0:T(8,128)(2,1)}) %reduce-scatter.2.cloned.1.call-update) | async-done | bytes 524304 | tf_op jit(solution)/shard_map/reduce_scatter | solution.py:1310
  343.2 1.6 multiply_reduce_fusion.2
  344.8 1.7 subtract_add_fusion
  346.6 6.3 %fusion.56 = f32[128,2048]{1,0:T(8,128)S(1)} fusion(bf16[2048,2048]{1,0:T(8,128)(2,1)} %bitcast.133, f32[128,2048]{1,0:T(8,128)S(1)} %subtract_add_fusion), kind=kOutput, calls=%fused_computation.109 | convolution fusion | flops 1074266112 | bytes 10485760 | tf_op jit(solution)/shard_map/dot_general | solution.py:29
  352.9 1.1 convolution_convert_fusion.6
  353.9 1.5 fusion.41
  355.5 2.1 fusion.13
  357.6 1.2 fusion.4
  359.0 1.0 copy.74
  360.0 1.8 pad_maximum_fusion.early_t
  361.9 114.2 %attend_back.1 = (f32[128,2048]{1,0:T(8,128)}, f32[128,2048]{1,0:T(8,128)}, f32[4,64,128]{2,1,0:T(8,128)}, f32[4,16,512]{2,1,0:T(8,128)}, f32[4,16,256]{2,1,0:T(...) custom-call(bf16[8,128,256]{2,1,0:T(8,128)(2,1)} %bitcast.149, bf16[1024,256]{1,0:T(8,128)(2,1)} %get-tuple-element.41.query, ...), custom_call_target="tpu_custom_call" | custom-call | flops 10000000000 | bytes 20971520 | tf_op jit(solution)/shard_map/attend_back/pallas_call | solution.py:1211
  476.1 1.7 slice.56
  477.9 1.0 slice.54
  478.9 2.6 fusion.11
  481.5 1.5 fusion.5
  483.6 0.7 copy.77
  484.3 0.7 copy.75
  485.1 0.9 slice_bitcast_fusion
  486.0 0.7 copy.76
  486.7 1.6 copy.80
  488.3 0.7 copy.78
  489.2 0.7 copy.81
  489.9 0.7 copy.79
  490.6 2.6 fusion.12
  493.2 1.6 copy.93
  494.8 1.5 copy.94
  (78 shorter events, 3.7 us)
Async XLA Ops:
  7.2 6.1 %copy-start = (bf16[4,16,16384]{2,1,0:T(8,128)(2,1)S(1)}, bf16[4,16,16384]{2,1,0:T(8,128)(2,1)}, u32[]{:S(2)}) copy-start(bf16[4,16,16384]{2,1,0:T(8,128)(2,1)} %param.47) | copy-start | bytes 6291460
  7.2 10.2 %copy-start.21 = (s32[1,128]{1,0:T(1,128)S(1)}, s32[1,128]{1,0:T(1,128)}, u32[]{:S(2)}) copy-start(s32[1,128]{1,0:T(1,128)} %param.29) | copy-start | bytes 1540
  7.2 336.0 %reduce-scatter.2.cloned.1.call-start = ((), (), s32[]{:S(2)}) async-start(), calls=%async_computation.1 | async-start | bytes 4718592 | tf_op jit(solution)/shard_map/reduce_scatter | solution.py:1310
  221.5 3.4 copy-start.19
  224.8 10.2 %copy-start.5 = (bf16[8,128,2048]{2,1,0:T(8,128)(2,1)}, bf16[8,128,2048]{2,1,0:T(8,128)(2,1)S(1)}, u32[]{:S(2)}) copy-start(bf16[8,128,2048]{2,1,0:T(8,128)(2,1)S(1)} %multiply_convert_fusion.1) | copy-start | bytes 12582916
  224.8 3.7 copy-start.22
  224.9 11.7 %slice-start = ((s8[8388608]{0:T(1024)(128)(4,1)}), s8[4194304]{0:T(1024)(128)(4,1)S(1)}, s32[]{:S(2)}) async-start(s8[8388608]{0:T(1024)(128)(4,1)} %bitcast.134), calls=%async_computation.2 | async-start | bytes 8388608
  228.6 6.5 %copy-start.7 = (bf16[1024,8,256]{0,2,1:T(8,128)(2,1)S(1)}, bf16[1024,8,256]{0,2,1:T(8,128)(2,1)}, u32[]{:S(2)}) copy-start(bf16[1024,8,256]{0,2,1:T(8,128)(2,1)} %copy.67) | copy-start | bytes 12582916
  228.6 8.0 %slice-start.1 = ((s8[8388608]{0:T(1024)(128)(4,1)}), s8[4194304]{0:T(1024)(128)(4,1)S(1)}, s32[]{:S(2)}) async-start(s8[8388608]{0:T(1024)(128)(4,1)} %bitcast.134), calls=%async_computation.3 | async-start | bytes 8388608
  236.6 9.4 %copy-start.16 = (bf16[1024,16]{0,1:T(8,128)(2,1)}, bf16[1024,16]{0,1:T(8,128)(2,1)S(1)}, u32[]{:S(2)}) copy-start(bf16[1024,16]{0,1:T(8,128)(2,1)S(1)} %convolution_convert_fusion.4) | copy-start | bytes 98308
  246.0 4.1 copy-start.18
  250.1 3.2 copy-start.2
  250.1 3.2 copy-start.17
  253.3 15.2 %copy-start.3 = (bf16[1024,2048]{1,0:T(8,128)(2,1)}, bf16[1024,2048]{1,0:T(8,128)(2,1)S(1)}, u32[]{:S(2)}) copy-start(bf16[1024,2048]{1,0:T(8,128)(2,1)S(1)} %multiply_convert_fusion) | copy-start | bytes 12582916
  254.7 13.9 %copy-start.10 = (f32[1024,1024]{0,1:T(8,128)S(1)}, f32[1024,1024]{0,1:T(8,128)}, u32[]{:S(2)}) copy-start(f32[1024,1024]{0,1:T(8,128)} %fusion.60) | copy-start | bytes 12582916
  268.5 3.4 copy-start.12
  275.5 13.2 %copy-start.8 = (bf16[1024,1024]{0,1:T(8,128)(2,1)}, bf16[1024,1024]{0,1:T(8,128)(2,1)S(1)}, u32[]{:S(2)}) copy-start(bf16[1024,1024]{0,1:T(8,128)(2,1)S(1)} %get-tuple-element.98) | copy-start | bytes 6291460
  275.5 13.2 %copy-start.9 = (bf16[1024,1024]{0,1:T(8,128)(2,1)}, bf16[1024,1024]{0,1:T(8,128)(2,1)S(1)}, u32[]{:S(2)}) copy-start(bf16[1024,1024]{0,1:T(8,128)(2,1)S(1)} %get-tuple-element.97) | copy-start | bytes 6291460
  292.0 7.0 %copy-start.6 = (bf16[8,128,2048]{2,1,0:T(8,128)(2,1)S(1)}, bf16[8,128,2048]{2,1,0:T(8,128)(2,1)}, u32[]{:S(2)}) copy-start(bf16[8,128,2048]{2,1,0:T(8,128)(2,1)} %copy-done.5) | copy-start | bytes 12582916
  297.3 2.3 copy-start.4
  299.0 2.3 copy-start.23
  305.9 38.9 %copy-start.14 = (bf16[1,128,2048]{2,1,0:T(8,128)(2,1)S(1)}, bf16[1,128,2048]{2,1,0:T(8,128)(2,1)}, u32[]{:S(2)}) copy-start(bf16[1,128,2048]{2,1,0:T(8,128)(2,1)} %param.31) | copy-start | bytes 1572868
  361.9 119.6 %copy-start.13 = (bf16[1,128,2048]{2,1,0:T(8,128)(2,1)S(1)}, bf16[1,128,2048]{2,1,0:T(8,128)(2,1)}, u32[]{:S(2)}) copy-start(bf16[1,128,2048]{2,1,0:T(8,128)(2,1)} %param.28) | copy-start | bytes 1572868
  361.9 119.6 %copy-start.20 = (f32[2048]{0:T(1024)S(1)}, f32[2048]{0:T(1024)}, u32[]{:S(2)}) copy-start(f32[2048]{0:T(1024)} %param.32) | copy-start | bytes 24580
  476.1 7.4 %copy-start.15 = (f32[4,32,128]{2,1,0:T(8,128)S(1)}, f32[4,32,128]{2,1,0:T(8,128)}, u32[]{:S(2)}) copy-start(f32[4,32,128]{2,1,0:T(8,128)} %get-tuple-element.56) | copy-start | bytes 196612
  476.1 8.2 %copy-start.11 = (f32[4,64,128]{2,1,0:T(8,128)S(1)}, f32[4,64,128]{2,1,0:T(8,128)}, u32[]{:S(2)}) copy-start(f32[4,64,128]{2,1,0:T(8,128)} %get-tuple-element.54) | copy-start | bytes 393220
  478.9 17.4 %copy-start.1 = (bf16[4,16,16384]{2,1,0:T(8,128)(2,1)S(1)}, bf16[4,16,16384]{2,1,0:T(8,128)(2,1)}, u32[]{:S(2)}) copy-start(bf16[4,16,16384]{2,1,0:T(8,128)(2,1)} %param.47) | copy-start | bytes 6291460
Sparse Core Ops, SparseCore 0:
  292.1 51.0 reduce-scatter.1

commit v5 on v3

--- a/solution.py
+++ b/solution.py
@@ -3,6 +3,7 @@
 
 import jax
 import jax.numpy as jnp
+import numpy as np
 from jax import lax
 from jax.experimental import pallas as pl
 from jax.experimental.pallas import tpu as pltpu
@@ -48,6 +49,13 @@
     frequency = jnp.exp(steps * (-2.0 * math.log(ROPE_BASE) / head_size))
     angles = positions[:, None] * frequency[None, :]
     return (jnp.cos(angles), jnp.sin(angles))
+
+
+def fixed_tables(length):
+    steps = np.arange(HD // 2, dtype=np.float32)
+    frequency = np.exp(steps * np.float32(-2.0 * math.log(ROPE_BASE) / HD))
+    angles = np.arange(length, dtype=np.float32)[:, None] * frequency[None, :]
+    return (np.cos(angles), np.sin(angles))
 
 
 def rotate(values, cos_table, sin_table):
@@ -124,6 +132,232 @@
     return (grad_query.reshape(length, heads, head_size), grad_keys * SCORE_SCALE, grad_values)
 
 
+def make_local(dp_size, seq_size):
+    devices = dp_size * seq_size
+    heads = NH // seq_size
+    kv_repeat = max(1, seq_size // KVH)
+
+    def local(
+        hidden,
+        token_document_numbers,
+        sequence_adapter_index,
+        cotangent,
+        attention_norm_gain,
+        feedforward_norm_gain,
+        query_weight,
+        key_weight,
+        value_weight,
+        attention_output_weight,
+        gate_weight,
+        up_weight,
+        down_weight,
+        adapter_query_key_value_input,
+        adapter_query_output,
+        adapter_key_value_output,
+        adapter_projection_input,
+        adapter_projection_output,
+        adapter_gate_up_input,
+        adapter_gate_up_output,
+        adapter_down_input,
+        adapter_down_output,
+    ):
+        tokens, width = hidden.shape[1:]
+        length = tokens * seq_size
+        rows = query_weight.shape[0]
+        key_width = key_weight.shape[1]
+        ff_width = gate_weight.shape[1]
+        ff_block = ff_width // devices
+        rank = adapter_projection_input.shape[2]
+        adapters = adapter_projection_input.shape[0]
+        me = lax.axis_index("seq")
+        q_width = heads * HD
+
+        def across(piece):
+            return lax.all_to_all(piece, "seq", split_axis=0, concat_axis=0, tiled=True)
+
+        def gather_dp(block):
+            return lax.all_gather(block, "dp", axis=0, tiled=True)
+
+        def gather_seq(block):
+            return lax.all_gather(block, "seq", axis=0, tiled=True)
+
+        def scatter_seq(total):
+            return lax.psum_scatter(total, "seq", scatter_dimension=0, tiled=True)
+
+        def by_owner(columns):
+            return columns.reshape(columns.shape[0], dp_size, seq_size, ff_block)
+
+        hidden_own = hidden[0].astype(F32)
+        hidden_all = gather_seq(hidden[0])
+        segments = gather_seq(token_document_numbers[0])
+        kv = jnp.stack([key_weight.reshape(rows, KVH, HD), value_weight.reshape(rows, KVH, HD)], 2)
+        kv = jnp.repeat(kv.reshape(rows, KVH, 2 * HD), kv_repeat, axis=1)
+        qkv = jnp.concatenate([query_weight.reshape(rows, seq_size, q_width), kv], axis=2)
+        qkv = across(jnp.swapaxes(qkv, 0, 1)).reshape(seq_size * rows, q_width + 2 * HD)
+        qkv = gather_dp(qkv)
+        gate_up = jnp.concatenate([by_owner(gate_weight), by_owner(up_weight)], axis=1)
+        gate_up = across(jnp.transpose(gate_up, (2, 0, 1, 3)))
+        gate_up = gather_dp(gate_up.reshape(seq_size * rows, 2 * dp_size * ff_block))
+        down = gather_dp(down_weight)
+        out_full = lax.all_gather(attention_output_weight, ("dp", "seq"), axis=0, tiled=True)
+        ff_own = dp_size * ff_block
+
+        adapter = sequence_adapter_index[0]
+        qkv_in = adapter_query_key_value_input[adapter]
+        q_out = lax.dynamic_slice_in_dim(adapter_query_output[adapter], me * q_width, q_width, 1)
+        kv_out = adapter_key_value_output[adapter]
+        kv_start = (me // kv_repeat) * HD
+        k_out = lax.dynamic_slice_in_dim(kv_out, kv_start, HD, 1)
+        v_out = lax.dynamic_slice_in_dim(kv_out, key_width + kv_start, HD, 1)
+        o_in = adapter_projection_input[adapter]
+        o_out = adapter_projection_output[adapter]
+        gu_in = adapter_gate_up_input[adapter]
+        gu_all = adapter_gate_up_output[adapter].reshape(rank, 2, dp_size, seq_size, ff_block)
+        gu_out = lax.dynamic_index_in_dim(gu_all, me, 3, keepdims=False)
+        g_out, u_out = gu_out[:, 0].reshape(rank, ff_own), gu_out[:, 1].reshape(rank, ff_own)
+        down_all = adapter_down_input[adapter].reshape(dp_size, seq_size, ff_block, rank)
+        down_in = lax.dynamic_index_in_dim(down_all, me, 1, keepdims=False).reshape(ff_own, rank)
+        down_out = adapter_down_output[adapter]
+
+        norm_one = rms_scale(hidden_all.astype(F32), attention_norm_gain).astype(BF16)
+        low_qkv = mm(norm_one, qkv_in).astype(BF16)
+        pre = mm(norm_one, qkv)
+        query_pre = pre[:, :q_width] + mm(low_qkv[:, :rank], q_out)
+        key_pre = pre[:, q_width : q_width + HD] + mm(low_qkv[:, rank : 2 * rank], k_out)
+        value_pre = pre[:, q_width + HD :] + mm(low_qkv[:, 2 * rank :], v_out)
+        cos_table, sin_table = angle_tables(jnp.arange(length, dtype=jnp.int32).astype(F32), HD)
+        query = rotate(query_pre.reshape(length, heads, HD), cos_table, sin_table).astype(BF16)
+        keys = rotate(key_pre.reshape(length, 1, HD), cos_table, sin_table).astype(BF16)[:, 0]
+        values = value_pre.astype(BF16)
+        attn_heads, log_totals = attend_forward(query, keys, values, segments)
+        attn = lax.all_gather(attn_heads, "seq", axis=1, tiled=True)
+        low_out = mm(attn, o_in).astype(BF16)
+        branch = mm(attn, out_full) + mm(low_out, o_out)
+        middle = hidden_all.astype(F32) + RESIDUAL_SCALE * branch
+        own_row = me * tokens
+        middle_own = lax.dynamic_slice_in_dim(middle, own_row, tokens, 0)
+        norm_two = rms_scale(middle, feedforward_norm_gain).astype(BF16)
+        low_gu = mm(norm_two, gu_in).astype(BF16)
+        wide = mm(norm_two, gate_up)
+        gate = wide[:, :ff_own] + mm(low_gu[:, :rank], g_out)
+        up_proj = wide[:, ff_own:] + mm(low_gu[:, rank:], u_out)
+        sigma = jax.nn.sigmoid(gate)
+        activation = (gate * sigma * up_proj).astype(BF16)
+        low_down = mm(activation, down_in).astype(BF16)
+        ffn = scatter_seq((mm(activation, down) + mm(low_down, down_out)).astype(BF16))
+        mixed = (middle_own + RESIDUAL_SCALE * ffn.astype(F32)).astype(BF16)
+
+        grad_ffn = gather_seq((RESIDUAL_SCALE * cotangent[0].astype(F32)).astype(BF16))
+        grad_low_down = mm_t(grad_ffn, down_out).astype(BF16)
+        grad_act = mm_t(grad_ffn, down) + mm_t(grad_low_down, down_in)
+        grad_gate = (grad_act * up_proj * sigma * (1.0 + gate * (1.0 - sigma))).astype(BF16)
+        grad_up = (grad_act * gate * sigma).astype(BF16)
+        grad_low_gu = jnp.concatenate([mm_t(grad_gate, g_out), mm_t(grad_up, u_out)], axis=1)
+        grad_low_gu = grad_low_gu.astype(BF16)
+        grad_norm_two = scatter_seq(
+            (
+                mm_t(jnp.concatenate([grad_gate, grad_up], axis=1), gate_up)
+                + mm_t(grad_low_gu, gu_in)
+            ).astype(BF16)
+        )
+        grad_middle = cotangent[0].astype(F32) + rms_back(
+            middle_own, feedforward_norm_gain, grad_norm_two.astype(F32)
+        )
+        grad_branch = (RESIDUAL_SCALE * grad_middle).astype(BF16)
+        grad_low_out = mm_t(grad_branch, o_out).astype(BF16)
+        grad_attn = (mm_t(grad_branch, out_full) + mm_t(grad_low_out, o_in)).astype(BF16)
+        grad_heads = lax.all_to_all(
+            jnp.swapaxes(grad_attn.reshape(tokens, seq_size, q_width), 0, 1),
+            "seq",
+            split_axis=0,
+            concat_axis=0,
+            tiled=True,
+        ).reshape(length, heads, HD)
+        grad_q, grad_k, grad_v = attend_backward(
+            query, keys, values, segments, log_totals, grad_heads
+        )
+        grad_query = rotate(grad_q.astype(F32), cos_table, -sin_table)
+        grad_query = grad_query.reshape(length, q_width).astype(BF16)
+        grad_key = rotate(grad_k[:, None], cos_table, -sin_table)[:, 0].astype(BF16)
+        grad_value = grad_v.astype(BF16)
+        grad_low_qkv = jnp.concatenate(
+            [mm_t(grad_query, q_out), mm_t(grad_key, k_out), mm_t(grad_value, v_out)], axis=1
+        ).astype(BF16)
+        grad_qkv = jnp.concatenate([grad_query, grad_key, grad_value], axis=1)
+        grad_norm_one = scatter_seq((mm_t(grad_qkv, qkv) + mm_t(grad_low_qkv, qkv_in)).astype(BF16))
+        grad_hidden = grad_middle + rms_back(
+            hidden_own, attention_norm_gain, grad_norm_one.astype(F32)
+        )
+
+        attn_own = lax.dynamic_slice_in_dim(attn, own_row, tokens, 0)
+        low_out_own = lax.dynamic_slice_in_dim(low_out, own_row, tokens, 0)
+        partial = jnp.concatenate(
+            [
+                t_mm(norm_one, grad_low_qkv),
+                t_mm(attn_own, grad_low_out),
+                t_mm(grad_branch, low_out_own),
+                t_mm(norm_two, grad_low_gu),
+                t_mm(grad_ffn, low_down),
+            ],
+            axis=1,
+        ).reshape(dp_size, seq_size, rows, 8 * rank)
+        own_q = t_mm(grad_query, low_qkv[:, :rank])
+        own_k = t_mm(grad_key, low_qkv[:, rank : 2 * rank])
+        own_v = t_mm(grad_value, low_qkv[:, 2 * rank :])
+        own_g = t_mm(grad_gate, low_gu[:, :rank]).reshape(dp_size, ff_block, rank)
+        own_u = t_mm(grad_up, low_gu[:, rank:]).reshape(dp_size, ff_block, rank)
+        own_d = t_mm(activation, grad_low_down).reshape(dp_size, ff_block, rank)
+
+        def placed(block, total, start, axis):
+            empty = list(block.shape)
+            empty[axis] = total
+            return lax.dynamic_update_slice_in_dim(jnp.zeros(empty, F32), block, start, axis)
+
+        def by_target(whole):
+            return whole.reshape(dp_size, seq_size, -1)
+
+        full_q = placed(own_q, width, me * q_width, 0)
+        full_kv = jnp.concatenate(
+            [placed(own_k, key_width, kv_start, 0), placed(own_v, key_width, kv_start, 0)], axis=0
+        )
+        spot = [placed(v[:, None], seq_size, me, 1) for v in (own_g, own_u, own_d)]
+        full_gu = jnp.concatenate([spot[0].reshape(ff_width, rank), spot[1].reshape(ff_width, rank)])
+        pieces = [by_target(v) for v in (partial, full_q, full_kv, full_gu, spot[2])]
+        send = jnp.concatenate(pieces, axis=2)
+        send = jnp.swapaxes(send, 0, 1).reshape(seq_size, -1)
+        mine = lax.psum_scatter(send, "seq", scatter_dimension=0, tiled=True)
+        mine = lax.all_to_all(
+            mine.reshape(dp_size, -1), "dp", split_axis=0, concat_axis=0, tiled=True
+        )
+        owners = lax.all_gather(sequence_adapter_index, "dp", axis=0, tiled=True)
+        numbers = jnp.arange(adapters, dtype=jnp.int32)
+        chooser = (owners[:, None] == numbers[None, :]).astype(F32)
+        mine = jnp.einsum("sa,si->ai", chooser, mine, precision=lax.Precision.HIGHEST)
+        sizes = [v.shape[2] for v in pieces]
+        cuts = [sum(sizes[:i]) for i in range(1, len(sizes))]
+        got, got_q, got_kv, got_gu, got_d = jnp.split(mine, cuts, axis=1)
+        got = got.reshape(adapters, rows, 8 * rank)
+
+        def turned(flat):
+            return jnp.swapaxes(flat.reshape(adapters, -1, rank), 1, 2)
+
+        return (
+            mixed[None],
+            grad_hidden.astype(BF16)[None],
+            got[:, :, : 3 * rank],
+            turned(got_q),
+            turned(got_kv),
+            got[:, :, 3 * rank : 4 * rank],
+            jnp.swapaxes(got[:, :, 4 * rank : 5 * rank], 1, 2),
+            got[:, :, 5 * rank : 7 * rank],
+            turned(got_gu),
+            got_d.reshape(adapters, ff_block, rank),
+            jnp.swapaxes(got[:, :, 7 * rank :], 1, 2),
+        )
+
+    return local
+
+
 MESH = pl.DeviceIdType.MESH
 
 
@@ -320,12 +554,12 @@
 
 
 PIECES = 4
-
-
-def gather_kernel(
+QB = 256
+
+
+def front_kernel(
     seq_size,
     hidden,
-    cotangent,
     documents,
     adapter_row,
     query_w,
@@ -333,15 +567,27 @@
     out_w,
     gate_w,
     up_w,
-    down_w,
+    gain,
+    qkv_in,
+    low_map,
+    cos_n,
+    sin_n,
     hidden_all,
-    cotangent_all,
-    documents_all,
     adapters_all,
     qkv_all,
     out_all,
     gu_all,
-    down_all,
+    attn_all,
+    norm_all,
+    query,
+    keys2,
+    values2,
+    keys_t,
+    log_totals,
+    seg_row,
+    seg_col,
+    low_t,
+    documents_all,
     chain_sems,
     plane_sems,
     local_sems,
@@ -349,18 +595,22 @@
     small_sems,
     side_sems,
     hidden_v,
-    cotangent_v,
+    norm_v,
     out_v,
-    down_v,
     qkv_v,
     gu_v,
+    weights_v,
+    key_z,
+    values_t,
+    bias,
+    attn_v,
 ):
     p = Place(seq_size)
     d, s, z, c = p.d, p.s, p.z, p.c
     rows = query_w.shape[0]
-    part = down_w.shape[0]
+    part = gate_w.shape[1] // (4 * seq_size)
+    tokens = hidden.shape[0]
     half_rows = seq_size * rows // 2
-
     landing = pl.ds(pl.multiple_of(rows * s, rows), rows)
     q_width = query_w.shape[1] // seq_size
 
@@ -368,12 +618,12 @@
         return pl.ds(pl.multiple_of(number * size, size), size)
 
     stage = [
-        (hidden, hidden_v),
-        (cotangent, cotangent_v),
+        (hidden, hidden_v.at[s]),
         (out_w, out_v),
-        (down_w, down_v),
         (query_w.at[:, column_block(s, q_width)], qkv_v.at[:, pl.ds(0, q_width)]),
         (kv_w.at[s], qkv_v.at[:, pl.ds(q_width, kv_w.shape[2])]),
+        (documents, documents_all.at[s]),
+        (adapter_row, adapters_all.at[d]),
     ]
     for i in range(8):
         matrix = (gate_w, up_w)[i // 4]
@@ -386,14 +636,13 @@
         pltpu.make_async_copy(src, dst, local_sems.at[1, i])
         for i, (src, dst) in enumerate(
             (
-                (hidden_v, hidden_all.at[s]),
-                (cotangent_v, cotangent_all.at[s]),
                 (out_v, out_all.at[d, z, c]),
-                (down_v, down_all.at[d]),
                 (qkv_v, qkv_all.at[d, landing]),
                 (gu_v, gu_all.at[d, landing]),
-                (documents, documents_all.at[s]),
-                (adapter_row, adapters_all.at[d]),
+                (qkv_all, weights_v),
+                (hidden_v, hidden_all),
+                (norm_v, norm_all),
+                (attn_v, attn_all.at[s]),
             )
         )
     ]
@@ -401,16 +650,14 @@
         copy.start()
     p.greet(range(1, seq_size), (p.dx, p.dy, p.dd))
 
-    hid = Chain(p, hidden, lambda i: hidden_all.at[i], chain_sems.at[0])
-    cot = Chain(p, cotangent, lambda i: cotangent_all.at[i], chain_sems.at[1])
+    hid = Chain(p, hidden, lambda i: hidden_v.at[i], chain_sems.at[0])
     out = Chain(p, out_w, lambda i: out_all.at[d, i // 2, i % 2], chain_sems.at[2])
+    att = Chain(p, attn_v, lambda i: attn_all.at[i], chain_sems.at[3])
 
     def qkv_pairs(j):
-        width = query_w.shape[1] // seq_size
-        columns = pl.ds(pl.multiple_of(width * j, width), width)
         return (
-            (query_w.at[:, columns], qkv_all.at[d, landing, pl.ds(0, width)]),
-            (kv_w.at[j], qkv_all.at[d, landing, pl.ds(width, kv_w.shape[2])]),
+            (query_w.at[:, column_block(j, q_width)], qkv_all.at[d, landing, pl.ds(0, q_width)]),
+            (kv_w.at[j], qkv_all.at[d, landing, pl.ds(q_width, kv_w.shape[2])]),
         )
 
     def gu_pairs(piece):
@@ -419,9 +666,9 @@
         def pairs(j):
             found = []
             for block in (2 * (piece % 2), 2 * (piece % 2) + 1):
-                columns = pl.ds(pl.multiple_of(part * (seq_size * block + j), part), part)
                 at = part * (4 * (piece // 2) + block)
-                found.append((matrix.at[:, columns], gu_all.at[d, landing, pl.ds(at, part)]))
+                source = matrix.at[:, column_block(seq_size * block + j, part)]
+                found.append((source, gu_all.at[d, landing, pl.ds(at, part)]))
             return found
 
         return pairs
@@ -436,7 +683,8 @@
         cut = pl.ds(2 * part * i, 2 * part)
         gu.append(
             Spread(
-                p, gu_pairs(i), [gu_all.at[d, others, cut]], spread_sems.at[1 + i, 0], spread_sems.at[1 + i, 1],
+                p, gu_pairs(i), [gu_all.at[d, others, cut]], spread_sems.at[1 + i, 0],
+                spread_sems.at[1 + i, 1],
             )
         )
         gu_planes.append(
@@ -452,12 +700,6 @@
         lambda e: qkv_all.at[e],
         lambda e, h: qkv_all.at[e, pl.ds(half_rows * h, half_rows)],
         plane_sems.at[0],
-    )
-    down = Plane(
-        p,
-        lambda e: down_w if e is d else down_all.at[e],
-        lambda e, h: down_all.at[e, pl.ds(part // 2 * h, part // 2)],
-        plane_sems.at[1],
     )
     half_chips = p.chips // 2
     out_plane = Plane(
@@ -469,7 +711,8 @@
 
     def documents_copy(step):
         return remote(
-            documents, documents_all.at[s], small_sems.at[0, step], small_sems.at[1, 0], p.seq(p.peer(step))
+            documents, documents_all.at[s], small_sems.at[0, step], small_sems.at[1, 0],
+            p.seq(p.peer(step)),
         )
 
     def adapters_copy(i, e):
@@ -484,6 +727,75 @@
     def side_wait(i, e):
         ref = out_all.at[e, :, 1 - c]
         remote(ref, ref, side_sems.at[0, i], side_sems.at[1, i], p.seq(p.sib)).wait_recv()
+
+    low_lane = lax.broadcasted_iota(jnp.int32, (tokens, 2 * HD), 1) < HD
+    weights = weights_v.reshape(4 * seq_size * rows, qkv_v.shape[1])
+
+    def process(slot):
+        at = pl.ds(pl.multiple_of(slot * tokens, tokens), tokens)
+        cos_part, sin_part = cos_n[at, :], sin_n[at, :]
+        normed = rms_scale(hidden_v[slot].astype(F32), gain[...]).astype(BF16)
+        norm_v[slot] = normed
+        low = dot_nn(normed, qkv_in[...]).astype(BF16)
+        pre = dot_nn(normed, weights[...]) + dot_nn(low, low_map[...])
+        padded = jnp.concatenate(
+            [low.astype(F32), jnp.zeros((tokens, 128 - low.shape[1]), F32)], axis=1
+        )
+        low_t[:, at] = padded.T[: low.shape[1]].astype(BF16)
+        for m in range(2):
+            pair = pre[:, 2 * HD * m : 2 * HD * (m + 1)]
+            turned = pair * cos_part + swap_halves(pair) * sin_part
+            query[at, pl.ds(2 * HD * m, 2 * HD)] = turned.astype(BF16)
+        pair = pre[:, 4 * HD :]
+        turned = pair * cos_part + swap_halves(pair) * sin_part
+        both = jnp.where(low_lane, turned, pair)
+        crossed = pltpu.roll(both, HD, 1)
+        keys2[at, :] = jnp.where(low_lane, both, crossed).astype(BF16)
+        values2[at, :] = jnp.where(low_lane, crossed, both).astype(BF16)
+        zero = jnp.zeros_like(both)
+        key_z[0, at, :] = jnp.where(low_lane, both, zero).astype(BF16)
+        key_z[1, at, :] = jnp.where(low_lane, zero, crossed).astype(BF16)
+        both_t = both.T
+        keys_t[:, at] = both_t[:HD].astype(BF16)
+        values_t[:, at] = both_t[HD:].astype(BF16)
+
+    def process_distance(k):
+        @pl.when(p.z >= k)
+        def _():
+            hid.side_recv(p.z - k)
+
+            @pl.loop(0, 2)
+            def _(core):
+                process(2 * (p.z - k) + core)
+
+        if k:
+
+            @pl.when(p.z + k < p.chips)
+            def _():
+                hid.side_recv(p.z + k)
+
+                @pl.loop(0, 2)
+                def _(core):
+                    process(2 * (p.z + k) + core)
+
+    def query_block(i):
+        start = i * QB
+        span = pl.ds(0, start + QB)
+        at = pl.ds(start, QB)
+        bias[span, :] = mask_bias(seg_col, seg_row, start, QB)
+
+        for m in range(2):
+            pair = pl.ds(2 * HD * m, 2 * HD)
+            query_pair = query[at, pair]
+            found = []
+            for e in range(2):
+                scores = dot_nt(key_z[e, span, :], query_pair) * SCORE_SCALE + bias[span, :]
+                top = jnp.max(scores, axis=0, keepdims=True)
+                raised = jnp.exp(scores - top)
+                total = jnp.sum(raised, axis=0, keepdims=True)
+                found.append(dot_nn(values_t[:, span], raised.astype(BF16)) / total)
+                log_totals[2 * m + e : 2 * m + e + 1, at] = top + jnp.log(total)
+            attn_v[at, pair] = jnp.concatenate(found, axis=0).T.astype(BF16)
 
     for step in range(1, seq_size):
         documents_copy(step).start()
@@ -491,68 +803,80 @@
         adapters_copy(i, e).start()
     qkv.start()
     hid.start()
-    for i, e in enumerate((p.dx, p.dy)):
-        remote(
-            down_w, down_all.at[d], down.sems.at[0, i], down.sems.at[1, i], p.dp(e)
-        ).start()
     for copy in stage:
         copy.wait()
-    for copy in keep:
-        copy.start()
-    for copy in keep:
-        copy.wait()
+    for i in range(3):
+        keep[i].start()
+    for i in range(3):
+        keep[i].wait()
     qkv.recv()
     qkv_plane.start()
     hid.step(1)
     gu[0].start()
-    down.forward()
+    remote(
+        documents_all.at[pl.ds(0, seq_size - 1)], documents_all.at[pl.ds(0, seq_size - 1)],
+        small_sems.at[0, 0], small_sems.at[1, 0], p.seq(p.sib),
+    ).wait_recv()
+    for slot in range(seq_size):
+        at = pl.ds(tokens * slot, tokens)
+        numbers = documents_all[slot].astype(F32)
+        seg_row[:, at] = numbers
+        seg_col[at, :] = jnp.broadcast_to(numbers[0:1, :], (tokens, tokens)).T
     qkv_plane.forward()
     hid.step(2)
     gu[1].start()
     gu[0].recv()
     gu_planes[0].start()
+    qkv_plane.recv()
+    keep[3].start()
+    keep[3].wait()
+    process_distance(0)
+    process_distance(1)
     hid.step(3)
     gu[2].start()
-    qkv_plane.recv()
     out.start()
     gu[1].recv()
     gu_planes[1].start()
     gu_planes[0].forward()
+    process_distance(2)
+    process_distance(3)
     gu[3].start()
     out.step(1)
+    keep[4].start()
+    keep[5].start()
+    query_block(0)
+    query_block(1)
     gu[2].recv()
     gu_planes[2].start()
     gu_planes[1].forward()
     out.step(2)
-    cot.start()
+    query_block(2)
+    query_block(3)
+    keep[6].start()
+    att.start()
     gu[3].recv()
     gu_planes[3].start()
     gu_planes[2].forward()
     out.step(3)
     out_plane.start()
-    cot.step(1)
+    att.step(1)
     gu_planes[3].forward()
-    cot.step(2)
+    att.step(2)
     out_plane.forward()
     side_copy(0, p.dx).start()
     side_copy(1, p.dy).start()
-    cot.step(3)
+    att.step(3)
     out_plane.recv()
     side_copy(2, p.dd).start()
     for i in range(4):
         gu_planes[i].recv()
-    down.recv()
-    for chain in (hid, out, cot):
+    for chain in (out, att):
         for other in range(p.chips):
             chain.side_recv(other)
+    for chain in (hid, out, att):
         chain.finish()
-    side_wait(0, p.dx)
-    side_wait(1, p.dy)
-    side_wait(2, p.dd)
-    remote(
-        documents_all.at[pl.ds(0, seq_size - 1)], documents_all.at[pl.ds(0, seq_size - 1)],
-        small_sems.at[0, 0], small_sems.at[1, 0], p.seq(p.sib),
-    ).wait_recv()
+    for i, e in enumerate((p.dx, p.dy, p.dd)):
+        side_wait(i, e)
     remote(
         adapters_all.at[pl.ds(0, 3)], adapters_all.at[pl.ds(0, 3)],
         small_sems.at[2, 3], small_sems.at[3, 0], p.dp(p.dx),
@@ -562,55 +886,76 @@
     for i, e in enumerate((p.dx, p.dy, p.dd)):
         adapters_copy(i, e).wait_send()
         side_copy(i, e).wait_send()
-    for group in [qkv, *gu, qkv_plane, down, out_plane, *gu_planes]:
+    for group in [qkv, *gu, qkv_plane, out_plane, *gu_planes]:
         group.finish()
-
-
-def gather_all(
-    seq_size, hidden, cotangent, documents, adapter_row, query_w, kv_w, out_w, gate_w, up_w, down_w
-):
-    tokens, width = hidden.shape
-    rows = query_w.shape[0]
-    part = down_w.shape[0]
+    for i in (4, 5, 6):
+        keep[i].wait()
+
+
+def front_all(seq_size, ins):
+    tokens, width = ins[0].shape
+    rows = ins[3].shape[0]
+    part = ins[6].shape[1] // (4 * seq_size)
     chips = seq_size // 2
-    qkv_width = query_w.shape[1] // seq_size + kv_w.shape[2]
+    q_width = ins[3].shape[1] // seq_size
+    qkv_width = q_width + ins[4].shape[2]
+    length = tokens * seq_size
+    low_width = ins[9].shape[1]
 
     def shape(*dims, dtype=BF16):
         return jax.ShapeDtypeStruct(dims, dtype)
 
     anywhere = pl.BlockSpec(memory_space=pl.ANY)
+    vmem = pl.BlockSpec(memory_space=pltpu.VMEM)
+    outs = (
+        shape(seq_size, tokens, width),
+        shape(4, 8, 128, dtype=jnp.int32),
+        shape(4, seq_size * rows, qkv_width),
+        shape(4, chips, 2, rows, width),
+        shape(4, seq_size * rows, 8 * part),
+        shape(seq_size, length, q_width),
+        shape(seq_size, tokens, width),
+        shape(length, q_width),
+        shape(length, 2 * HD),
+        shape(length, 2 * HD),
+        shape(HD, length),
+        shape(4, length, dtype=F32),
+        shape(8, length, dtype=F32),
+        shape(length, tokens, dtype=F32),
+        shape(low_width, length),
+    )
     return pl.pallas_call(
-        functools.partial(gather_kernel, seq_size),
-        out_shape=(
-            shape(seq_size, tokens, width),
-            shape(seq_size, tokens, width),
-            shape(seq_size, 8, tokens, dtype=jnp.int32),
-            shape(4, 8, 128, dtype=jnp.int32),
-            shape(4, seq_size * rows, qkv_width),
-            shape(4, chips, 2, rows, width),
-            shape(4, seq_size * rows, 8 * part),
-            shape(4, part, width),
-        ),
-        in_specs=[anywhere] * 10,
-        out_specs=(anywhere,) * 8,
+        functools.partial(front_kernel, seq_size),
+        out_shape=outs,
+        in_specs=[anywhere] * 8 + [vmem] * 5,
+        out_specs=(anywhere,) * 7 + (vmem,) * 8,
         scratch_shapes=[
-            pltpu.SemaphoreType.DMA((3, 4, seq_size)),
+            pltpu.VMEM((seq_size, 8, tokens), jnp.int32),
+            pltpu.SemaphoreType.DMA((4, 4, seq_size)),
             pltpu.SemaphoreType.DMA((3 + PIECES, 2, 4)),
-            pltpu.SemaphoreType.DMA((2, 14)),
+            pltpu.SemaphoreType.DMA((2, 16)),
             pltpu.SemaphoreType.DMA((1 + PIECES, 2)),
             pltpu.SemaphoreType.DMA((4, seq_size)),
             pltpu.SemaphoreType.DMA((2, 3)),
-            pltpu.VMEM((tokens, width), BF16),
-            pltpu.VMEM((tokens, width), BF16),
+            pltpu.VMEM((seq_size, tokens, width), BF16),
+            pltpu.VMEM((seq_size, tokens, width), BF16),
             pltpu.VMEM((rows, width), BF16),
-            pltpu.VMEM((part, width), BF16),
             pltpu.VMEM((rows, qkv_width), BF16),
             pltpu.VMEM((rows, 8 * part), BF16),
+            pltpu.VMEM((4, seq_size * rows, qkv_width), BF16),
+            pltpu.VMEM((2, length, 2 * HD), BF16),
+            pltpu.VMEM((HD, length), BF16),
+            pltpu.VMEM((length, QB), F32),
+            pltpu.VMEM((length, q_width), BF16),
         ],
-        compiler_params=pltpu.CompilerParams(collective_id=0, has_side_effects=True),
-        cost_estimate=pl.CostEstimate(flops=0, bytes_accessed=2 * 30 * 2**20, transcendentals=0),
-        name="gather_all",
-    )(hidden, cotangent, documents, adapter_row, query_w, kv_w, out_w, gate_w, up_w, down_w)
+        compiler_params=pltpu.CompilerParams(
+            collective_id=0, has_side_effects=True, vmem_limit_bytes=60 * 2**20
+        ),
+        cost_estimate=pl.CostEstimate(
+            flops=5 * 10**9, bytes_accessed=60 * 2**20, transcendentals=4 * 2**20
+        ),
+        name="attend_front",
+    )(*ins)
 
 
 def dot_nn(a, b):
@@ -719,6 +1064,11 @@
             @pl.when(p.z >= k)
             def _():
                 self._down(p.z - k).wait_send()
+
+
+def chain_order(z):
+    second = jnp.where(z == 0, 2, jnp.where(z == 1, 0, jnp.where(z == 2, 3, 1)))
+    return (jnp.where(z < 2, 3, 0), second, jnp.where(z % 2 == 0, 1, 2), z)
 
 
 def swap_halves(values):
@@ -736,9 +1086,6 @@
     query_pos = start + lax.broadcasted_iota(jnp.int32, (length, size), 1)
     same = seg_col[pl.ds(0, length), 0:1] == seg_row[0:1, pl.ds(start, size)]
     return jnp.where((key_pos <= query_pos) & same, 0.0, -1e30).astype(F32)
-
-
-QB = 256
 
 
 def back_kernel(
@@ -968,45 +1315,33 @@
 
     tokens = sum_v.shape[1]
 
-    def fill(slot):
-        rows = pl.ds(pl.multiple_of(slot * tokens, tokens), tokens)
+    def give(to):
+        rows = pl.ds(pl.multiple_of(2 * to * tokens, 2 * tokens), 2 * tokens)
         left, low = grad_qkv[rows, :], grad_low[rows, :]
         for j in range(4):
             cut = pl.ds(512 * j, 512)
-            sum_v[slot, :, cut] = (
-                dot_nt(left, qkv_v[cut, :]) + dot_nt(low, qkv_in[cut, :])
-            ).astype(BF16)
-
-    for k in (3, 2, 1, 0):
-
-        def give(to):
-            fill(2 * to)
-            fill(2 * to + 1)
-            total.side_start(to)
-
-        @pl.when(p.z + k < chips)
-        def _():
-            give(p.z + k)
-
-        if k:
-
-            @pl.when(p.z >= k)
-            def _():
-                give(p.z - k)
-
-            total.step(k)
-        if k == 2:
-            outer = dot_nn(low_qkv_t[...], grad_qkv[...])
-            outer = jnp.concatenate([outer, jnp.zeros((80, outer.shape[1]), F32)], axis=0)
-            turned[...] = outer.T
-            deliver_heads(False)
-            for j in range(8):
-                cut = pl.ds(256 * j, 256)
-                piece = jnp.concatenate(
-                    [dot_nn(grad_low_t, norm_v[:, cut]), early_t[:, cut]], axis=0
-                )
-                share[cut, :] = piece.T.astype(BF16)
-            deliver_share(False)
+            value = dot_nt(left, qkv_v[cut, :]) + dot_nt(low, qkv_in[cut, :])
+            sum_v[2 * to, :, cut] = value[:tokens].astype(BF16)
+            sum_v[2 * to + 1, :, cut] = value[tokens:].astype(BF16)
+        total.side_start(to)
+
+    order = chain_order(p.z)
+    give(order[0])
+    total.step(3)
+    give(order[1])
+    give(order[2])
+    give(order[3])
+    outer = dot_nn(low_qkv_t[...], grad_qkv[...])
+    outer = jnp.concatenate([outer, jnp.zeros((80, outer.shape[1]), F32)], axis=0)
+    turned[...] = outer.T
+    deliver_heads(False)
+    total.step(2)
+    for j in range(8):
+        cut = pl.ds(256 * j, 256)
+        piece = jnp.concatenate([dot_nn(grad_low_t, norm_v[:, cut]), early_t[:, cut]], axis=0)
+        share[cut, :] = piece.T.astype(BF16)
+    deliver_share(False)
+    total.step(1)
     ffn.last()
     ffn_sum[...] = ffn_v[s].astype(F32)
     for buffer, i in ((gu_in, 0), (down_in, 1), (q_got, 2), (kv_got, 3), (share_in, 4)):
@@ -1112,11 +1447,322 @@
     )(*ins)
 
 
-def make_local(dp_size, seq_size):
-    devices = dp_size * seq_size
+def mid_kernel(
+    seq_size,
+    attn_all,
+    hidden_all,
+    out_all,
+    gu_all,
+    cotangent,
+    down_w,
+    gain,
+    o_in,
+    o_out,
+    gu_in,
+    gu_map,
+    down_in,
+    down_out,
+    ffn_part,
+    middle_own,
+    grad_middle,
+    grad_attn,
+    early_t,
+    gu_grad,
+    down_grad,
+    out_v,
+    gu_v,
+    down_v,
+    cot_v,
+    norm_v,
+    both_v,
+    wide,
+    act_v,
+    sum_v,
+    sum_side,
+    sum_up,
+    sum_down,
+    attn_own,
+    low_own,
+    lows,
+    lows_t,
+    chain_sems,
+    plane_sems,
+    sum_sems,
+    local_sems,
+):
+    p = Place(seq_size)
+    d, s, z, c = p.d, p.s, p.z, p.c
+    tokens, width = cotangent.shape
+    part = down_w.shape[0]
+    span = 2 * tokens
+    hidden_width = 4 * part
+    rank = o_in.shape[1]
+    heads_width = attn_all.shape[2]
+    step_width = 512
+    loads = [
+        pltpu.make_async_copy(src, dst, local_sems.at[0, i])
+        for i, (src, dst) in enumerate(
+            [(down_w, down_v.at[d]), (cotangent, cot_v.at[s]), (hidden_all, norm_v), (out_all, out_v)]
+            + [
+                (attn_all.at[j], both_v.at[:, pl.ds(heads_width * j, heads_width)])
+                for j in range(seq_size)
+            ]
+            + [(gu_all, gu_v)]
+        )
+    ]
+    for copy in loads:
+        copy.start()
+    barrier = pltpu.get_barrier_semaphore()
+    p_up, p_down = p.z < p.chips - 1, p.z > 0
+
+    @pl.when(p_up)
+    def _():
+        pl.semaphore_signal(barrier, 1, device_id=p.seq(s + 2), device_id_type=MESH)
+
+    @pl.when(p_down)
+    def _():
+        pl.semaphore_signal(barrier, 1, device_id=p.seq(s - 2), device_id_type=MESH)
+
+    for place in (p.seq(p.sib), p.dp(p.dx), p.dp(p.dy)):
+        pl.semaphore_signal(barrier, 1, device_id=place, device_id_type=MESH)
+
+    @pl.when(p_up & p_down)
+    def _():
+        pl.semaphore_wait(barrier, 5)
+
+    @pl.when(jnp.logical_not(p_up & p_down))
+    def _():
+        pl.semaphore_wait(barrier, 4)
+
+    cot = Chain(p, cotangent, lambda i: cot_v.at[i], chain_sems)
+    down = Plane(
+        p,
+        lambda e: down_v.at[e],
+        lambda e, h: down_v.at[e, pl.ds(part // 2 * h, part // 2)],
+        plane_sems,
+    )
+    total = ChainSum(p, sum_v, sum_side, sum_up, sum_down, sum_sems)
+    down_all = down_v.reshape(4 * part, width)
+    cot.start()
+    loads[0].wait()
+    down.start()
+    for copy in loads[1:-1]:
+        copy.wait()
+
+    def columns(body, count):
+        @pl.loop(0, count)
+        def _(n):
+            body(pl.ds(pl.multiple_of(n * step_width, step_width), step_width))
+
+    def flat(ref, zz, cut=slice(None)):
+        return ref[pl.ds(2 * zz, 2), :, cut].reshape(span, -1)
+
+    lows[...] = jnp.zeros_like(lows)
+
+    def forward(zz):
+        rows = pl.ds(span * zz, span)
+        low = dot_nn(both_v[rows, :], o_in[...]).astype(BF16)
+
+        def branch(cut):
+            value = dot_nn(both_v[rows, :], out_v[:, cut]) + dot_nn(low, o_out[:, cut])
+            wide[rows, cut] = flat(norm_v, zz, cut).astype(F32) + RESIDUAL_SCALE * value
+
+        columns(branch, width // step_width)
+
+        @pl.when(z == zz)
+        def _():
+            mine = pl.ds(pl.multiple_of(s * tokens, tokens), tokens)
+            middle_own[...] = wide[mine, :]
+            attn_own[...] = both_v[mine, :]
+            low_own[...] = dot_nn(attn_own[...], o_in[...]).astype(BF16)
+
+        middle = wide[rows, :]
+        normed = rms_scale(middle, gain[...]).astype(BF16)
+        norm_v[2 * zz] = normed[:tokens]
+        norm_v[2 * zz + 1] = normed[tokens:]
+        low_gu = dot_nn(normed, gu_in[...]).astype(BF16)
+        lows[rows, 0 : 2 * rank] = low_gu.astype(F32)
+
+        def gate_up(cut):
+            value = dot_nn(flat(norm_v, zz), gu_v[:, cut]) + dot_nn(low_gu, gu_map[:, cut])
+            wide[rows, cut] = value
+
+        columns(gate_up, 2 * hidden_width // step_width)
+
+    for zz in range(p.chips):
+        if zz == 0:
+            loads[-1].wait()
+        forward(zz)
+        if zz == 0:
+            cot.step(1)
+        if zz == 2:
+            cot.step(2)
+            down.forward()
+    cot.step(3)
+    down.recv()
+    for zz in range(p.chips):
+        cot.side_recv(zz)
+
+    def backward(zz):
+        rows = pl.ds(pl.multiple_of(span * zz, span), span)
+        grad = flat(cot_v, zz)
+        low = dot_nt(grad, down_out[...]).astype(BF16)
+        lows[rows, 5 * rank : 6 * rank] = low.astype(F32)
+
+        def hidden_part(n):
+            cut = pl.ds(pl.multiple_of(n * step_width, step_width), step_width)
+            upper = pl.ds(pl.multiple_of(hidden_width + n * step_width, step_width), step_width)
+            grad_act = RESIDUAL_SCALE * (
+                dot_nt(flat(cot_v, zz), down_all[cut, :]) + dot_nt(low, down_in[cut, :])
+            )
+            gate, up = wide[rows, cut], wide[rows, upper]
+            sigma = 1.0 / (1.0 + jnp.exp(-gate))
+            raised = gate * sigma
+            act_v[rows, cut] = (raised * up).astype(BF16)
+            both_v[rows, cut] = (grad_act * up * sigma * (1.0 + gate * (1.0 - sigma))).astype(BF16)
+            both_v[rows, upper] = (grad_act * raised).astype(BF16)
+
+        pl.loop(0, hidden_width // step_width)(hidden_part)
+        low_gu = dot_nt(both_v[rows, :], gu_map[...]).astype(BF16)
+        lows[rows, 2 * rank : 4 * rank] = low_gu.astype(F32)
+
+        def model_part(cut):
+            value = dot_nt(both_v[rows, :], gu_v[cut, :]) + dot_nt(low_gu, gu_in[cut, :])
+            sum_v[2 * zz, :, cut] = value[:tokens].astype(BF16)
+            sum_v[2 * zz + 1, :, cut] = value[tokens:].astype(BF16)
+
+        columns(model_part, width // step_width)
+        total.side_start(zz)
+
+    order = chain_order(z)
+    backward(order[0])
+    total.step(3)
+    backward(order[1])
+    backward(order[2])
+    total.step(2)
+    backward(order[3])
+    lows[:, 4 * rank : 5 * rank] = dot_nn(act_v[...], down_in[...])
+    for zz in range(p.chips):
+        lows_t[:, pl.ds(span * zz, span)] = lows[pl.ds(span * zz, span), :].T.astype(BF16)
+    total.step(1)
+    length = seq_size * tokens
+
+    for n in range(width // step_width):
+        cut = pl.ds(step_width * n, step_width)
+        early_t[2 * rank : 4 * rank, cut] = dot_nn(
+            lows_t[2 * rank : 4 * rank, :], norm_v[:, :, cut].reshape(length, step_width)
+        )
+        early_t[4 * rank : 5 * rank, cut] = RESIDUAL_SCALE * dot_nn(
+            lows_t[4 * rank : 5 * rank, :], cot_v[:, :, cut].reshape(length, step_width)
+        )
+        source = pl.ds(0, rank) if n < hidden_width // step_width else pl.ds(rank, rank)
+        gu_grad[:, cut] = dot_nn(lows_t[source, :], both_v[:, cut])
+        if n < hidden_width // step_width:
+            down_grad[:, cut] = RESIDUAL_SCALE * dot_nn(
+                lows_t[5 * rank : 6 * rank, :], act_v[:, cut]
+            )
+
+    @pl.loop(0, p.chips)
+    def _(zz):
+        rows = pl.ds(pl.multiple_of(span * zz, span), span)
+        low = lows[rows, 4 * rank : 5 * rank].astype(BF16)
+
+        def block(cut):
+            value = dot_nn(act_v[rows, :], down_all[:, cut]) + dot_nn(low, down_out[:, cut])
+            norm_v[2 * zz, :, cut] = value[:tokens].astype(BF16)
+            norm_v[2 * zz + 1, :, cut] = value[tokens:].astype(BF16)
+
+        columns(block, width // step_width)
+
+    store = pltpu.make_async_copy(norm_v, ffn_part, local_sems.at[1, 0])
+    store.start()
+    total.last()
+    middle = middle_own[...]
+    mean = jnp.mean(middle * middle, axis=-1, keepdims=True)
+    r = lax.rsqrt(mean + EPSILON)
+    scaled = sum_v[s].astype(F32) * gain[...]
+    inner = jnp.mean(scaled * middle, axis=-1, keepdims=True)
+    grad_mid = cot_v[s].astype(F32) + r * scaled - r * r * r * inner * middle
+    grad_middle[...] = grad_mid
+    branch = (RESIDUAL_SCALE * grad_mid).astype(BF16)
+    low = dot_nt(branch, o_out[...]).astype(BF16)
+    for j in range(seq_size):
+        cut = pl.ds(heads_width * j, heads_width)
+        grad_attn[j] = (dot_nt(branch, out_v[cut, :]) + dot_nt(low, o_in[cut, :])).astype(BF16)
+    pair = jnp.concatenate(
+        [low.astype(F32), low_own[...].astype(F32), jnp.zeros((tokens, 128 - 2 * rank), F32)], axis=1
+    )
+    pair = pair.T.astype(BF16)
+    early_t[0:rank, :] = dot_nn(pair[0:rank], attn_own[...])
+    early_t[rank : 2 * rank, :] = dot_nn(pair[rank : 2 * rank], branch)
+    cot.finish()
+    down.finish()
+    total.finish()
+    store.wait()
+
+
+def mid_all(seq_size, ins):
+    tokens, width = ins[4].shape
+    part = ins[5].shape[0]
+    length = seq_size * tokens
+    rank = ins[7].shape[1]
+    chips = seq_size // 2
+    heads_width = ins[0].shape[2]
+
+    def shape(*dims, dtype=F32):
+        return jax.ShapeDtypeStruct(dims, dtype)
+
+    vmem = pl.BlockSpec(memory_space=pltpu.VMEM)
+    anywhere = pl.BlockSpec(memory_space=pl.ANY)
+    many, few = (seq_size, tokens, width), (chips, tokens, width)
+    outs = (
+        shape(*many, dtype=BF16),
+        shape(tokens, width),
+        shape(tokens, width),
+        shape(seq_size, tokens, heads_width, dtype=BF16),
+        shape(5 * rank, width),
+        shape(rank, 8 * part),
+        shape(rank, 4 * part),
+    )
+    return pl.pallas_call(
+        functools.partial(mid_kernel, seq_size),
+        out_shape=outs,
+        in_specs=[anywhere] * 6 + [vmem] * 7,
+        out_specs=(anywhere,) + (vmem,) * 6,
+        scratch_shapes=[
+            pltpu.VMEM((width, width), BF16),
+            pltpu.VMEM((width, 8 * part), BF16),
+            pltpu.VMEM((4, part, width), BF16),
+            pltpu.VMEM(many, BF16),
+            pltpu.VMEM(many, BF16),
+            pltpu.VMEM((length, width), BF16),
+            pltpu.VMEM((length, 8 * part), F32),
+            pltpu.VMEM((length, 4 * part), BF16),
+            pltpu.VMEM(many, BF16),
+            pltpu.VMEM(few, BF16),
+            pltpu.VMEM(few, BF16),
+            pltpu.VMEM(few, BF16),
+            pltpu.VMEM((tokens, width), BF16),
+            pltpu.VMEM((tokens, rank), BF16),
+            pltpu.VMEM((length, 128), F32),
+            pltpu.VMEM((128, length), BF16),
+            pltpu.SemaphoreType.DMA((4, seq_size)),
+            pltpu.SemaphoreType.DMA((2, 4)),
+            pltpu.SemaphoreType.DMA((6, chips)),
+            pltpu.SemaphoreType.DMA((2, 13)),
+        ],
+        compiler_params=pltpu.CompilerParams(
+            collective_id=2, has_side_effects=True, vmem_limit_bytes=63 * 2**20
+        ),
+        cost_estimate=pl.CostEstimate(
+            flops=40 * 10**9, bytes_accessed=40 * 2**20, transcendentals=4 * 2**20
+        ),
+        name="feed_forward",
+    )(*ins)
+
+
+def make_kernel_local(dp_size, seq_size):
     heads = NH // seq_size
-    kv_repeat = max(1, seq_size // KVH)
-    kernels = dp_size == 4 and seq_size == 8
 
     def local(
         hidden,
@@ -1146,37 +1792,58 @@
         length = tokens * seq_size
         rows = query_weight.shape[0]
         key_width = key_weight.shape[1]
-        ff_width = gate_weight.shape[1]
-        ff_block = ff_width // devices
+        ff_block = gate_weight.shape[1] // (dp_size * seq_size)
+        ff_own = dp_size * ff_block
         rank = adapter_projection_input.shape[2]
-        adapters = adapter_projection_input.shape[0]
+        q_width = heads * HD
         me = lax.axis_index("seq")
-        q_width = heads * HD
-
-        def across(piece):
-            return lax.all_to_all(piece, "seq", split_axis=0, concat_axis=0, tiled=True)
-
-        def gather_dp(block):
-            return lax.all_gather(block, "dp", axis=0, tiled=True)
-
-        def gather_seq(block):
-            return lax.all_gather(block, "seq", axis=0, tiled=True)
-
-        def scatter_seq(total):
-            return lax.psum_scatter(total, "seq", scatter_dimension=0, tiled=True)
-
-        def by_owner(columns):
-            return columns.reshape(columns.shape[0], dp_size, seq_size, ff_block)
-
-        hidden_own = hidden[0].astype(F32)
-        if kernels:
-            kv = jnp.concatenate(
-                [key_weight.reshape(rows, KVH, HD), value_weight.reshape(rows, KVH, HD)], axis=2
-            )
-            gathered = gather_all(
-                seq_size,
+        adapter = sequence_adapter_index[0]
+
+        def pick(maps):
+            return lax.dynamic_index_in_dim(maps, adapter, 0, keepdims=False)
+
+        def pick_columns(maps, start, size):
+            return lax.dynamic_slice(maps, (adapter, 0, start), (1, rank, size))[0]
+
+        qkv_in = pick(adapter_query_key_value_input)
+        q_out = pick_columns(adapter_query_output, me * q_width, q_width)
+        k_out = pick_columns(adapter_key_value_output, me * HD, HD)
+        v_out = pick_columns(adapter_key_value_output, key_width + me * HD, HD)
+        none_q, none_h = jnp.zeros((rank, q_width), BF16), jnp.zeros((rank, HD), BF16)
+        low_map = jnp.concatenate(
+            [
+                jnp.concatenate([q_out, none_h, none_h], axis=1),
+                jnp.concatenate([none_q, k_out, none_h], axis=1),
+                jnp.concatenate([none_q, none_h, v_out], axis=1),
+            ],
+            axis=0,
+        )
+        kv = jnp.concatenate(
+            [key_weight.reshape(rows, KVH, HD), value_weight.reshape(rows, KVH, HD)], axis=2
+        )
+        cos_fixed, sin_fixed = fixed_tables(length)
+        cos_n = jnp.asarray(np.tile(cos_fixed, (1, 4)))
+        sin_n = jnp.asarray(np.tile(np.concatenate([-sin_fixed, sin_fixed], axis=1), (1, 2)))
+        (
+            hidden_all,
+            owners,
+            qkv,
+            out_full,
+            gate_up,
+            attn,
+            norm_one,
+            query,
+            keys2,
+            values2,
+            keys_t,
+            log_totals,
+            seg_row,
+            seg_col,
+            low_t,
+        ) = front_all(
+            seq_size,
+            (
                 hidden[0],
-                cotangent[0],
                 jnp.broadcast_to(token_document_numbers, (8, tokens)),
                 jnp.broadcast_to(sequence_adapter_index[:, None], (8, 128)),
                 query_weight,
@@ -1184,253 +1851,87 @@
                 attention_output_weight,
                 gate_weight,
                 up_weight,
+                attention_norm_gain[None],
+                qkv_in,
+                low_map,
+                cos_n,
+                sin_n,
+            ),
+        )
+        gu_out = pick(adapter_gate_up_output).reshape(rank, 2, dp_size, seq_size, ff_block)
+        gu_out = lax.dynamic_index_in_dim(gu_out, me, 3, keepdims=False).reshape(rank, 2, ff_own)
+        none_f = jnp.zeros((rank, ff_own), BF16)
+        gu_map = jnp.concatenate(
+            [
+                jnp.concatenate([gu_out[:, 0], none_f], axis=1),
+                jnp.concatenate([none_f, gu_out[:, 1]], axis=1),
+            ],
+            axis=0,
+        )
+        down_in = pick(adapter_down_input).reshape(dp_size, seq_size, ff_block, rank)
+        down_in = lax.dynamic_index_in_dim(down_in, me, 1, keepdims=False).reshape(ff_own, rank)
+        ffn_part, middle, grad_middle, grad_attn, early, gu_grad, down_grad = mid_all(
+            seq_size,
+            (
+                attn,
+                hidden_all,
+                out_full.reshape(width, width),
+                gate_up.reshape(width, 2 * ff_own),
+                cotangent[0],
                 down_weight,
-            )
-            hidden_all = gathered[0].reshape(length, width)
-            cotangent_all = gathered[1].reshape(length, width)
-            segments = gathered[2][:, 0].reshape(length)
-            owners = gathered[3][:, 0, 0]
-            qkv = gathered[4].reshape(width, -1)
-            out_full = gathered[5].reshape(width, width)
-            gate_up = gathered[6].reshape(width, -1)
-            down = gathered[7].reshape(dp_size * ff_block, width)
-        else:
-            hidden_all = gather_seq(hidden[0])
-            segments = gather_seq(token_document_numbers[0])
-            kv = jnp.stack([key_weight.reshape(rows, KVH, HD), value_weight.reshape(rows, KVH, HD)], 2)
-            kv = jnp.repeat(kv.reshape(rows, KVH, 2 * HD), kv_repeat, axis=1)
-            qkv = jnp.concatenate([query_weight.reshape(rows, seq_size, q_width), kv], axis=2)
-            qkv = across(jnp.swapaxes(qkv, 0, 1)).reshape(seq_size * rows, q_width + 2 * HD)
-            qkv = gather_dp(qkv)
-            gate_up = jnp.concatenate([by_owner(gate_weight), by_owner(up_weight)], axis=1)
-            gate_up = across(jnp.transpose(gate_up, (2, 0, 1, 3)))
-            gate_up = gather_dp(gate_up.reshape(seq_size * rows, 2 * dp_size * ff_block))
-            down = gather_dp(down_weight)
-            out_full = lax.all_gather(attention_output_weight, ("dp", "seq"), axis=0, tiled=True)
-            cotangent_all = gather_seq(cotangent[0])
-            owners = lax.all_gather(sequence_adapter_index, "dp", axis=0, tiled=True)
-        ff_own = dp_size * ff_block
-
-        adapter = sequence_adapter_index[0]
-        qkv_in = adapter_query_key_value_input[adapter]
-        q_out = lax.dynamic_slice_in_dim(adapter_query_output[adapter], me * q_width, q_width, 1)
-        kv_out = adapter_key_value_output[adapter]
-        kv_start = (me // kv_repeat) * HD
-        k_out = lax.dynamic_slice_in_dim(kv_out, kv_start, HD, 1)
-        v_out = lax.dynamic_slice_in_dim(kv_out, key_width + kv_start, HD, 1)
-        o_in = adapter_projection_input[adapter]
-        o_out = adapter_projection_output[adapter]
-        gu_in = adapter_gate_up_input[adapter]
-        gu_all = adapter_gate_up_output[adapter].reshape(rank, 2, dp_size, seq_size, ff_block)
-        gu_out = lax.dynamic_index_in_dim(gu_all, me, 3, keepdims=False)
-        g_out, u_out = gu_out[:, 0].reshape(rank, ff_own), gu_out[:, 1].reshape(rank, ff_own)
-        down_all = adapter_down_input[adapter].reshape(dp_size, seq_size, ff_block, rank)
-        down_in = lax.dynamic_index_in_dim(down_all, me, 1, keepdims=False).reshape(ff_own, rank)
-        down_out = adapter_down_output[adapter]
-
-        norm_one = rms_scale(hidden_all.astype(F32), attention_norm_gain).astype(BF16)
-        low_qkv = mm(norm_one, qkv_in).astype(BF16)
-        pre = mm(norm_one, qkv)
-        query_pre = pre[:, :q_width] + mm(low_qkv[:, :rank], q_out)
-        key_pre = pre[:, q_width : q_width + HD] + mm(low_qkv[:, rank : 2 * rank], k_out)
-        value_pre = pre[:, q_width + HD :] + mm(low_qkv[:, 2 * rank :], v_out)
-        cos_table, sin_table = angle_tables(jnp.arange(length, dtype=jnp.int32).astype(F32), HD)
-        query = rotate(query_pre.reshape(length, heads, HD), cos_table, sin_table).astype(BF16)
-        keys = rotate(key_pre.reshape(length, 1, HD), cos_table, sin_table).astype(BF16)[:, 0]
-        values = value_pre.astype(BF16)
-        attn_heads, log_totals = attend_forward(query, keys, values, segments)
-        attn = lax.all_gather(attn_heads, "seq", axis=1, tiled=True)
-        low_out = mm(attn, o_in).astype(BF16)
-        branch = mm(attn, out_full) + mm(low_out, o_out)
-        middle = hidden_all.astype(F32) + RESIDUAL_SCALE * branch
-        own_row = me * tokens
-        middle_own = lax.dynamic_slice_in_dim(middle, own_row, tokens, 0)
-        norm_two = rms_scale(middle, feedforward_norm_gain).astype(BF16)
-        low_gu = mm(norm_two, gu_in).astype(BF16)
-        wide = mm(norm_two, gate_up)
-        gate = wide[:, :ff_own] + mm(low_gu[:, :rank], g_out)
-        up_proj = wide[:, ff_own:] + mm(low_gu[:, rank:], u_out)
-        sigma = jax.nn.sigmoid(gate)
-        activation = (gate * sigma * up_proj).astype(BF16)
-        low_down = mm(activation, down_in).astype(BF16)
-        ffn_part = (mm(activation, down) + mm(low_down, down_out)).astype(BF16)
-
-        grad_ffn = (RESIDUAL_SCALE * cotangent_all.astype(F32)).astype(BF16)
-        grad_low_down = mm_t(grad_ffn, down_out).astype(BF16)
-        grad_act = mm_t(grad_ffn, down) + mm_t(grad_low_down, down_in)
-        grad_gate = (grad_act * up_proj * sigma * (1.0 + gate * (1.0 - sigma))).astype(BF16)
-        grad_up = (grad_act * gate * sigma).astype(BF16)
-        grad_low_gu = jnp.concatenate([mm_t(grad_gate, g_out), mm_t(grad_up, u_out)], axis=1)
-        grad_low_gu = grad_low_gu.astype(BF16)
-        grad_norm_two = scatter_seq(
+                feedforward_norm_gain[None],
+                pick(adapter_projection_input),
+                pick(adapter_projection_output),
+                pick(adapter_gate_up_input),
+                gu_map,
+                down_in,
+                pick(adapter_down_output),
+            ),
+        )
+        norm_sum, ffn_sum, share, gu_got, down_got, q_got, kv_got = back_all(
+            seq_size,
             (
-                mm_t(jnp.concatenate([grad_gate, grad_up], axis=1), gate_up)
-                + mm_t(grad_low_gu, gu_in)
-            ).astype(BF16)
-        )
-        grad_middle = cotangent[0].astype(F32) + rms_back(
-            middle_own, feedforward_norm_gain, grad_norm_two.astype(F32)
-        )
-        grad_branch = (RESIDUAL_SCALE * grad_middle).astype(BF16)
-        grad_low_out = mm_t(grad_branch, o_out).astype(BF16)
-        grad_attn = (mm_t(grad_branch, out_full) + mm_t(grad_low_out, o_in)).astype(BF16)
-        attn_own = lax.dynamic_slice_in_dim(attn, own_row, tokens, 0)
-        low_out_own = lax.dynamic_slice_in_dim(low_out, own_row, tokens, 0)
-        if kernels:
-            early = jnp.concatenate(
-                [
-                    t_mm(grad_low_out, attn_own),
-                    t_mm(low_out_own, grad_branch),
-                    t_mm(grad_low_gu, norm_two),
-                    t_mm(low_down, grad_ffn),
-                ],
-                axis=0,
-            )
-            gu_grad = jnp.concatenate(
-                [t_mm(low_gu[:, :rank], grad_gate), t_mm(low_gu[:, rank:], grad_up)], axis=1
-            )
-            none_q = jnp.zeros((rank, q_width), BF16)
-            none_h = jnp.zeros((rank, HD), BF16)
-            low_map = jnp.concatenate(
-                [
-                    jnp.concatenate([q_out, none_h, none_h], axis=1),
-                    jnp.concatenate([none_q, k_out, none_h], axis=1),
-                    jnp.concatenate([none_q, none_h, v_out], axis=1),
-                ],
-                axis=0,
-            )
-            sums = back_all(
-                seq_size,
-                (
-                    jnp.swapaxes(grad_attn.reshape(tokens, seq_size, q_width), 0, 1),
-                    query.reshape(length, q_width),
-                    jnp.concatenate([keys, keys], axis=1),
-                    jnp.concatenate([values, values], axis=1),
-                    keys.T,
-                    jnp.swapaxes(log_totals, 0, 1).reshape(heads, length),
-                    segments[None],
-                    jnp.broadcast_to(segments[:, None], (length, 128)),
-                    cos_table.T,
-                    sin_table.T,
-                    jnp.tile(cos_table, (1, 4)),
-                    jnp.tile(jnp.concatenate([-sin_table, sin_table], axis=1), (1, 2)),
-                    qkv,
-                    qkv_in,
-                    low_map,
-                    low_qkv.T,
-                    norm_one,
-                    ffn_part.reshape(seq_size, tokens, width),
-                    early,
-                    gu_grad,
-                    t_mm(grad_low_down, activation),
-                    gathered[3],
-                ),
-            )
-            norm_sum, ffn_sum, share, gu_got, down_got, q_got, kv_got = sums
-            mixed = (middle_own + RESIDUAL_SCALE * ffn_sum).astype(BF16)
-            grad_hidden = grad_middle + rms_back(hidden_own, attention_norm_gain, norm_sum)
-            lower = lax.axis_index("dp") < dp_size // 2
-            kv_got = jnp.where(lower, kv_got[:, :, rank : 2 * rank], kv_got[:, :, 2 * rank : 3 * rank])
-            share_t = jnp.swapaxes(share, 1, 2)
-            return (
-                mixed[None],
-                grad_hidden.astype(BF16)[None],
-                share[:, :, : 3 * rank],
-                jnp.swapaxes(q_got[:, :, :rank], 1, 2),
-                jnp.swapaxes(kv_got, 1, 2),
-                share[:, :, 3 * rank : 4 * rank],
-                share_t[:, 4 * rank : 5 * rank],
-                share[:, :, 5 * rank : 7 * rank],
-                gu_got,
-                jnp.swapaxes(down_got, 1, 2),
-                share_t[:, 7 * rank :],
-            )
-        ffn = lax.psum_scatter(ffn_part, "seq", scatter_dimension=0, tiled=True)
-        mixed = (middle_own + RESIDUAL_SCALE * ffn.astype(F32)).astype(BF16)
-        grad_heads = lax.all_to_all(
-            jnp.swapaxes(grad_attn.reshape(tokens, seq_size, q_width), 0, 1),
-            "seq",
-            split_axis=0,
-            concat_axis=0,
-            tiled=True,
-        ).reshape(length, heads, HD)
-        grad_q, grad_k, grad_v = attend_backward(
-            query, keys, values, segments, log_totals, grad_heads
-        )
-        grad_query = rotate(grad_q.astype(F32), cos_table, -sin_table)
-        grad_query = grad_query.reshape(length, q_width).astype(BF16)
-        grad_key = rotate(grad_k[:, None], cos_table, -sin_table)[:, 0].astype(BF16)
-        grad_value = grad_v.astype(BF16)
-        grad_low_qkv = jnp.concatenate(
-            [mm_t(grad_query, q_out), mm_t(grad_key, k_out), mm_t(grad_value, v_out)], axis=1
-        ).astype(BF16)
-        grad_qkv = jnp.concatenate([grad_query, grad_key, grad_value], axis=1)
-        grad_norm_one = scatter_seq((mm_t(grad_qkv, qkv) + mm_t(grad_low_qkv, qkv_in)).astype(BF16))
-        grad_hidden = grad_middle + rms_back(
-            hidden_own, attention_norm_gain, grad_norm_one.astype(F32)
-        )
-
-        partial = jnp.concatenate(
-            [
-                t_mm(norm_one, grad_low_qkv),
-                t_mm(attn_own, grad_low_out),
-                t_mm(grad_branch, low_out_own),
-                t_mm(norm_two, grad_low_gu),
-                t_mm(grad_ffn, low_down),
-            ],
-            axis=1,
-        ).reshape(dp_size, seq_size, rows, 8 * rank)
-        own_q = t_mm(grad_query, low_qkv[:, :rank])
-        own_k = t_mm(grad_key, low_qkv[:, rank : 2 * rank])
-        own_v = t_mm(grad_value, low_qkv[:, 2 * rank :])
-        own_g = t_mm(grad_gate, low_gu[:, :rank]).reshape(dp_size, ff_block, rank)
-        own_u = t_mm(grad_up, low_gu[:, rank:]).reshape(dp_size, ff_block, rank)
-        own_d = t_mm(activation, grad_low_down).reshape(dp_size, ff_block, rank)
-
-        def placed(block, total, start, axis):
-            empty = list(block.shape)
-            empty[axis] = total
-            return lax.dynamic_update_slice_in_dim(jnp.zeros(empty, F32), block, start, axis)
-
-        def by_target(whole):
-            return whole.reshape(dp_size, seq_size, -1)
-
-        full_q = placed(own_q, width, me * q_width, 0)
-        full_kv = jnp.concatenate(
-            [placed(own_k, key_width, kv_start, 0), placed(own_v, key_width, kv_start, 0)], axis=0
-        )
-        spot = [placed(v[:, None], seq_size, me, 1) for v in (own_g, own_u, own_d)]
-        full_gu = jnp.concatenate([spot[0].reshape(ff_width, rank), spot[1].reshape(ff_width, rank)])
-        pieces = [by_target(v) for v in (partial, full_q, full_kv, full_gu, spot[2])]
-        send = jnp.concatenate(pieces, axis=2)
-        send = jnp.swapaxes(send, 0, 1).reshape(seq_size, -1)
-        mine = lax.psum_scatter(send, "seq", scatter_dimension=0, tiled=True)
-        mine = lax.all_to_all(
-            mine.reshape(dp_size, -1), "dp", split_axis=0, concat_axis=0, tiled=True
-        )
-        numbers = jnp.arange(adapters, dtype=jnp.int32)
-        chooser = (owners[:, None] == numbers[None, :]).astype(F32)
-        mine = jnp.einsum("sa,si->ai", chooser, mine, precision=lax.Precision.HIGHEST)
-        sizes = [v.shape[2] for v in pieces]
-        cuts = [sum(sizes[:i]) for i in range(1, len(sizes))]
-        got, got_q, got_kv, got_gu, got_d = jnp.split(mine, cuts, axis=1)
-        got = got.reshape(adapters, rows, 8 * rank)
-
-        def turned(flat):
-            return jnp.swapaxes(flat.reshape(adapters, -1, rank), 1, 2)
-
+                grad_attn,
+                query,
+                keys2,
+                values2,
+                keys_t,
+                log_totals,
+                seg_row,
+                seg_col,
+                jnp.asarray(np.ascontiguousarray(cos_fixed.T)),
+                jnp.asarray(np.ascontiguousarray(sin_fixed.T)),
+                cos_n,
+                sin_n,
+                qkv.reshape(width, -1),
+                qkv_in,
+                low_map,
+                low_t,
+                norm_one.reshape(length, width),
+                ffn_part,
+                early,
+                gu_grad,
+                down_grad,
+                owners,
+            ),
+        )
+        mixed = (middle + RESIDUAL_SCALE * ffn_sum).astype(BF16)
+        grad_hidden = grad_middle + rms_back(hidden[0].astype(F32), attention_norm_gain, norm_sum)
+        lower = lax.axis_index("dp") < dp_size // 2
+        kv_got = jnp.where(lower, kv_got[:, :, rank : 2 * rank], kv_got[:, :, 2 * rank : 3 * rank])
+        share_t = jnp.swapaxes(share, 1, 2)
         return (
             mixed[None],
             grad_hidden.astype(BF16)[None],
-            got[:, :, : 3 * rank],
-            turned(got_q),
-            turned(got_kv),
-            got[:, :, 3 * rank : 4 * rank],
-            jnp.swapaxes(got[:, :, 4 * rank : 5 * rank], 1, 2),
-            got[:, :, 5 * rank : 7 * rank],
-            turned(got_gu),
-            got_d.reshape(adapters, ff_block, rank),
-            jnp.swapaxes(got[:, :, 7 * rank :], 1, 2),
+            share[:, :, : 3 * rank],
+            jnp.swapaxes(q_got[:, :, :rank], 1, 2),
+            jnp.swapaxes(kv_got, 1, 2),
+            share[:, :, 3 * rank : 4 * rank],
+            share_t[:, 4 * rank : 5 * rank],
+            share[:, :, 5 * rank : 7 * rank],
+            gu_got,
+            jnp.swapaxes(down_got, 1, 2),
+            share_t[:, 7 * rank :],
         )
 
     return local
@@ -1457,5 +1958,9 @@
         by_row,
         by_column,
     )
-    local = make_local(mesh.shape["dp"], mesh.shape["seq"])
+    dp_size, seq_size = mesh.shape["dp"], mesh.shape["seq"]
+    if dp_size == 4 and seq_size == KVH:
+        local = make_kernel_local(dp_size, seq_size)
+    else:
+        local = make_local(dp_size, seq_size)
     return jax.shard_map(local, mesh=mesh, in_specs=in_specs, out_specs=out_specs, check_vma=False)

time: 564 us -> 416 us (0.74)
  matrix products: 114 us -> 0 us
  Pallas kernels: 275 us -> 377 us
  waiting for transfers between devices: 54.1 us -> 0 us
  other arithmetic: 48.2 us -> 7.37 us
  local copies, waits for them, and re-layouts: 46.6 us -> 22 us
  between operations: 15.9 us -> 1.88 us
    dot_general x36 -> x0, matrix products: 114 us -> none  [the longest x15 57.6 us: mm(): return jnp.dot(a, b, preferred_element_type=F32)]
    pallas_call x1 -> x2, Pallas kernels: 161 us -> 271 us  [the longest x1 166 us: front_all(): pl.pallas_call(functools.partial(front_kernel, seq_size), out_shape=outs,...]
    all_gather x1 -> x0, waiting for transfers between devices: 39.6 us -> none  [local(): attn = lax.all_gather(attn_heads, 'seq', axis=1, tiled=True)]
    reduce_scatter x1 -> x0, waiting for transfers between devices: 14.4 us -> none  [scatter_seq(): return lax.psum_scatter(total, 'seq', scatter_dimension=0, tiled=True)]
    unnamed x130 -> x33, local copies, waits for them, and re-layouts: 19.9 us -> 6.48 us
    reduce_sum x3 -> x0, other arithmetic: 12.6 us -> none  [the longest x1 7.66 us: rms_scale(): mean_square = jnp.mean(values * values, axis=-1, keepdims=True)]
    convert_element_type x5 -> x0, other arithmetic: 9.49 us -> none  [the longest x2 8.68 us: local(): rms_scale(hidden_all.astype(F32), attention_norm_gain).astype(BF16)]
    pallas_call x1, Pallas kernels: 114 us -> 106 us  [back_all(): pl.pallas_call(functools.partial(back_kernel, seq_size), out_shape=outs,...]
  transfers between devices with their start and end apart: 2 -> 0, of which waited for: 2 -> 0; matrix products, arithmetic and copies ran while one was open for 8% -> 0% of each run, Pallas kernels for 0% -> 0%
where the time goes in v5:
time: 416 us; the launch traced here: 408 us
  Pallas kernels  377 us (91%)
  local copies, waits for them, and re-layouts  22 us (5%)
  other arithmetic  7.37 us (2%)
    pallas_call x1, Pallas kernels, front_all(): pl.pallas_call(functools.partial(front_kernel, seq_size), out_shape=outs,...  166 us
    pallas_call x1, Pallas kernels, back_all(): pl.pallas_call(functools.partial(back_kernel, seq_size), out_shape=outs,...  106 us
    pallas_call x1, Pallas kernels, mid_all(): pl.pallas_call(functools.partial(mid_kernel, seq_size), out_shape=outs, i...  105 us

profile of v5, /device:TPU:8, one launch (start us, length us, event | category | flops | bytes accessed | tf_op | source)
XLA Modules:
  0.0 408.2 jit_solution(15697192078884213580)
XLA Ops:
  0.6 0.0 copy-start
  1.4 0.6 broadcast_in_dim.40.adapter_row
  2.0 1.2 broadcast_in_dim.38.documents
  3.2 0.8 dynamic-slice_bitcast_fusion.4
  4.0 0.7 dynamic-slice_bitcast_fusion.2
  4.7 0.7 fusion.13.low_map
  5.4 0.8 constant_dynamic-slice_fusion.4
  6.3 1.0 reshape.76
  7.3 1.0 reshape.77
  8.3 0.8 maximum_bitcast_fusion.kv_w
  9.0 0.9 constant_dynamic-slice_fusion.3
  10.0 1.5 dynamic-slice_bitcast_fusion
  11.5 0.0 copy-done
  11.5 1.0 constant_dynamic-slice_fusion.1
  12.6 0.1 constant_dynamic-slice_fusion
  12.6 0.9 copy.53
  13.5 1.0 copy.49
  14.5 1.0 copy.51
  15.5 1.0 copy.50
  16.5 1.1 constant_dynamic-slice_fusion.2
  17.6 0.1 copy.64
  17.7 0.4 dynamic-slice_reduce_fusion
  18.2 0.1 fusion.15
  18.3 0.7 fusion.10.gu_map
  19.0 165.9 %attend_front.1 = (bf16[8,128,2048]{2,1,0:T(8,128)(2,1)}, s32[4,8,128]{2,1,0:T(8,128)}, bf16[4,512,384]{2,1,0:T(8,128)(2,1)}, bf16[4,4,2,64,2048]{4,3,2,1,0:T(8,...) custom-call(bf16[128,2048]{1,0:T(8,128)(2,1)} %bitcast.60, ...), custom_call_target="tpu_custom_call" | custom-call | flops 5000000000 | bytes 62914560 | tf_op jit(solution)/shard_map/attend_front/pallas_call | solution.py:927
  184.9 104.7 %feed_forward.1 = (bf16[8,128,2048]{2,1,0:T(8,128)(2,1)}, f32[128,2048]{1,0:T(8,128)}, f32[128,2048]{1,0:T(8,128)}, bf16[8,128,256]{2,1,0:T(8,128)(2,1)}, f32[80...) custom-call(bf16[8,1024,256]{2,1,0:T(8,128)(2,1)} %get-tuple-element.40.attn_all, ...), custom_call_target="tpu_custom_call" | custom-call | flops 40000000000 | bytes 41943040 | tf_op jit(solution)/shard_map/feed_forward/pallas_call | solution.py:1727
  289.6 0.0 copy-start.5
  289.6 0.0 copy-start.3
  289.6 0.0 copy-start.10
  289.6 106.4 %attend_back.1 = (f32[128,2048]{1,0:T(8,128)}, f32[128,2048]{1,0:T(8,128)}, f32[4,64,128]{2,1,0:T(8,128)}, f32[4,16,512]{2,1,0:T(8,128)}, f32[4,16,256]{2,1,0:T(...) custom-call(bf16[8,128,256]{2,1,0:T(8,128)(2,1)} %get-tuple-element.45.grad_attn, ...), custom_call_target="tpu_custom_call" | custom-call | flops 10000000000 | bytes 20971520 | tf_op jit(solution)/shard_map/attend_back/pallas_call | solution.py:1402
  396.0 0.0 copy-start.1
  396.0 0.0 copy-start.4
  396.0 0.0 copy-start.6
  396.1 0.0 copy-start.2
  396.1 0.0 copy-start.8
  396.1 0.0 copy-done.5
  396.1 2.3 fusion.6
  398.4 0.0 copy-done.3
  398.4 0.0 copy-done.10
  398.4 0.0 copy-start.7
  398.4 0.0 copy-start.9
  398.4 1.6 fusion
  400.0 0.0 copy-done.1
  400.0 0.0 copy-done.4
  400.0 1.3 fusion.7
  401.3 0.0 copy-done.6
  401.3 0.1 select_bitcast_fusion
  401.4 0.7 copy.56
  402.1 0.0 copy-done.2
  402.1 0.7 copy.54
  402.8 0.0 copy-done.8
  402.8 0.7 copy.55
  403.5 0.1 slice.38
  403.6 0.7 copy.59
  404.4 0.1 slice.36
  404.5 0.7 copy.57
  405.2 0.1 fusion.14
  405.3 0.7 copy.60
  406.0 0.7 copy.58
  406.7 0.0 copy-done.7
  406.7 0.7 copy.71
  407.4 0.0 copy-done.9
  407.4 0.6 copy.72
  (11 shorter events, 0.2 us)
Async XLA Ops:
  0.6 10.9 %copy-start = (bf16[4,2048,48]{1,2,0:T(8,128)(2,1)S(1)}, bf16[4,2048,48]{1,2,0:T(8,128)(2,1)}, u32[]{:S(2)}) copy-start(bf16[4,2048,48]{1,2,0:T(8,128)(2,1)} %param.39) | copy-start | bytes 2359300
  289.6 106.5 %copy-start.5 = (f32[128,2048]{1,0:T(8,128)S(1)}, f32[128,2048]{1,0:T(8,128)}, u32[]{:S(2)}) copy-start(f32[128,2048]{1,0:T(8,128)} %get-tuple-element.44) | copy-start | bytes 3145732
  289.6 108.8 %copy-start.3 = (bf16[1,128,2048]{2,1,0:T(8,128)(2,1)S(1)}, bf16[1,128,2048]{2,1,0:T(8,128)(2,1)}, u32[]{:S(2)}) copy-start(bf16[1,128,2048]{2,1,0:T(8,128)(2,1)} %param.26) | copy-start | bytes 1572868
  289.6 108.8 %copy-start.10 = (f32[2048]{0:T(1024)S(1)}, f32[2048]{0:T(1024)}, u32[]{:S(2)}) copy-start(f32[2048]{0:T(1024)} %param.30) | copy-start | bytes 24580
  396.0 3.9 copy-start.1
  396.0 3.9 copy-start.4
  396.0 5.2 %copy-start.6 = (f32[4,32,128]{2,1,0:T(8,128)S(1)}, f32[4,32,128]{2,1,0:T(8,128)}, u32[]{:S(2)}) copy-start(f32[4,32,128]{2,1,0:T(8,128)} %get-tuple-element.66) | copy-start | bytes 196612
  396.1 6.0 %copy-start.2 = (f32[4,64,128]{2,1,0:T(8,128)S(1)}, f32[4,64,128]{2,1,0:T(8,128)}, u32[]{:S(2)}) copy-start(f32[4,64,128]{2,1,0:T(8,128)} %get-tuple-element.64) | copy-start | bytes 393220
  396.1 6.8 %copy-start.8 = (f32[4,64,128]{2,1,0:T(8,128)S(1)}, f32[4,64,128]{2,1,0:T(8,128)}, u32[]{:S(2)}) copy-start(f32[4,64,128]{2,1,0:T(8,128)} %get-tuple-element.65) | copy-start | bytes 393220
  398.4 8.3 %copy-start.7 = (f32[4,16,512]{2,1,0:T(8,128)S(1)}, f32[4,16,512]{2,1,0:T(8,128)}, u32[]{:S(2)}) copy-start(f32[4,16,512]{2,1,0:T(8,128)} %get-tuple-element.124) | copy-start | bytes 393220
  398.4 9.0 %copy-start.9 = (f32[4,16,256]{2,1,0:T(8,128)S(1)}, f32[4,16,256]{2,1,0:T(8,128)}, u32[]{:S(2)}) copy-start(f32[4,16,256]{2,1,0:T(8,128)} %get-tuple-element.68) | copy-start | bytes 196612

commit v6 on v5

--- a/solution.py
+++ b/solution.py
@@ -492,6 +492,36 @@
                 self._side(self.slot(high), high).wait_send()
 
 
+class Chains:
+    def __init__(self, place, own, slot, rows, sems, parts=2):
+        size = rows // parts
+        self.all = [
+            Chain(
+                place,
+                own.at[pl.ds(size * i, size)],
+                lambda n, i=i: slot(n).at[pl.ds(size * i, size)],
+                sems.at[i],
+            )
+            for i in range(parts)
+        ]
+
+    def start(self):
+        for chain in self.all:
+            chain.start()
+
+    def step(self, k):
+        for chain in self.all:
+            chain.step(k)
+
+    def side_recv(self, z):
+        for chain in self.all:
+            chain.side_recv(z)
+
+    def finish(self):
+        for chain in self.all:
+            chain.finish()
+
+
 class Plane:
     def __init__(self, place, block, half, sems):
         self.p, self.block, self.half, self.sems = place, block, half, sems
@@ -560,16 +590,14 @@
 def front_kernel(
     seq_size,
     hidden,
-    documents,
-    adapter_row,
+    numbers,
     query_w,
     kv_w,
     out_w,
     gate_w,
     up_w,
     gain,
-    qkv_in,
-    low_map,
+    maps,
     cos_n,
     sin_n,
     hidden_all,
@@ -608,11 +636,15 @@
     p = Place(seq_size)
     d, s, z, c = p.d, p.s, p.z, p.c
     rows = query_w.shape[0]
+    documents, adapter_row = numbers.at[0], numbers.at[1]
+    low_rows = maps.shape[0] // 2
+    qkv_in = maps.at[pl.ds(0, low_rows)]
     part = gate_w.shape[1] // (4 * seq_size)
     tokens = hidden.shape[0]
     half_rows = seq_size * rows // 2
     landing = pl.ds(pl.multiple_of(rows * s, rows), rows)
     q_width = query_w.shape[1] // seq_size
+    low_map = maps.at[pl.ds(low_rows, low_rows), pl.ds(0, qkv_v.shape[1])]
 
     def column_block(number, size):
         return pl.ds(pl.multiple_of(number * size, size), size)
@@ -650,9 +682,9 @@
         copy.start()
     p.greet(range(1, seq_size), (p.dx, p.dy, p.dd))
 
-    hid = Chain(p, hidden, lambda i: hidden_v.at[i], chain_sems.at[0])
-    out = Chain(p, out_w, lambda i: out_all.at[d, i // 2, i % 2], chain_sems.at[2])
-    att = Chain(p, attn_v, lambda i: attn_all.at[i], chain_sems.at[3])
+    hid = Chains(p, hidden, lambda i: hidden_v.at[i], tokens, chain_sems.at[0])
+    out = Chain(p, out_w, lambda i: out_all.at[d, i // 2, i % 2], chain_sems.at[1, 0])
+    att = Chains(p, attn_v, lambda i: attn_all.at[i], attn_v.shape[0], chain_sems.at[2])
 
     def qkv_pairs(j):
         return (
@@ -736,7 +768,7 @@
         cos_part, sin_part = cos_n[at, :], sin_n[at, :]
         normed = rms_scale(hidden_v[slot].astype(F32), gain[...]).astype(BF16)
         norm_v[slot] = normed
-        low = dot_nn(normed, qkv_in[...]).astype(BF16)
+        low = dot_nt(normed, qkv_in[...]).astype(BF16)
         pre = dot_nn(normed, weights[...]) + dot_nn(low, low_map[...])
         padded = jnp.concatenate(
             [low.astype(F32), jnp.zeros((tokens, 128 - low.shape[1]), F32)], axis=1
@@ -802,6 +834,7 @@
     for i, e in enumerate((p.dx, p.dy, p.dd)):
         adapters_copy(i, e).start()
     qkv.start()
+    out.start()
     hid.start()
     for copy in stage:
         copy.wait()
@@ -811,8 +844,9 @@
         keep[i].wait()
     qkv.recv()
     qkv_plane.start()
+    out.step(1)
     hid.step(1)
-    gu[0].start()
+    out.step(2)
     remote(
         documents_all.at[pl.ds(0, seq_size - 1)], documents_all.at[pl.ds(0, seq_size - 1)],
         small_sems.at[0, 0], small_sems.at[1, 0], p.seq(p.sib),
@@ -823,51 +857,49 @@
         seg_row[:, at] = numbers
         seg_col[at, :] = jnp.broadcast_to(numbers[0:1, :], (tokens, tokens)).T
     qkv_plane.forward()
+    out.step(3)
+    out_plane.start()
     hid.step(2)
-    gu[1].start()
-    gu[0].recv()
-    gu_planes[0].start()
+    gu[0].start()
     qkv_plane.recv()
     keep[3].start()
     keep[3].wait()
     process_distance(0)
     process_distance(1)
+    out_plane.forward()
+    side_copy(0, p.dx).start()
+    side_copy(1, p.dy).start()
     hid.step(3)
+    gu[1].start()
     gu[2].start()
-    out.start()
-    gu[1].recv()
-    gu_planes[1].start()
-    gu_planes[0].forward()
     process_distance(2)
     process_distance(3)
+    gu[0].recv()
+    gu_planes[0].start()
     gu[3].start()
-    out.step(1)
+    out_plane.recv()
+    side_copy(2, p.dd).start()
     keep[4].start()
     keep[5].start()
     query_block(0)
     query_block(1)
-    gu[2].recv()
-    gu_planes[2].start()
-    gu_planes[1].forward()
-    out.step(2)
+    gu[1].recv()
+    gu_planes[1].start()
+    gu_planes[0].forward()
     query_block(2)
     query_block(3)
     keep[6].start()
     att.start()
+    gu[2].recv()
+    gu_planes[2].start()
+    gu_planes[1].forward()
     gu[3].recv()
     gu_planes[3].start()
+    att.step(1)
     gu_planes[2].forward()
-    out.step(3)
-    out_plane.start()
-    att.step(1)
+    att.step(2)
     gu_planes[3].forward()
-    att.step(2)
-    out_plane.forward()
-    side_copy(0, p.dx).start()
-    side_copy(1, p.dy).start()
     att.step(3)
-    out_plane.recv()
-    side_copy(2, p.dd).start()
     for i in range(4):
         gu_planes[i].recv()
     for chain in (out, att):
@@ -894,13 +926,13 @@
 
 def front_all(seq_size, ins):
     tokens, width = ins[0].shape
-    rows = ins[3].shape[0]
-    part = ins[6].shape[1] // (4 * seq_size)
+    rows = ins[2].shape[0]
+    part = ins[5].shape[1] // (4 * seq_size)
     chips = seq_size // 2
-    q_width = ins[3].shape[1] // seq_size
-    qkv_width = q_width + ins[4].shape[2]
+    q_width = ins[2].shape[1] // seq_size
+    qkv_width = q_width + ins[3].shape[2]
     length = tokens * seq_size
-    low_width = ins[9].shape[1]
+    low_width = ins[8].shape[0] // 2
 
     def shape(*dims, dtype=BF16):
         return jax.ShapeDtypeStruct(dims, dtype)
@@ -927,11 +959,11 @@
     return pl.pallas_call(
         functools.partial(front_kernel, seq_size),
         out_shape=outs,
-        in_specs=[anywhere] * 8 + [vmem] * 5,
+        in_specs=[anywhere] * 7 + [vmem] * 4,
         out_specs=(anywhere,) * 7 + (vmem,) * 8,
         scratch_shapes=[
             pltpu.VMEM((seq_size, 8, tokens), jnp.int32),
-            pltpu.SemaphoreType.DMA((4, 4, seq_size)),
+            pltpu.SemaphoreType.DMA((3, 2, 4, seq_size)),
             pltpu.SemaphoreType.DMA((3 + PIECES, 2, 4)),
             pltpu.SemaphoreType.DMA((2, 16)),
             pltpu.SemaphoreType.DMA((1 + PIECES, 2)),
@@ -967,39 +999,40 @@
 
 
 class ChainSum:
-    def __init__(self, place, part, side_in, up_in, down_in, sems):
+    def __init__(self, place, part, side_in, up_in, down_in, sems, first, size):
         self.p, self.part = place, part
+        self.first, self.size = first, size
+        self.cut = pl.ds(first, size)
         self.side_in, self.up_in, self.down_in = side_in, up_in, down_in
         self.sems = sems
 
     def _side(self, z):
         p = self.p
         return remote(
-            self.part.at[2 * z + 1 - p.c], self.side_in.at[z],
+            self.part.at[2 * z + 1 - p.c, self.cut], self.side_in.at[z, self.cut],
             self.sems.at[0, z], self.sems.at[1, z], p.seq(p.sib),
         )
 
     def _up(self, z):
         p = self.p
         return remote(
-            self.part.at[2 * z + p.c], self.up_in.at[z],
+            self.part.at[2 * z + p.c, self.cut], self.up_in.at[z, self.cut],
             self.sems.at[2, z], self.sems.at[3, z], p.seq(p.s + 2),
         )
 
     def _down(self, z):
         p = self.p
         return remote(
-            self.part.at[2 * z + p.c], self.down_in.at[z],
+            self.part.at[2 * z + p.c, self.cut], self.down_in.at[z, self.cut],
             self.sems.at[4, z], self.sems.at[5, z], p.seq(p.s - 2),
         )
 
     def _add(self, z, incoming):
         slot = 2 * z + self.p.c
-        rows = self.part.shape[1]
-
-        @pl.loop(0, rows // 16)
+
+        @pl.loop(0, self.size // 16)
         def _(i):
-            cut = pl.ds(pl.multiple_of(i * 16, 16), 16)
+            cut = pl.ds(pl.multiple_of(self.first + i * 16, 16), 16)
             total = self.part[slot, cut].astype(F32) + incoming[z, cut].astype(F32)
             self.part[slot, cut] = total.astype(BF16)
 
@@ -1064,6 +1097,31 @@
             @pl.when(p.z >= k)
             def _():
                 self._down(p.z - k).wait_send()
+
+
+class ChainSums:
+    def __init__(self, place, part, side_in, up_in, down_in, sems, parts=2):
+        size = part.shape[1] // parts
+        self.all = [
+            ChainSum(place, part, side_in, up_in, down_in, sems.at[i], size * i, size)
+            for i in range(parts)
+        ]
+
+    def side_start(self, z):
+        for chain in self.all:
+            chain.side_start(z)
+
+    def step(self, k):
+        for chain in self.all:
+            chain.step(k)
+
+    def last(self):
+        for chain in self.all:
+            chain.last()
+
+    def finish(self):
+        for chain in self.all:
+            chain.finish()
 
 
 def chain_order(z):
@@ -1103,8 +1161,7 @@
     cos_n,
     sin_n,
     qkv_w,
-    qkv_in,
-    low_map,
+    maps,
     low_qkv_t,
     norm_one,
     ffn_part,
@@ -1154,6 +1211,9 @@
     p = Place(seq_size)
     d, s = p.d, p.s
     length = query.shape[0]
+    low_rows = maps.shape[0] // 2
+    qkv_in = maps.at[pl.ds(0, low_rows)]
+    low_map = maps.at[pl.ds(low_rows, low_rows), pl.ds(0, qkv_w.shape[1])]
     chips = p.chips
     loads = [
         pltpu.make_async_copy(src, dst, load_sems.at[i])
@@ -1246,8 +1306,8 @@
             start = pl.multiple_of((td * seq_size + ts) * rows, rows)
             deliver(share.at[pl.ds(start, rows)], share_in.at[d, s], td, ts, 4, wait)
 
-    ffn = ChainSum(p, ffn_v, ffn_side, ffn_up, ffn_down, ffn_sems)
-    total = ChainSum(p, sum_v, sum_side, sum_up, sum_down, sum_sems)
+    ffn = ChainSums(p, ffn_v, ffn_side, ffn_up, ffn_down, ffn_sems)
+    total = ChainSums(p, sum_v, sum_side, sum_up, sum_down, sum_sems)
 
     low_lane = lax.broadcasted_iota(jnp.int32, (length, 2 * HD), 1) < HD
     zero = jnp.zeros((length, 2 * HD), BF16)
@@ -1320,7 +1380,7 @@
         left, low = grad_qkv[rows, :], grad_low[rows, :]
         for j in range(4):
             cut = pl.ds(512 * j, 512)
-            value = dot_nt(left, qkv_v[cut, :]) + dot_nt(low, qkv_in[cut, :])
+            value = dot_nt(left, qkv_v[cut, :]) + dot_nn(low, qkv_in[:, cut])
             sum_v[2 * to, :, cut] = value[:tokens].astype(BF16)
             sum_v[2 * to + 1, :, cut] = value[tokens:].astype(BF16)
         total.side_start(to)
@@ -1375,19 +1435,19 @@
     (grad_attn, query, keys2) = ins[:3]
     _, tokens, width_q = grad_attn.shape
     length = query.shape[0]
-    width = ins[16].shape[1]
+    width = ins[15].shape[1]
     qkv_width = ins[12].shape[1]
     chips = seq_size // 2
     rows = width // (4 * seq_size)
-    rank = ins[19].shape[0]
-    block = ins[19].shape[1] // 8
+    rank = ins[18].shape[0]
+    block = ins[18].shape[1] // 8
 
     def shape(*dims):
         return jax.ShapeDtypeStruct(dims, F32)
 
     vmem = pl.BlockSpec(memory_space=pltpu.VMEM)
     anywhere = pl.BlockSpec(memory_space=pl.ANY)
-    far = (0, 12, 16, 17)
+    far = (0, 12, 15, 16)
     outs = (
         shape(tokens, width),
         shape(tokens, width),
@@ -1432,8 +1492,8 @@
             pltpu.VMEM((4, HD // 2, 128), F32),
             pltpu.SemaphoreType.DMA((4,)),
             pltpu.SemaphoreType.DMA((2, seq_size)),
-            pltpu.SemaphoreType.DMA((6, chips)),
-            pltpu.SemaphoreType.DMA((6, chips)),
+            pltpu.SemaphoreType.DMA((2, 6, chips)),
+            pltpu.SemaphoreType.DMA((2, 6, chips)),
             pltpu.SemaphoreType.DMA((5,)),
             pltpu.SemaphoreType.DMA((5,)),
         ],
@@ -1456,12 +1516,7 @@
     cotangent,
     down_w,
     gain,
-    o_in,
-    o_out,
-    gu_in,
-    gu_map,
-    down_in,
-    down_out,
+    maps,
     ffn_part,
     middle_own,
     grad_middle,
@@ -1496,7 +1551,9 @@
     part = down_w.shape[0]
     span = 2 * tokens
     hidden_width = 4 * part
-    rank = o_in.shape[1]
+    rank = maps.shape[0] // 8
+    o_in, o_out, gu_in, gu_map, down_out, down_in = mid_views(maps)
+    down_in = down_in.at[:, pl.ds(0, hidden_width)]
     heads_width = attn_all.shape[2]
     step_width = 512
     loads = [
@@ -1534,14 +1591,14 @@
     def _():
         pl.semaphore_wait(barrier, 4)
 
-    cot = Chain(p, cotangent, lambda i: cot_v.at[i], chain_sems)
+    cot = Chains(p, cotangent, lambda i: cot_v.at[i], tokens, chain_sems)
     down = Plane(
         p,
         lambda e: down_v.at[e],
         lambda e, h: down_v.at[e, pl.ds(part // 2 * h, part // 2)],
         plane_sems,
     )
-    total = ChainSum(p, sum_v, sum_side, sum_up, sum_down, sum_sems)
+    total = ChainSums(p, sum_v, sum_side, sum_up, sum_down, sum_sems)
     down_all = down_v.reshape(4 * part, width)
     cot.start()
     loads[0].wait()
@@ -1550,54 +1607,48 @@
         copy.wait()
 
     def columns(body, count):
-        @pl.loop(0, count)
-        def _(n):
-            body(pl.ds(pl.multiple_of(n * step_width, step_width), step_width))
-
-    def flat(ref, zz, cut=slice(None)):
-        return ref[pl.ds(2 * zz, 2), :, cut].reshape(span, -1)
-
+        for n in range(count):
+            body(pl.ds(n * step_width, step_width))
+
+    def tiles(body, count):
+        for zz in range(p.chips):
+            for n in range(count):
+                body(pl.ds(span * zz, span), pl.ds(n * step_width, step_width))
+
+    length = seq_size * tokens
+    norm_rows = norm_v.reshape(length, width)
+    cot_rows = cot_v.reshape(length, width)
+    sum_rows = sum_v.reshape(length, width)
     lows[...] = jnp.zeros_like(lows)
-
-    def forward(zz):
-        rows = pl.ds(span * zz, span)
-        low = dot_nn(both_v[rows, :], o_in[...]).astype(BF16)
-
-        def branch(cut):
-            value = dot_nn(both_v[rows, :], out_v[:, cut]) + dot_nn(low, o_out[:, cut])
-            wide[rows, cut] = flat(norm_v, zz, cut).astype(F32) + RESIDUAL_SCALE * value
-
-        columns(branch, width // step_width)
-
-        @pl.when(z == zz)
-        def _():
-            mine = pl.ds(pl.multiple_of(s * tokens, tokens), tokens)
-            middle_own[...] = wide[mine, :]
-            attn_own[...] = both_v[mine, :]
-            low_own[...] = dot_nn(attn_own[...], o_in[...]).astype(BF16)
-
-        middle = wide[rows, :]
-        normed = rms_scale(middle, gain[...]).astype(BF16)
-        norm_v[2 * zz] = normed[:tokens]
-        norm_v[2 * zz + 1] = normed[tokens:]
-        low_gu = dot_nn(normed, gu_in[...]).astype(BF16)
-        lows[rows, 0 : 2 * rank] = low_gu.astype(F32)
-
-        def gate_up(cut):
-            value = dot_nn(flat(norm_v, zz), gu_v[:, cut]) + dot_nn(low_gu, gu_map[:, cut])
-            wide[rows, cut] = value
-
-        columns(gate_up, 2 * hidden_width // step_width)
-
-    for zz in range(p.chips):
-        if zz == 0:
-            loads[-1].wait()
-        forward(zz)
-        if zz == 0:
-            cot.step(1)
-        if zz == 2:
-            cot.step(2)
-            down.forward()
+    mine = pl.ds(pl.multiple_of(s * tokens, tokens), tokens)
+    lows[:, 0:rank] = dot_nt(both_v[...], o_in[...])
+
+    def branch(rows, cut):
+        low = lows[rows, 0:rank].astype(BF16)
+        value = dot_nn(both_v[rows, :], out_v[:, cut]) + dot_nn(low, o_out[:, cut])
+        wide[rows, cut] = norm_rows[rows, cut].astype(F32) + RESIDUAL_SCALE * value
+
+    tiles(branch, width // step_width)
+    middle_own[...] = wide[mine, :]
+    attn_own[...] = both_v[mine, :]
+    low_own[...] = dot_nt(attn_own[...], o_in[...]).astype(BF16)
+    cot.step(1)
+    down.forward()
+
+    @pl.loop(0, length // 64)
+    def _(i):
+        rows = pl.ds(pl.multiple_of(i * 64, 64), 64)
+        norm_rows[rows, :] = rms_scale(wide[rows, :], gain[...]).astype(BF16)
+
+    loads[-1].wait()
+    lows[:, 0 : 2 * rank] = dot_nt(norm_rows[...], gu_in[...])
+    cot.step(2)
+
+    def gate_up(rows, cut):
+        low = lows[rows, 0 : 2 * rank].astype(BF16)
+        wide[rows, cut] = dot_nn(norm_rows[rows, :], gu_v[:, cut]) + dot_nn(low, gu_map[:, cut])
+
+    tiles(gate_up, 2 * hidden_width // step_width)
     cot.step(3)
     down.recv()
     for zz in range(p.chips):
@@ -1605,15 +1656,14 @@
 
     def backward(zz):
         rows = pl.ds(pl.multiple_of(span * zz, span), span)
-        grad = flat(cot_v, zz)
-        low = dot_nt(grad, down_out[...]).astype(BF16)
+        low = dot_nt(cot_rows[rows, :], down_out[...]).astype(BF16)
         lows[rows, 5 * rank : 6 * rank] = low.astype(F32)
 
-        def hidden_part(n):
-            cut = pl.ds(pl.multiple_of(n * step_width, step_width), step_width)
-            upper = pl.ds(pl.multiple_of(hidden_width + n * step_width, step_width), step_width)
+        for n in range(hidden_width // step_width):
+            cut = pl.ds(n * step_width, step_width)
+            upper = pl.ds(hidden_width + n * step_width, step_width)
             grad_act = RESIDUAL_SCALE * (
-                dot_nt(flat(cot_v, zz), down_all[cut, :]) + dot_nt(low, down_in[cut, :])
+                dot_nt(cot_rows[rows, :], down_all[cut, :]) + dot_nn(low, down_in[:, cut])
             )
             gate, up = wide[rows, cut], wide[rows, upper]
             sigma = 1.0 / (1.0 + jnp.exp(-gate))
@@ -1622,14 +1672,12 @@
             both_v[rows, cut] = (grad_act * up * sigma * (1.0 + gate * (1.0 - sigma))).astype(BF16)
             both_v[rows, upper] = (grad_act * raised).astype(BF16)
 
-        pl.loop(0, hidden_width // step_width)(hidden_part)
         low_gu = dot_nt(both_v[rows, :], gu_map[...]).astype(BF16)
         lows[rows, 2 * rank : 4 * rank] = low_gu.astype(F32)
 
         def model_part(cut):
-            value = dot_nt(both_v[rows, :], gu_v[cut, :]) + dot_nt(low_gu, gu_in[cut, :])
-            sum_v[2 * zz, :, cut] = value[:tokens].astype(BF16)
-            sum_v[2 * zz + 1, :, cut] = value[tokens:].astype(BF16)
+            value = dot_nt(both_v[rows, :], gu_v[cut, :]) + dot_nn(low_gu, gu_in[:, cut])
+            sum_rows[rows, cut] = value.astype(BF16)
 
         columns(model_part, width // step_width)
         total.side_start(zz)
@@ -1641,19 +1689,18 @@
     backward(order[2])
     total.step(2)
     backward(order[3])
-    lows[:, 4 * rank : 5 * rank] = dot_nn(act_v[...], down_in[...])
+    lows[:, 4 * rank : 5 * rank] = dot_nt(act_v[...], down_in[...])
     for zz in range(p.chips):
         lows_t[:, pl.ds(span * zz, span)] = lows[pl.ds(span * zz, span), :].T.astype(BF16)
     total.step(1)
-    length = seq_size * tokens
 
     for n in range(width // step_width):
         cut = pl.ds(step_width * n, step_width)
         early_t[2 * rank : 4 * rank, cut] = dot_nn(
-            lows_t[2 * rank : 4 * rank, :], norm_v[:, :, cut].reshape(length, step_width)
+            lows_t[2 * rank : 4 * rank, :], norm_rows[:, cut]
         )
         early_t[4 * rank : 5 * rank, cut] = RESIDUAL_SCALE * dot_nn(
-            lows_t[4 * rank : 5 * rank, :], cot_v[:, :, cut].reshape(length, step_width)
+            lows_t[4 * rank : 5 * rank, :], cot_rows[:, cut]
         )
         source = pl.ds(0, rank) if n < hidden_width // step_width else pl.ds(rank, rank)
         gu_grad[:, cut] = dot_nn(lows_t[source, :], both_v[:, cut])
@@ -1662,18 +1709,13 @@
                 lows_t[5 * rank : 6 * rank, :], act_v[:, cut]
             )
 
-    @pl.loop(0, p.chips)
-    def _(zz):
-        rows = pl.ds(pl.multiple_of(span * zz, span), span)
+
+    def feed_forward(rows, cut):
         low = lows[rows, 4 * rank : 5 * rank].astype(BF16)
-
-        def block(cut):
-            value = dot_nn(act_v[rows, :], down_all[:, cut]) + dot_nn(low, down_out[:, cut])
-            norm_v[2 * zz, :, cut] = value[:tokens].astype(BF16)
-            norm_v[2 * zz + 1, :, cut] = value[tokens:].astype(BF16)
-
-        columns(block, width // step_width)
-
+        value = dot_nn(act_v[rows, :], down_all[:, cut]) + dot_nn(low, down_out[:, cut])
+        norm_rows[rows, cut] = value.astype(BF16)
+
+    tiles(feed_forward, width // step_width)
     store = pltpu.make_async_copy(norm_v, ffn_part, local_sems.at[1, 0])
     store.start()
     total.last()
@@ -1688,7 +1730,7 @@
     low = dot_nt(branch, o_out[...]).astype(BF16)
     for j in range(seq_size):
         cut = pl.ds(heads_width * j, heads_width)
-        grad_attn[j] = (dot_nt(branch, out_v[cut, :]) + dot_nt(low, o_in[cut, :])).astype(BF16)
+        grad_attn[j] = (dot_nt(branch, out_v[cut, :]) + dot_nn(low, o_in[:, cut])).astype(BF16)
     pair = jnp.concatenate(
         [low.astype(F32), low_own[...].astype(F32), jnp.zeros((tokens, 128 - 2 * rank), F32)], axis=1
     )
@@ -1705,7 +1747,7 @@
     tokens, width = ins[4].shape
     part = ins[5].shape[0]
     length = seq_size * tokens
-    rank = ins[7].shape[1]
+    rank = ins[7].shape[0] // 8
     chips = seq_size // 2
     heads_width = ins[0].shape[2]
 
@@ -1727,7 +1769,7 @@
     return pl.pallas_call(
         functools.partial(mid_kernel, seq_size),
         out_shape=outs,
-        in_specs=[anywhere] * 6 + [vmem] * 7,
+        in_specs=[anywhere] * 6 + [vmem] * 2,
         out_specs=(anywhere,) + (vmem,) * 6,
         scratch_shapes=[
             pltpu.VMEM((width, width), BF16),
@@ -1746,9 +1788,9 @@
             pltpu.VMEM((tokens, rank), BF16),
             pltpu.VMEM((length, 128), F32),
             pltpu.VMEM((128, length), BF16),
-            pltpu.SemaphoreType.DMA((4, seq_size)),
+            pltpu.SemaphoreType.DMA((2, 4, seq_size)),
             pltpu.SemaphoreType.DMA((2, 4)),
-            pltpu.SemaphoreType.DMA((6, chips)),
+            pltpu.SemaphoreType.DMA((2, 6, chips)),
             pltpu.SemaphoreType.DMA((2, 13)),
         ],
         compiler_params=pltpu.CompilerParams(
@@ -1761,9 +1803,202 @@
     )(*ins)
 
 
+def mid_views(maps):
+    rank = maps.shape[0] // 8
+    starts = (0, 1, 2, 4, 6, 7, 8)
+    return [
+        maps.at[pl.ds(rank * a, rank * (b - a))] for a, b in zip(starts[:-1], starts[1:], strict=True)
+    ]
+
+
+def prepare_kernel(
+    seq_size,
+    adapter_ref,
+    documents,
+    key_w,
+    value_w,
+    qkv_in_all,
+    q_out_all,
+    kv_out_all,
+    o_in_all,
+    o_out_all,
+    gu_in_all,
+    gu_out_all,
+    down_in_all,
+    down_out_all,
+    numbers,
+    kv,
+    front_maps,
+    mid_maps,
+    heads_v,
+    sems,
+):
+    me = lax.axis_index("seq")
+    adapter = adapter_ref[0]
+    rank = o_out_all.shape[1]
+    q_width = q_out_all.shape[2] // seq_size
+    part = down_in_all.shape[2] // (4 * seq_size)
+    qkv_in = front_maps.at[pl.ds(0, 3 * rank)]
+    low_map = front_maps.at[pl.ds(3 * rank, 3 * rank)]
+    o_in, o_out, gu_in, gu_map, down_out, down_in = mid_views(mid_maps)
+    low_map[...] = jnp.zeros(low_map.shape, BF16)
+    gu_map[...] = jnp.zeros(gu_map.shape, BF16)
+    down_in[...] = jnp.zeros(down_in.shape, BF16)
+
+    def block(number, size):
+        return pl.ds(pl.multiple_of(number * size, size), size)
+
+    moves = [
+        (qkv_in_all.at[adapter], qkv_in),
+        (o_in_all.at[adapter], o_in),
+        (o_out_all.at[adapter], o_out),
+        (gu_in_all.at[adapter], gu_in),
+        (down_out_all.at[adapter], down_out),
+        (q_out_all.at[adapter, :, block(me, q_width)], low_map.at[pl.ds(0, rank), pl.ds(0, q_width)]),
+        (kv_out_all.at[adapter, :, block(me // 2, 2 * HD)], heads_v.at[0]),
+        (kv_out_all.at[adapter, :, block(seq_size // 2 + me // 2, 2 * HD)], heads_v.at[1]),
+    ]
+    for e in range(4):
+        moves.append(
+            (
+                down_in_all.at[adapter, :, block(seq_size * e + me, part)],
+                down_in.at[:, pl.ds(part * e, part)],
+            )
+        )
+        for upper in range(2):
+            moves.append(
+                (
+                    gu_out_all.at[adapter, :, block(seq_size * (4 * upper + e) + me, part)],
+                    gu_map.at[pl.ds(rank * upper, rank), pl.ds(part * (4 * upper + e), part)],
+                )
+            )
+    moves = [pltpu.make_async_copy(a, b, sems.at[i]) for i, (a, b) in enumerate(moves)]
+    for move in moves:
+        move.start()
+    numbers[0] = jnp.broadcast_to(documents[...], numbers.shape[1:])
+    numbers[1] = jnp.full(numbers.shape[1:], adapter, jnp.int32)
+    rows = key_w.shape[0]
+    low_lane = lax.broadcasted_iota(jnp.int32, (rows, 2 * HD), 1) < HD
+    for j in range(seq_size // 2):
+        cut = pl.ds(2 * HD * j, 2 * HD)
+        left, right = key_w[:, cut].astype(F32), value_w[:, cut].astype(F32)
+        kv[2 * j] = jnp.where(low_lane, left, pltpu.roll(right, HD, 1)).astype(BF16)
+        kv[2 * j + 1] = jnp.where(low_lane, pltpu.roll(left, HD, 1), right).astype(BF16)
+    for move in moves:
+        move.wait()
+    low_lane = lax.broadcasted_iota(jnp.int32, (rank, 2 * HD), 1) < HD
+    odd = me % 2 == 1
+    for i in range(2):
+        value = heads_v[i].astype(F32)
+        turned = pltpu.roll(value, HD, 1)
+        value = jnp.where(odd, turned, value) if i == 0 else jnp.where(odd, value, turned)
+        kept = low_lane if i == 0 else jnp.logical_not(low_lane)
+        low_map[pl.ds(rank * (1 + i), rank), pl.ds(q_width, 2 * HD)] = jnp.where(
+            kept, value, 0.0
+        ).astype(BF16)
+
+
+def prepare_all(seq_size, adapter_index, documents, key_w, value_w, maps):
+    q_out = maps[1]
+    rank = q_out.shape[1]
+    rows = key_w.shape[0]
+    tokens = documents.shape[1]
+
+    def shape(*dims, dtype=BF16):
+        return jax.ShapeDtypeStruct(dims, dtype)
+
+    vmem = pl.BlockSpec(memory_space=pltpu.VMEM)
+    width = q_out.shape[2]
+    outs = (
+        shape(2, 8, tokens, dtype=jnp.int32),
+        shape(seq_size, rows, 2 * HD),
+        shape(6 * rank, width),
+        shape(8 * rank, width),
+    )
+    return pl.pallas_call(
+        functools.partial(prepare_kernel, seq_size),
+        out_shape=outs,
+        in_specs=[pl.BlockSpec(memory_space=pltpu.SMEM), vmem, vmem, vmem]
+        + [pl.BlockSpec(memory_space=pl.ANY)] * 9,
+        out_specs=(vmem,) * len(outs),
+        scratch_shapes=[pltpu.VMEM((2, rank, 2 * HD), BF16), pltpu.SemaphoreType.DMA((20,))],
+        compiler_params=pltpu.CompilerParams(vmem_limit_bytes=62 * 2**20),
+        name="prepare",
+    )(adapter_index, documents, key_w, value_w, *maps)
+
+
+def finish_kernel(count, *refs):
+    far, outs = refs[:count], refs[count : count + 11]
+    near, sems = refs[count + 11 : 2 * count + 11], refs[-1]
+    loads = [pltpu.make_async_copy(a, b, sems.at[i]) for i, (a, b) in enumerate(zip(far, near, strict=True))]
+    for load in loads:
+        load.start()
+    middle, ffn_sum, grad_middle, norm_sum, hidden, gain, share, gu_got, down_got, q_got, kv_got = near
+    mixed, grad_hidden, qkv_in, q_out, kv_out, o_in, o_out, gu_in, gu_out, down_in, down_out = outs
+    rank = o_in.shape[1]
+    lower = lax.axis_index("dp") < 2
+    for load in loads:
+        load.wait()
+    for a in range(share.shape[0]):
+        own = share[a].T
+        qkv_in[a] = own[: 3 * rank]
+        o_in[a] = own[3 * rank : 4 * rank]
+        o_out[a] = own[4 * rank : 5 * rank]
+        gu_in[a] = own[5 * rank : 7 * rank]
+        down_out[a] = own[7 * rank :]
+        gu_out[a] = gu_got[a]
+        down_in[a] = down_got[a]
+        q_out[a] = q_got[a].T[:rank]
+        turned = kv_got[a].T
+        kv_out[a] = jnp.where(lower, turned[rank : 2 * rank], turned[2 * rank : 3 * rank])
+
+    @pl.loop(0, middle.shape[0] // 32)
+    def _(i):
+        rows = pl.ds(pl.multiple_of(i * 32, 32), 32)
+        mixed[0, rows, :] = (middle[rows, :] + RESIDUAL_SCALE * ffn_sum[rows, :]).astype(BF16)
+        back = rms_back(hidden[rows, :].astype(F32), gain[...], norm_sum[rows, :])
+        grad_hidden[0, rows, :] = (grad_middle[rows, :] + back).astype(BF16)
+
+
+def finish_all(ins):
+    tokens, width = ins[0].shape
+    adapters, rows = ins[6].shape[:2]
+    rank = ins[7].shape[1]
+
+    def shape(*dims, dtype=F32):
+        return jax.ShapeDtypeStruct(dims, dtype)
+
+    vmem = pl.BlockSpec(memory_space=pltpu.VMEM)
+    outs = (
+        shape(1, tokens, width, dtype=BF16),
+        shape(1, tokens, width, dtype=BF16),
+        shape(adapters, 3 * rank, rows),
+        shape(adapters, rank, rows),
+        shape(adapters, rank, rows // 2),
+        shape(adapters, rank, rows),
+        shape(adapters, rank, rows),
+        shape(adapters, 2 * rank, rows),
+        shape(*ins[7].shape),
+        shape(*ins[8].shape),
+        shape(adapters, rank, rows),
+    )
+    made = pl.pallas_call(
+        functools.partial(finish_kernel, len(ins)),
+        out_shape=outs,
+        in_specs=[pl.BlockSpec(memory_space=pltpu.HBM)] * len(ins),
+        out_specs=(vmem,) * len(outs),
+        scratch_shapes=[pltpu.VMEM(v.shape, v.dtype) for v in ins]
+        + [pltpu.SemaphoreType.DMA((len(ins),))],
+        compiler_params=pltpu.CompilerParams(vmem_limit_bytes=62 * 2**20),
+        name="finish",
+    )(*ins)
+    made = list(made)
+    for i in (2, 5, 7, 9):
+        made[i] = jnp.swapaxes(made[i], 1, 2)
+    return tuple(made)
+
+
 def make_kernel_local(dp_size, seq_size):
-    heads = NH // seq_size
-
     def local(
         hidden,
         token_document_numbers,
@@ -1790,36 +2025,25 @@
     ):
         tokens, width = hidden.shape[1:]
         length = tokens * seq_size
-        rows = query_weight.shape[0]
-        key_width = key_weight.shape[1]
-        ff_block = gate_weight.shape[1] // (dp_size * seq_size)
-        ff_own = dp_size * ff_block
-        rank = adapter_projection_input.shape[2]
-        q_width = heads * HD
-        me = lax.axis_index("seq")
-        adapter = sequence_adapter_index[0]
-
-        def pick(maps):
-            return lax.dynamic_index_in_dim(maps, adapter, 0, keepdims=False)
-
-        def pick_columns(maps, start, size):
-            return lax.dynamic_slice(maps, (adapter, 0, start), (1, rank, size))[0]
-
-        qkv_in = pick(adapter_query_key_value_input)
-        q_out = pick_columns(adapter_query_output, me * q_width, q_width)
-        k_out = pick_columns(adapter_key_value_output, me * HD, HD)
-        v_out = pick_columns(adapter_key_value_output, key_width + me * HD, HD)
-        none_q, none_h = jnp.zeros((rank, q_width), BF16), jnp.zeros((rank, HD), BF16)
-        low_map = jnp.concatenate(
-            [
-                jnp.concatenate([q_out, none_h, none_h], axis=1),
-                jnp.concatenate([none_q, k_out, none_h], axis=1),
-                jnp.concatenate([none_q, none_h, v_out], axis=1),
-            ],
-            axis=0,
-        )
-        kv = jnp.concatenate(
-            [key_weight.reshape(rows, KVH, HD), value_weight.reshape(rows, KVH, HD)], axis=2
+        numbers, kv, front_maps, mid_maps = (
+            prepare_all(
+                seq_size,
+                sequence_adapter_index,
+                token_document_numbers,
+                key_weight,
+                value_weight,
+                (
+                    jnp.swapaxes(adapter_query_key_value_input, 1, 2),
+                    adapter_query_output,
+                    adapter_key_value_output,
+                    jnp.swapaxes(adapter_projection_input, 1, 2),
+                    adapter_projection_output,
+                    jnp.swapaxes(adapter_gate_up_input, 1, 2),
+                    adapter_gate_up_output,
+                    jnp.swapaxes(adapter_down_input, 1, 2),
+                    adapter_down_output,
+                ),
+            )
         )
         cos_fixed, sin_fixed = fixed_tables(length)
         cos_n = jnp.asarray(np.tile(cos_fixed, (1, 4)))
@@ -1844,48 +2068,29 @@
             seq_size,
             (
                 hidden[0],
-                jnp.broadcast_to(token_document_numbers, (8, tokens)),
-                jnp.broadcast_to(sequence_adapter_index[:, None], (8, 128)),
+                numbers,
                 query_weight,
-                jnp.swapaxes(kv, 0, 1),
+                kv,
                 attention_output_weight,
                 gate_weight,
                 up_weight,
                 attention_norm_gain[None],
-                qkv_in,
-                low_map,
+                front_maps,
                 cos_n,
                 sin_n,
             ),
         )
-        gu_out = pick(adapter_gate_up_output).reshape(rank, 2, dp_size, seq_size, ff_block)
-        gu_out = lax.dynamic_index_in_dim(gu_out, me, 3, keepdims=False).reshape(rank, 2, ff_own)
-        none_f = jnp.zeros((rank, ff_own), BF16)
-        gu_map = jnp.concatenate(
-            [
-                jnp.concatenate([gu_out[:, 0], none_f], axis=1),
-                jnp.concatenate([none_f, gu_out[:, 1]], axis=1),
-            ],
-            axis=0,
-        )
-        down_in = pick(adapter_down_input).reshape(dp_size, seq_size, ff_block, rank)
-        down_in = lax.dynamic_index_in_dim(down_in, me, 1, keepdims=False).reshape(ff_own, rank)
         ffn_part, middle, grad_middle, grad_attn, early, gu_grad, down_grad = mid_all(
             seq_size,
             (
                 attn,
                 hidden_all,
                 out_full.reshape(width, width),
-                gate_up.reshape(width, 2 * ff_own),
+                gate_up.reshape(width, -1),
                 cotangent[0],
                 down_weight,
                 feedforward_norm_gain[None],
-                pick(adapter_projection_input),
-                pick(adapter_projection_output),
-                pick(adapter_gate_up_input),
-                gu_map,
-                down_in,
-                pick(adapter_down_output),
+                mid_maps,
             ),
         )
         norm_sum, ffn_sum, share, gu_got, down_got, q_got, kv_got = back_all(
@@ -1904,8 +2109,7 @@
                 cos_n,
                 sin_n,
                 qkv.reshape(width, -1),
-                qkv_in,
-                low_map,
+                front_maps,
                 low_t,
                 norm_one.reshape(length, width),
                 ffn_part,
@@ -1915,23 +2119,20 @@
                 owners,
             ),
         )
-        mixed = (middle + RESIDUAL_SCALE * ffn_sum).astype(BF16)
-        grad_hidden = grad_middle + rms_back(hidden[0].astype(F32), attention_norm_gain, norm_sum)
-        lower = lax.axis_index("dp") < dp_size // 2
-        kv_got = jnp.where(lower, kv_got[:, :, rank : 2 * rank], kv_got[:, :, 2 * rank : 3 * rank])
-        share_t = jnp.swapaxes(share, 1, 2)
-        return (
-            mixed[None],
-            grad_hidden.astype(BF16)[None],
-            share[:, :, : 3 * rank],
-            jnp.swapaxes(q_got[:, :, :rank], 1, 2),
-            jnp.swapaxes(kv_got, 1, 2),
-            share[:, :, 3 * rank : 4 * rank],
-            share_t[:, 4 * rank : 5 * rank],
-            share[:, :, 5 * rank : 7 * rank],
-            gu_got,
-            jnp.swapaxes(down_got, 1, 2),
-            share_t[:, 7 * rank :],
+        return finish_all(
+            (
+                middle,
+                ffn_sum,
+                grad_middle,
+                norm_sum,
+                hidden[0],
+                attention_norm_gain[None],
+                share,
+                gu_got,
+                down_got,
+                q_got,
+                kv_got,
+            )
         )
 
     return local

time: 416 us -> 378 us (0.909)
  the two profiles are of different devices: /device:TPU:8 before, /device:TPU:16 now
where the time goes in v6:
time: 378 us; the launch traced here: 372 us
  Pallas kernels  370 us (98%)
    pallas_call x1, Pallas kernels, front_all(): pl.pallas_call(functools.partial(front_kernel, seq_size), out_shape=outs,...  152 us
    pallas_call x1, Pallas kernels, back_all(): pl.pallas_call(functools.partial(back_kernel, seq_size), out_shape=outs,...  108 us
    pallas_call x1, Pallas kernels, mid_all(): pl.pallas_call(functools.partial(mid_kernel, seq_size), out_shape=outs, i...  102 us

profile of v6, /device:TPU:16, one launch (start us, length us, event | category | flops | bytes accessed | tf_op | source)
XLA Modules:
  0.0 371.8 jit_solution(11207038715472766757)
XLA Ops:
  1.3 3.2 prepare.1
  4.5 152.2 %attend_front.1 = (bf16[8,128,2048]{2,1,0:T(8,128)(2,1)}, s32[4,8,128]{2,1,0:T(8,128)}, bf16[4,512,384]{2,1,0:T(8,128)(2,1)}, bf16[4,4,2,64,2048]{4,3,2,1,0:T(8,...) custom-call(bf16[128,2048]{1,0:T(8,128)(2,1)} %bitcast.19, ...), custom_call_target="tpu_custom_call" | custom-call | flops 5000000000 | bytes 62914560 | tf_op jit(solution)/shard_map/attend_front/pallas_call | solution.py:959
  156.6 102.1 %feed_forward.1 = (bf16[8,128,2048]{2,1,0:T(8,128)(2,1)}, f32[128,2048]{1,0:T(8,128)}, f32[128,2048]{1,0:T(8,128)}, bf16[8,128,256]{2,1,0:T(8,128)(2,1)}, f32[80...) custom-call(bf16[8,1024,256]{2,1,0:T(8,128)(2,1)} %get-tuple-element.58.attn_all, ...), custom_call_target="tpu_custom_call" | custom-call | flops 40000000000 | bytes 41943040 | tf_op jit(solution)/shard_map/feed_forward/pallas_call | solution.py:1769
  258.7 108.1 %attend_back.1 = (f32[128,2048]{1,0:T(8,128)}, f32[128,2048]{1,0:T(8,128)}, f32[4,64,128]{2,1,0:T(8,128)}, f32[4,16,512]{2,1,0:T(8,128)}, f32[4,16,256]{2,1,0:T(...) custom-call(bf16[8,128,256]{2,1,0:T(8,128)(2,1)} %get-tuple-element.64.grad_attn, ...), custom_call_target="tpu_custom_call" | custom-call | flops 10000000000 | bytes 20971520 | tf_op jit(solution)/shard_map/attend_back/pallas_call | solution.py:1462
  366.8 4.6 %finish.1 = (bf16[1,128,2048]{2,1,0:T(8,128)(2,1)}, bf16[1,128,2048]{2,1,0:T(8,128)(2,1)}, f32[4,48,64]{2,1,0:T(8,128)}, f32[4,16,64]{2,1,0:T(8,128)}, f32[4,16,...) custom-call(f32[128,2048]{1,0:T(8,128)} %get-tuple-element.63.refs_0, ...), custom_call_target="tpu_custom_call" | custom-call | tf_op jit(solution)/shard_map/finish/pallas_call | solution.py:1985

commit v7 on v6

--- a/solution.py
+++ b/solution.py
@@ -860,7 +860,6 @@
     out.step(3)
     out_plane.start()
     hid.step(2)
-    gu[0].start()
     qkv_plane.recv()
     keep[3].start()
     keep[3].wait()
@@ -870,6 +869,7 @@
     side_copy(0, p.dx).start()
     side_copy(1, p.dy).start()
     hid.step(3)
+    gu[0].start()
     gu[1].start()
     gu[2].start()
     process_distance(2)

time: 378 us -> 378 us (level)
  the two profiles are of different devices: /device:TPU:16 before, /device:TPU:17 now
where the time goes in v7:
time: 378 us; the launch traced here: 372 us
  Pallas kernels  370 us (98%)
    pallas_call x1, Pallas kernels, front_all(): pl.pallas_call(functools.partial(front_kernel, seq_size), out_shape=outs,...  161 us
    pallas_call x1, Pallas kernels, back_all(): pl.pallas_call(functools.partial(back_kernel, seq_size), out_shape=outs,...  106 us
    pallas_call x1, Pallas kernels, mid_all(): pl.pallas_call(functools.partial(mid_kernel, seq_size), out_shape=outs, i...  95 us

profile of v7, /device:TPU:17, one launch (start us, length us, event | category | flops | bytes accessed | tf_op | source)
XLA Modules:
  0.0 371.6 jit_solution(534596511692389416)
XLA Ops:
  1.3 3.2 prepare.1
  4.5 161.4 %attend_front.1 = (bf16[8,128,2048]{2,1,0:T(8,128)(2,1)}, s32[4,8,128]{2,1,0:T(8,128)}, bf16[4,512,384]{2,1,0:T(8,128)(2,1)}, bf16[4,4,2,64,2048]{4,3,2,1,0:T(8,...) custom-call(bf16[128,2048]{1,0:T(8,128)(2,1)} %bitcast.19, ...), custom_call_target="tpu_custom_call" | custom-call | flops 5000000000 | bytes 62914560 | tf_op jit(solution)/shard_map/attend_front/pallas_call | solution.py:959
  165.9 95.0 %feed_forward.1 = (bf16[8,128,2048]{2,1,0:T(8,128)(2,1)}, f32[128,2048]{1,0:T(8,128)}, f32[128,2048]{1,0:T(8,128)}, bf16[8,128,256]{2,1,0:T(8,128)(2,1)}, f32[80...) custom-call(bf16[8,1024,256]{2,1,0:T(8,128)(2,1)} %get-tuple-element.58.attn_all, ...), custom_call_target="tpu_custom_call" | custom-call | flops 40000000000 | bytes 41943040 | tf_op jit(solution)/shard_map/feed_forward/pallas_call | solution.py:1769
  260.9 105.6 %attend_back.1 = (f32[128,2048]{1,0:T(8,128)}, f32[128,2048]{1,0:T(8,128)}, f32[4,64,128]{2,1,0:T(8,128)}, f32[4,16,512]{2,1,0:T(8,128)}, f32[4,16,256]{2,1,0:T(...) custom-call(bf16[8,128,256]{2,1,0:T(8,128)(2,1)} %get-tuple-element.64.grad_attn, ...), custom_call_target="tpu_custom_call" | custom-call | flops 10000000000 | bytes 20971520 | tf_op jit(solution)/shard_map/attend_back/pallas_call | solution.py:1462
  366.6 4.6 %finish.1 = (bf16[1,128,2048]{2,1,0:T(8,128)(2,1)}, bf16[1,128,2048]{2,1,0:T(8,128)(2,1)}, f32[4,48,64]{2,1,0:T(8,128)}, f32[4,16,64]{2,1,0:T(8,128)}, f32[4,16,...) custom-call(f32[128,2048]{1,0:T(8,128)} %get-tuple-element.63.refs_0, ...), custom_call_target="tpu_custom_call" | custom-call | tf_op jit(solution)/shard_map/finish/pallas_call | solution.py:1985
